TPU v7x, 32 devices: a whole 2x2x4 slice. The times are simulated.
32 devices in a mesh: row: 8 (over y, x, core), col: 4 (over z).
Axes of the slice: x: 2, y: 2, z: 4, core: 2. Of those that a mesh axis runs over, the one named last changes fastest.
Arguments:
- cotangent: bfloat16 [12288, 256], P(('row', 'col')), may hold values from -6 to 6
- seed_label: int32 [12288], P(('row', 'col')), may hold values from 0 to 511
- tile_values: bfloat16 [8, 4, 8, 48, 128, 128], P('row', 'col'), may hold values from 0 to 0.008239746
- tile_rows: int32 [8, 4, 8, 48], P('row', 'col'), may hold values from 0 to 11
- tile_cols: int32 [8, 4, 8, 48], P('row', 'col'), may hold values from 0 to 2
- tile_scale: int32 [8, 4, 8, 48], P('row', 'col'), may hold values from 0 to 4
Outputs:
- first_grad: bfloat16 [12288, 256], P(('row', 'col'))
- label_grad: bfloat16 [12288, 256], P(('row', 'col'))
All inputs are finite; a program needn't handle non-finite values.
Results may differ from a plain program's by a relative error of at most 0.019.
Values may be sent and summed in bfloat16 or wider, within the bound.
No kernel may reach another device: no remote copies, remote signals or barrier semaphores. Data moves between devices by JAX's collectives and lax.ppermute only.
A program may use at most 64 MiB of HBM per device.

v0:
```python
import jax
import jax.numpy as jnp
from jax import lax
from jax.sharding import PartitionSpec as P

ALPHA = 0.9


def group_term(sources, blocks, tile_item):
    tile_block, row_ids, col_ids, scale_ids = tile_item
    picked = jnp.take(sources, row_ids, axis=0)
    products = jnp.einsum("tij,tic->tjc", tile_block, picked, preferred_element_type=jnp.float32)
    weights = scale_ids.astype(jnp.float32)[:, None] * (
        col_ids[:, None] == jnp.arange(blocks, dtype=jnp.int32)[None, :]
    ).astype(jnp.float32)
    summed = jnp.einsum("tb,tjc->bjc", weights, products, precision=lax.Precision.HIGHEST)
    return summed.reshape(blocks * summed.shape[1], summed.shape[2])


def propagate(labels, tile_set, blocks):
    segment, classes = labels.shape
    tile_size = tile_set[0].shape[-1]
    gathered = lax.all_gather(labels, "col", axis=0, tiled=True)
    sources = gathered.reshape(gathered.shape[0] // tile_size, tile_size, classes)
    group_terms = lax.map(lambda tile_item: group_term(sources, blocks, tile_item), tile_set)
    flat_terms = group_terms.reshape(group_terms.shape[0] * segment, classes)
    return lax.psum_scatter(
        flat_terms.astype(jnp.bfloat16), "row", scatter_dimension=0, tiled=True
    ).astype(jnp.float32)


def local(cotangent, seed_label, tile_values, tile_rows, tile_cols, tile_scale):
    segment, classes = cotangent.shape
    blocks = segment // tile_values.shape[-1]
    tile_set = (tile_values[0, 0], tile_rows[0, 0], tile_cols[0, 0], tile_scale[0, 0])
    keep_mask = (seed_label[:, None] != jnp.arange(classes, dtype=jnp.int32)[None, :]).astype(
        jnp.float32
    )
    first_in = (cotangent.astype(jnp.float32) * keep_mask).astype(jnp.bfloat16)
    first_grad = (ALPHA * propagate(first_in, tile_set, blocks)).astype(jnp.bfloat16)
    second_in = (first_grad.astype(jnp.float32) * keep_mask).astype(jnp.bfloat16)
    second = propagate(second_in, tile_set, blocks)
    label_grad = ALPHA * second + (1.0 - ALPHA) * keep_mask * (
        cotangent.astype(jnp.float32) + first_grad.astype(jnp.float32)
    )
    return (first_grad, label_grad.astype(jnp.bfloat16))


def solution(mesh):
    return jax.shard_map(
        local,
        mesh=mesh,
        in_specs=(
            P(("row", "col"), None),
            P(("row", "col")),
            P("row", "col", None, None, None, None),
            P("row", "col", None, None),
            P("row", "col", None, None),
            P("row", "col", None, None),
        ),
        out_specs=(P(("row", "col"), None), P(("row", "col"), None)),
        check_vma=False,
    )
```

profile of v0, /device:TPU:0, one launch (start us, length us, event | category | flops | bytes accessed | tf_op | source)
XLA Modules:
  0.0 359.0 jit_solution(4480990061473477681)
XLA Ops:
  8.3 21.3 %all_gather.6 = bf16[1536,256]{1,0:T(8,128)(2,1)S(1)} all-gather(bf16[384,256]{1,0:T(8,128)(2,1)S(1)} %fusion.40), channel_id=1, replica_groups=mesh['row'=8,'col'=4] {'col'}, dimensions={0}, use_global_device_ids=true | all-gather | bytes 983040 | tf_op jit(solution)/shard_map/all_gather | solution.py:23
  29.7 111.2 %while.20 = (s32[]{:T(128)}, bf16[8,384,256]{2,1,0:T(8,128)(2,1)S(1)}, s32[8,48]{1,0:T(8,128)}, s32[8,48]{1,0:T(8,128)}, bf16[8,48,128,128]{3,2,1,0:T(8,128)(2,1...) while((s32[]{:T(128)}, bf16[8,384,256]{2,1,0:T(8,128)(2,1)S(1)}, s32[8,48]{1,0:T(8,128)}, ...), condition=%wide.region_1.3_spmd, body=%wide.region_0.2_spmd.sunk | while | flops 460850784 | bytes 24582720 | solution.py:25
  30.4 2.5 gather_fusion
  32.9 3.4 fusion.63
  37.0 6.5 %fusion.65 = bf16[3,128,256]{2,0,1:T(4,128)(2,1)S(1)} fusion(f32[48,128,256]{2,1,0:T(8,128)S(1)} %fusion.63, f32[48]{0:T(128)S(1)} %get-tuple-element.206, s32[48]{0:T(128)S(1)} %get-tuple-element.207), kind=kOutput, calls=%fused_computation.2.clone.1 | convolution fusion | flops 56623392 | bytes 6488448 | tf_op jit(solution)/shard_map/while/body/eval_jaxpr/tb,tjc->bjc/dot_general | solution.py:16
  44.3 2.5 gather_fusion
  46.8 3.4 fusion.63
  50.9 6.5 %fusion.65 = bf16[3,128,256]{2,0,1:T(4,128)(2,1)S(1)} fusion(f32[48,128,256]{2,1,0:T(8,128)S(1)} %fusion.63, f32[48]{0:T(128)S(1)} %get-tuple-element.206, s32[48]{0:T(128)S(1)} %get-tuple-element.207), kind=kOutput, calls=%fused_computation.2.clone.1 | convolution fusion | flops 56623392 | bytes 6488448 | tf_op jit(solution)/shard_map/while/body/eval_jaxpr/tb,tjc->bjc/dot_general | solution.py:16
  58.2 2.5 gather_fusion
  60.7 3.4 fusion.63
  64.8 6.5 %fusion.65 = bf16[3,128,256]{2,0,1:T(4,128)(2,1)S(1)} fusion(f32[48,128,256]{2,1,0:T(8,128)S(1)} %fusion.63, f32[48]{0:T(128)S(1)} %get-tuple-element.206, s32[48]{0:T(128)S(1)} %get-tuple-element.207), kind=kOutput, calls=%fused_computation.2.clone.1 | convolution fusion | flops 56623392 | bytes 6488448 | tf_op jit(solution)/shard_map/while/body/eval_jaxpr/tb,tjc->bjc/dot_general | solution.py:16
  72.1 2.5 gather_fusion
  74.6 3.4 fusion.63
  78.7 6.5 %fusion.65 = bf16[3,128,256]{2,0,1:T(4,128)(2,1)S(1)} fusion(f32[48,128,256]{2,1,0:T(8,128)S(1)} %fusion.63, f32[48]{0:T(128)S(1)} %get-tuple-element.206, s32[48]{0:T(128)S(1)} %get-tuple-element.207), kind=kOutput, calls=%fused_computation.2.clone.1 | convolution fusion | flops 56623392 | bytes 6488448 | tf_op jit(solution)/shard_map/while/body/eval_jaxpr/tb,tjc->bjc/dot_general | solution.py:16
  86.0 2.5 gather_fusion
  88.5 3.4 fusion.63
  92.6 6.5 %fusion.65 = bf16[3,128,256]{2,0,1:T(4,128)(2,1)S(1)} fusion(f32[48,128,256]{2,1,0:T(8,128)S(1)} %fusion.63, f32[48]{0:T(128)S(1)} %get-tuple-element.206, s32[48]{0:T(128)S(1)} %get-tuple-element.207), kind=kOutput, calls=%fused_computation.2.clone.1 | convolution fusion | flops 56623392 | bytes 6488448 | tf_op jit(solution)/shard_map/while/body/eval_jaxpr/tb,tjc->bjc/dot_general | solution.py:16
  99.9 2.5 gather_fusion
  102.4 3.4 fusion.63
  106.5 6.5 %fusion.65 = bf16[3,128,256]{2,0,1:T(4,128)(2,1)S(1)} fusion(f32[48,128,256]{2,1,0:T(8,128)S(1)} %fusion.63, f32[48]{0:T(128)S(1)} %get-tuple-element.206, s32[48]{0:T(128)S(1)} %get-tuple-element.207), kind=kOutput, calls=%fused_computation.2.clone.1 | convolution fusion | flops 56623392 | bytes 6488448 | tf_op jit(solution)/shard_map/while/body/eval_jaxpr/tb,tjc->bjc/dot_general | solution.py:16
  113.8 2.5 gather_fusion
  116.3 3.4 fusion.63
  120.4 6.5 %fusion.65 = bf16[3,128,256]{2,0,1:T(4,128)(2,1)S(1)} fusion(f32[48,128,256]{2,1,0:T(8,128)S(1)} %fusion.63, f32[48]{0:T(128)S(1)} %get-tuple-element.206, s32[48]{0:T(128)S(1)} %get-tuple-element.207), kind=kOutput, calls=%fused_computation.2.clone.1 | convolution fusion | flops 56623392 | bytes 6488448 | tf_op jit(solution)/shard_map/while/body/eval_jaxpr/tb,tjc->bjc/dot_general | solution.py:16
  127.7 2.5 gather_fusion
  130.2 3.4 fusion.63
  134.3 6.5 %fusion.65 = bf16[3,128,256]{2,0,1:T(4,128)(2,1)S(1)} fusion(f32[48,128,256]{2,1,0:T(8,128)S(1)} %fusion.63, f32[48]{0:T(128)S(1)} %get-tuple-element.206, s32[48]{0:T(128)S(1)} %get-tuple-element.207), kind=kOutput, calls=%fused_computation.2.clone.1 | convolution fusion | flops 56623392 | bytes 6488448 | tf_op jit(solution)/shard_map/while/body/eval_jaxpr/tb,tjc->bjc/dot_general | solution.py:16
  142.1 37.9 %reduce-scatter.3.cloned.1.call-done = bf16[384,256]{1,0:T(8,128)(2,1)} async-done(((bf16[3072,256]{1,0:T(8,128)(2,1)}), bf16[384,256]{1,0:T(8,128)(2,1)}) %reduce-scatter.3.cloned.1.call-update) | async-done | bytes 196624 | tf_op jit(solution)/shard_map/reduce_scatter | solution.py:27
  181.1 19.7 %all_gather.7 = bf16[1536,256]{1,0:T(8,128)(2,1)S(1)} all-gather(bf16[384,256]{1,0:T(8,128)(2,1)S(1)} %get-tuple-element.111), channel_id=1, replica_groups=mesh['row'=8,'col'=4] {'col'}, dimensions={0}, use_global_device_ids=true | all-gather | bytes 983040 | tf_op jit(solution)/shard_map/all_gather | solution.py:23
  201.0 111.2 %while.21 = (s32[]{:T(128)}, bf16[8,384,256]{2,1,0:T(8,128)(2,1)S(1)}, s32[8,48]{1,0:T(8,128)}, s32[8,48]{1,0:T(8,128)}, bf16[8,48,128,128]{3,2,1,0:T(8,128)(2,1...) while((s32[]{:T(128)}, bf16[8,384,256]{2,1,0:T(8,128)(2,1)S(1)}, s32[8,48]{1,0:T(8,128)}, ...), condition=%wide.region_4.6_spmd, body=%wide.region_3.5_spmd.sunk | while | flops 460850784 | bytes 24582720 | solution.py:25
  201.7 2.5 gather_fusion.1
  204.2 3.4 fusion.70
  208.4 6.5 %fusion.72 = bf16[3,128,256]{2,0,1:T(4,128)(2,1)S(1)} fusion(f32[48,128,256]{2,1,0:T(8,128)S(1)} %fusion.70, f32[48]{0:T(128)S(1)} %get-tuple-element.217, s32[48]{0:T(128)S(1)} %get-tuple-element.218), kind=kOutput, calls=%fused_computation.30.clone.1 | convolution fusion | flops 56623392 | bytes 6488448 | tf_op jit(solution)/shard_map/while/body/eval_jaxpr/tb,tjc->bjc/dot_general | solution.py:16
  215.6 2.5 gather_fusion.1
  218.1 3.4 fusion.70
  222.3 6.5 %fusion.72 = bf16[3,128,256]{2,0,1:T(4,128)(2,1)S(1)} fusion(f32[48,128,256]{2,1,0:T(8,128)S(1)} %fusion.70, f32[48]{0:T(128)S(1)} %get-tuple-element.217, s32[48]{0:T(128)S(1)} %get-tuple-element.218), kind=kOutput, calls=%fused_computation.30.clone.1 | convolution fusion | flops 56623392 | bytes 6488448 | tf_op jit(solution)/shard_map/while/body/eval_jaxpr/tb,tjc->bjc/dot_general | solution.py:16
  232.0 3.4 fusion.70
  236.2 6.5 %fusion.72 = bf16[3,128,256]{2,0,1:T(4,128)(2,1)S(1)} fusion(f32[48,128,256]{2,1,0:T(8,128)S(1)} %fusion.70, f32[48]{0:T(128)S(1)} %get-tuple-element.217, s32[48]{0:T(128)S(1)} %get-tuple-element.218), kind=kOutput, calls=%fused_computation.30.clone.1 | convolution fusion | flops 56623392 | bytes 6488448 | tf_op jit(solution)/shard_map/while/body/eval_jaxpr/tb,tjc->bjc/dot_general | solution.py:16
  245.9 3.4 fusion.70
  250.1 6.5 %fusion.72 = bf16[3,128,256]{2,0,1:T(4,128)(2,1)S(1)} fusion(f32[48,128,256]{2,1,0:T(8,128)S(1)} %fusion.70, f32[48]{0:T(128)S(1)} %get-tuple-element.217, s32[48]{0:T(128)S(1)} %get-tuple-element.218), kind=kOutput, calls=%fused_computation.30.clone.1 | convolution fusion | flops 56623392 | bytes 6488448 | tf_op jit(solution)/shard_map/while/body/eval_jaxpr/tb,tjc->bjc/dot_general | solution.py:16
  259.8 3.4 fusion.70
  264.0 6.5 %fusion.72 = bf16[3,128,256]{2,0,1:T(4,128)(2,1)S(1)} fusion(f32[48,128,256]{2,1,0:T(8,128)S(1)} %fusion.70, f32[48]{0:T(128)S(1)} %get-tuple-element.217, s32[48]{0:T(128)S(1)} %get-tuple-element.218), kind=kOutput, calls=%fused_computation.30.clone.1 | convolution fusion | flops 56623392 | bytes 6488448 | tf_op jit(solution)/shard_map/while/body/eval_jaxpr/tb,tjc->bjc/dot_general | solution.py:16
  273.7 3.4 fusion.70
  277.9 6.5 %fusion.72 = bf16[3,128,256]{2,0,1:T(4,128)(2,1)S(1)} fusion(f32[48,128,256]{2,1,0:T(8,128)S(1)} %fusion.70, f32[48]{0:T(128)S(1)} %get-tuple-element.217, s32[48]{0:T(128)S(1)} %get-tuple-element.218), kind=kOutput, calls=%fused_computation.30.clone.1 | convolution fusion | flops 56623392 | bytes 6488448 | tf_op jit(solution)/shard_map/while/body/eval_jaxpr/tb,tjc->bjc/dot_general | solution.py:16
  287.6 3.4 fusion.70
  291.8 6.5 %fusion.72 = bf16[3,128,256]{2,0,1:T(4,128)(2,1)S(1)} fusion(f32[48,128,256]{2,1,0:T(8,128)S(1)} %fusion.70, f32[48]{0:T(128)S(1)} %get-tuple-element.217, s32[48]{0:T(128)S(1)} %get-tuple-element.218), kind=kOutput, calls=%fused_computation.30.clone.1 | convolution fusion | flops 56623392 | bytes 6488448 | tf_op jit(solution)/shard_map/while/body/eval_jaxpr/tb,tjc->bjc/dot_general | solution.py:16
  301.5 3.4 fusion.70
  305.7 6.5 %fusion.72 = bf16[3,128,256]{2,0,1:T(4,128)(2,1)S(1)} fusion(f32[48,128,256]{2,1,0:T(8,128)S(1)} %fusion.70, f32[48]{0:T(128)S(1)} %get-tuple-element.217, s32[48]{0:T(128)S(1)} %get-tuple-element.218), kind=kOutput, calls=%fused_computation.30.clone.1 | convolution fusion | flops 56623392 | bytes 6488448 | tf_op jit(solution)/shard_map/while/body/eval_jaxpr/tb,tjc->bjc/dot_general | solution.py:16
  313.4 37.0 %reduce-scatter.5.cloned.1.call-done = bf16[384,256]{1,0:T(8,128)(2,1)} async-done(((bf16[3072,256]{1,0:T(8,128)(2,1)}), bf16[384,256]{1,0:T(8,128)(2,1)}) %reduce-scatter.5.cloned.1.call-update) | async-done | bytes 196624 | tf_op jit(solution)/shard_map/reduce_scatter | solution.py:27
  (105 shorter events, 44.9 us)
Async XLA Ops:
  7.2 172.9 %reduce-scatter.3.cloned.1.call-start = ((), (), s32[]{:S(2)}) async-start(), calls=%async_computation.2 | async-start | bytes 1769472 | tf_op jit(solution)/shard_map/reduce_scatter | solution.py:27
  29.7 150.4 %copy-start.4 = (s32[384]{0:T(512)S(1)}, s32[384]{0:T(512)}, u32[]{:S(2)}) copy-start(s32[384]{0:T(512)} %param.13) | copy-start | bytes 4612
  140.9 1.2 copy-start.1
  142.1 208.4 %reduce-scatter.5.cloned.1.call-start = ((), (), s32[]{:S(2)}) async-start(), calls=%async_computation.3 | async-start | bytes 1769472 | tf_op jit(solution)/shard_map/reduce_scatter | solution.py:27
  181.1 169.4 %copy-start.3 = (bf16[384,256]{1,0:T(8,128)(2,1)}, bf16[384,256]{1,0:T(8,128)(2,1)S(1)}, u32[]{:S(2)}) copy-start(bf16[384,256]{1,0:T(8,128)(2,1)S(1)} %get-tuple-element.112) | copy-start | bytes 589828
  201.0 149.5 %copy-start.2 = (bf16[384,256]{1,0:T(8,128)(2,1)S(1)}, bf16[384,256]{1,0:T(8,128)(2,1)}, u32[]{:S(2)}) copy-start(bf16[384,256]{1,0:T(8,128)(2,1)} %param.12) | copy-start | bytes 589828
  312.2 1.2 copy-start
Sparse Core Ops, SparseCore 0:
  142.2 37.8 reduce-scatter.2
  313.5 36.8 reduce-scatter.4
where the time goes:
time: 361 us; the launch traced here: 359 us
  matrix products  159 us (44%)
  waiting for transfers between devices  75 us (21%)
  local copies, waits for them, and re-layouts  42.9 us (12%)
  blocking collectives  41 us (11%)
  other arithmetic  26.6 us (7%)
  between operations  14.1 us (4%)
    dot_general x16, matrix products, group_term(): jnp.einsum('tb,tjc->bjc', weights, products, precision=lax.Precision.HIGH...  104 us
    reduce_scatter x2, waiting for transfers between devices, propagate(): lax.psum_scatter(flat_terms.astype(jnp.bfloat16), 'row', scatter_dimensio...  75 us
    dot_general x16, matrix products, group_term(): jnp.einsum('tij,tic->tjc', tile_block, picked, preferred_element_type=jnp...  55 us
    all_gather x2, blocking collectives, propagate(): gathered = lax.all_gather(labels, 'col', axis=0, tiled=True)  41 us
    gather x16, local copies, waits for them, and re-layouts, group_term(): picked = jnp.take(sources, row_ids, axis=0)  39.7 us
    eq x16, other arithmetic, group_term(): col_ids[:, None] == jnp.arange(blocks, dtype=jnp.int32)[None, :]  11.5 us
    and x16, other arithmetic, group_term(): picked = jnp.take(sources, row_ids, axis=0)  11.3 us
  transfers between devices with their start and end apart: 2, of which 2 were waited for; matrix products, arithmetic and copies ran while one was open for 0% of the time, Pallas kernels for 0%

commit v1 on v0

v1 whole, which is shorter than its diff:
```python
import functools

import jax
import jax.numpy as jnp
from jax import lax
from jax.experimental import pallas as pl
from jax.experimental.pallas import tpu as pltpu
from jax.sharding import PartitionSpec as P

ALPHA = 0.9
CHUNKS = 2
VMEM_LIMIT = 40 * 1024 * 1024


def params(limit=VMEM_LIMIT):
    return pltpu.CompilerParams(vmem_limit_bytes=limit)


def keep_of(seed_row, first_class, classes):
    ids = lax.broadcasted_iota(jnp.int32, (classes, seed_row.shape[1]), 0) + first_class
    return ids != seed_row


def prepare_kernel(cot_ref, seed_ref, *out_refs):
    rows = out_refs[0].shape[0]
    for i, out_ref in enumerate(out_refs):
        part = cot_ref[:, i * rows : (i + 1) * rows].astype(jnp.float32).T
        keep = keep_of(seed_ref[...], i * rows, rows)
        out_ref[...] = jnp.where(keep, part, 0.0).astype(out_ref.dtype)


def prepare(cotangent, seed_row):
    segment, classes = cotangent.shape
    shape = jax.ShapeDtypeStruct((classes // CHUNKS, segment), jnp.bfloat16)
    return pl.pallas_call(
        prepare_kernel,
        out_shape=[shape] * CHUNKS,
        name="prepare",
        compiler_params=params(),
    )(cotangent, seed_row)


def densify_kernel(place_ref, rows_ref, cols_ref, scale_ref, tiles_ref, out_ref, total_ref):
    slots, tile = tiles_ref.shape[3], tiles_ref.shape[4]
    blocks = out_ref.shape[2] // tile
    target = jnp.bitwise_xor(place_ref[0], pl.program_id(0))
    mine = place_ref[1]
    total_ref[...] = jnp.zeros_like(total_ref)

    def add(slot, carry):
        row, col = rows_ref[target, slot], cols_ref[target, slot]
        owner = row // blocks
        place = jnp.bitwise_xor(owner, mine) * blocks + row - owner * blocks
        scale = scale_ref[target, slot].astype(jnp.float32)
        where = (
            pl.ds(pl.multiple_of(place * tile, tile), tile),
            pl.ds(pl.multiple_of(col * tile, tile), tile),
        )
        total_ref[where] += scale * tiles_ref[0, 0, 0, slot].astype(jnp.float32)
        return carry

    lax.fori_loop(0, slots, add, 0)
    out_ref[0] = total_ref[...].astype(out_ref.dtype)


def densify(place, tile_values, tile_rows, tile_cols, tile_scale, depth, segment):
    _, _, targets, slots, tile, _ = tile_values.shape
    return pl.pallas_call(
        densify_kernel,
        grid_spec=pltpu.PrefetchScalarGridSpec(
            num_scalar_prefetch=4,
            grid=(targets,),
            in_specs=[
                pl.BlockSpec(
                    (1, 1, 1, slots, tile, tile),
                    lambda m, place, *_: (0, 0, jnp.bitwise_xor(place[0], m), 0, 0, 0),
                )
            ],
            out_specs=pl.BlockSpec((1, depth, segment), lambda m, *_: (m, 0, 0)),
            scratch_shapes=[pltpu.VMEM((depth, segment), jnp.float32)],
        ),
        out_shape=jax.ShapeDtypeStruct((targets, depth, segment), jnp.bfloat16),
        name="densify",
        compiler_params=params(),
    )(place, tile_rows[0, 0], tile_cols[0, 0], tile_scale[0, 0], tile_values)


def multiply_kernel(parts, *refs):
    label_refs, matrix_ref, out_ref = refs[:parts], refs[parts], refs[parts + 1]
    segment = matrix_ref.shape[2]
    total = None
    for i, label_ref in enumerate(label_refs):
        term = jnp.dot(
            label_ref[...],
            matrix_ref[0, i * segment : (i + 1) * segment, :],
            preferred_element_type=jnp.float32,
        )
        total = term if total is None else total + term
    out_ref[0] = total.astype(out_ref.dtype)


def multiply(labels, matrix, odd, dtype):
    targets, depth, segment = matrix.shape
    rows = labels[0].shape[0]
    return pl.pallas_call(
        functools.partial(multiply_kernel, len(labels)),
        grid=(targets // 2,),
        in_specs=[pl.BlockSpec((rows, segment), lambda m: (0, 0))] * len(labels)
        + [pl.BlockSpec((1, depth, segment), lambda m: (2 * m + odd, 0, 0))],
        out_specs=pl.BlockSpec((1, rows, segment), lambda m: (m, 0, 0)),
        out_shape=jax.ShapeDtypeStruct((targets // 2, rows, segment), dtype),
        name="multiply_theirs" if odd else "multiply_mine",
        compiler_params=params(),
        cost_estimate=pl.CostEstimate(
            flops=targets * depth * segment * rows,
            bytes_accessed=targets * depth * segment,
            transcendentals=0,
        ),
    )(*labels, matrix)


def pair_kernel(mine_ref, theirs_ref, *out_refs):
    for i, out_ref in enumerate(out_refs):
        total = mine_ref[i] + theirs_ref[i].astype(jnp.float32)
        out_ref[...] = total.astype(out_ref.dtype)


def pair(mine, theirs):
    count, rows, segment = mine.shape
    return pl.pallas_call(
        pair_kernel,
        out_shape=[jax.ShapeDtypeStruct((rows, segment), jnp.float32)]
        + [jax.ShapeDtypeStruct((rows, segment), jnp.bfloat16)] * (count - 1),
        name="pair_sum",
        compiler_params=params(),
    )(mine, theirs)


def middle_kernel(first_class, seed_ref, *refs):
    pieces, (grad_ref, next_ref) = refs[:-2], refs[-2:]
    total = pieces[0][...]
    for piece in pieces[1:]:
        total = total + piece[...].astype(jnp.float32)
    grad = (ALPHA * total).astype(jnp.bfloat16)
    grad_ref[...] = grad.astype(jnp.float32).T.astype(jnp.bfloat16)
    keep = keep_of(seed_ref[...], first_class, grad.shape[0])
    next_ref[...] = jnp.where(keep, grad.astype(jnp.float32), 0.0).astype(jnp.bfloat16)


def middle(seed_row, pieces, first_class):
    rows, segment = pieces[0].shape
    return pl.pallas_call(
        functools.partial(middle_kernel, first_class),
        out_shape=[
            jax.ShapeDtypeStruct((segment, rows), jnp.bfloat16),
            jax.ShapeDtypeStruct((rows, segment), jnp.bfloat16),
        ],
        name="first_grad",
        compiler_params=params(),
    )(seed_row, *pieces)


def final_kernel(first_ref, second_ref, *refs):
    pieces, out_ref = refs[:-1], refs[-1]
    total = pieces[0][...]
    for piece in pieces[1:]:
        total = total + piece[...].astype(jnp.float32)
    kept = first_ref[...].astype(jnp.float32) + second_ref[...].astype(jnp.float32)
    out_ref[...] = (ALPHA * total + (1.0 - ALPHA) * kept).T.astype(jnp.bfloat16)


def final(first_in, second_in, pieces):
    rows, segment = first_in.shape
    return pl.pallas_call(
        final_kernel,
        out_shape=jax.ShapeDtypeStruct((segment, rows), jnp.bfloat16),
        name="label_grad",
        compiler_params=params(),
    )(first_in, second_in, *pieces)


def flip(array, axis, size, bits):
    return lax.ppermute(array, axis, [(i, i ^ bits) for i in range(size)])


def gather(labels, n_col):
    return [labels] + [flip(labels, "col", n_col, k) for k in range(1, n_col)]


def reduce(labels, matrix, n_row):
    theirs = multiply(labels, matrix, 1, jnp.bfloat16)
    arrived = flip(theirs, "row", n_row, 1)
    mine = multiply(labels, matrix, 0, jnp.float32)
    own, *others = pair(mine, arrived)
    return [own] + [flip(part, "row", n_row, 2 * (j + 1)) for j, part in enumerate(others)]


def local(n_row, n_col, cotangent, seed_label, tile_values, tile_rows, tile_cols, tile_scale):
    segment, classes = cotangent.shape
    rows = classes // CHUNKS
    place = jnp.stack([lax.axis_index("row"), lax.axis_index("col")]).astype(jnp.int32)
    seed_row = seed_label[None, :]
    first_in = prepare(cotangent, seed_row)
    matrix = densify(
        place, tile_values, tile_rows, tile_cols, tile_scale, n_col * segment, segment
    )
    grads, seconds = [], []
    for i in range(CHUNKS):
        pieces = reduce(gather(first_in[i], n_col), matrix, n_row)
        grad, second_in = middle(seed_row, pieces, i * rows)
        grads.append(grad)
        seconds.append(second_in)
    results = []
    for i in range(CHUNKS):
        pieces = reduce(gather(seconds[i], n_col), matrix, n_row)
        results.append(final(first_in[i], seconds[i], pieces))
    return jnp.concatenate(grads, axis=1), jnp.concatenate(results, axis=1)


def solution(mesh):
    return jax.shard_map(
        functools.partial(local, mesh.shape["row"], mesh.shape["col"]),
        mesh=mesh,
        in_specs=(
            P(("row", "col"), None),
            P(("row", "col")),
            P("row", "col", None, None, None, None),
            P("row", "col", None, None),
            P("row", "col", None, None),
            P("row", "col", None, None),
        ),
        out_specs=(P(("row", "col"), None), P(("row", "col"), None)),
        check_vma=False,
    )
```

time: 361 us -> 82.6 us (0.23)
  matrix products: 159 us -> 0 us
  waiting for transfers between devices: 75 us -> 12.4 us
  blocking collectives: 41 us -> 0 us
  local copies, waits for them, and re-layouts: 42.9 us -> 3.67 us
  starting transfers between devices: 0.08 us -> 34.8 us
  Pallas kernels: 0 us -> 29.1 us
  other arithmetic: 26.6 us -> 1.47 us
  between operations: 14.1 us -> 0.89 us
    dot_general x32 -> x0, matrix products: 159 us -> none  [the longest x16 104 us: group_term(): jnp.einsum('tb,tjc->bjc', weights, products, precision=lax.Precision.HIGH...]
    reduce_scatter x2 -> x0, waiting for transfers between devices: 75 us -> none  [propagate(): lax.psum_scatter(flat_terms.astype(jnp.bfloat16), 'row', scatter_dimensio...]
    all_gather x2 -> x0, blocking collectives: 41 us -> none  [propagate(): gathered = lax.all_gather(labels, 'col', axis=0, tiled=True)]
    gather x16 -> x0, local copies, waits for them, and re-layouts: 39.7 us -> none  [group_term(): picked = jnp.take(sources, row_ids, axis=0)]
    ppermute x0 -> x28, starting transfers between devices: none -> 34.8 us  [flip(): return lax.ppermute(array, axis, [(i, i ^ bits) for i in range(size)])]
    pallas_call x0 -> x18, Pallas kernels: none -> 29.1 us  [the longest x1 15 us: densify(): pl.pallas_call(densify_kernel, grid_spec=pltpu.PrefetchScalarGridSpec(num...]
    ppermute x0 -> x28, waiting for transfers between devices: none -> 12.4 us  [flip(): return lax.ppermute(array, axis, [(i, i ^ bits) for i in range(size)])]
    eq x16 -> x0, other arithmetic: 11.5 us -> none  [group_term(): col_ids[:, None] == jnp.arange(blocks, dtype=jnp.int32)[None, :]]
  transfers between devices with their start and end apart: 2 -> 28, of which waited for: 2 -> 9; matrix products, arithmetic and copies ran while one was open for 0% -> 1% of each run, Pallas kernels for 0% -> 35%
where the time goes in v1:
time: 82.6 us; the launch traced here: 82.3 us
  starting transfers between devices  34.8 us (42%)
  Pallas kernels  29.1 us (35%)
  waiting for transfers between devices  12.4 us (15%)
  local copies, waits for them, and re-layouts  3.67 us (4%)
  other arithmetic  1.47 us (2%)
  between operations  0.89 us (1%)
    ppermute x28, starting transfers between devices, flip(): return lax.ppermute(array, axis, [(i, i ^ bits) for i in range(size)])  34.8 us
    pallas_call x1, Pallas kernels, densify(): pl.pallas_call(densify_kernel, grid_spec=pltpu.PrefetchScalarGridSpec(num...  15 us
    pallas_call x8, Pallas kernels, multiply(): pl.pallas_call(functools.partial(multiply_kernel, len(labels)), grid=(tar...  13.1 us
    ppermute x28, waiting for transfers between devices, flip(): return lax.ppermute(array, axis, [(i, i ^ bits) for i in range(size)])  12.4 us
    unnamed x8, local copies, waits for them, and re-layouts  2.99 us
  transfers between devices with their start and end apart: 28, of which 9 were waited for; matrix products, arithmetic and copies ran while one was open for 1% of the time, Pallas kernels for 35%

profile of v1, /device:TPU:0, one launch (start us, length us, event | category | flops | bytes accessed | tf_op | source)
XLA Modules:
  0.0 82.3 jit_solution(13312994947389609161)
XLA Ops:
  0.6 0.7 broadcast_in_dim.3.seed_ref
  1.3 0.9 %copy-done = bf16[384,256]{1,0:T(8,128)(2,1)S(1)} copy-done((bf16[384,256]{1,0:T(8,128)(2,1)S(1)}, bf16[384,256]{1,0:T(8,128)(2,1)}, u32[]{:S(2)}) %copy-start) | copy-done | bytes 196632
  2.4 3.1 %collective-permute-start = (bf16[128,384]{1,0:T(8,128)(2,1)S(1)}, bf16[128,384]{1,0:T(8,128)(2,1)S(1)}, u32[]{:S(2)}, u32[]{:S(2)}) collective-permute-start(bf16[128,384]{1,0:T(8,128)(2,1)S(1)} %get-tuple-element.24.refs_0_.first_ref), channel_id=1, source_target_pairs={{0,1},{1,0},{2,3},{3,2},{4,5},{5,4},{6,7},{7,6},{8,9},{9,8},{10,11... | collective-permute-start | bytes 294920 | tf_op jit(solution)/shard_map/ppermute | solution.py:183
  5.5 2.6 %collective-permute-start.1 = (bf16[128,384]{1,0:T(8,128)(2,1)S(1)}, bf16[128,384]{1,0:T(8,128)(2,1)S(1)}, u32[]{:S(2)}, u32[]{:S(2)}) collective-permute-start(bf16[128,384]{1,0:T(8,128)(2,1)S(1)} %get-tuple-element.24.refs_0_.first_ref), channel_id=1, source_target_pairs={{0,2},{1,3},{2,0},{3,1},{4,6},{5,7},{6,4},{7,5},{8,10},{9,11},{10,... | collective-permute-start | bytes 294920 | tf_op jit(solution)/shard_map/ppermute | solution.py:183
  8.1 0.9 %collective-permute-start.7 = (bf16[128,384]{1,0:T(8,128)(2,1)S(1)}, bf16[128,384]{1,0:T(8,128)(2,1)S(1)}, u32[]{:S(2)}, u32[]{:S(2)}) collective-permute-start(bf16[128,384]{1,0:T(8,128)(2,1)S(1)} %get-tuple-element.30.refs_0_.first_ref), channel_id=1, source_target_pairs={{0,1},{1,0},{2,3},{3,2},{4,5},{5,4},{6,7},{7,6},{8,9},{9,8},{10,11... | collective-permute-start | bytes 294920 | tf_op jit(solution)/shard_map/ppermute | solution.py:183
  9.0 3.5 %collective-permute-start.8 = (bf16[128,384]{1,0:T(8,128)(2,1)S(1)}, bf16[128,384]{1,0:T(8,128)(2,1)S(1)}, u32[]{:S(2)}, u32[]{:S(2)}) collective-permute-start(bf16[128,384]{1,0:T(8,128)(2,1)S(1)} %get-tuple-element.30.refs_0_.first_ref), channel_id=1, source_target_pairs={{0,2},{1,3},{2,0},{3,1},{4,6},{5,7},{6,4},{7,5},{8,10},{9,11},{10,... | collective-permute-start | bytes 294920 | tf_op jit(solution)/shard_map/ppermute | solution.py:183
  12.5 0.6 collective-permute-start.9
  13.2 0.7 copy-done.1
  13.9 0.7 copy-done.2
  14.6 0.7 copy-done.3
  15.2 15.0 %densify.1.refs_4_ = bf16[8,1536,384]{2,1,0:T(8,128)(2,1)S(1)} custom-call(s32[2]{0:T(128)S(1)} %pad_add_fusion.place_ref, s32[8,48]{1,0:T(8,128)S(1)} %bitcast.5, s32[8,48]{1,0:T(8,128)S(1)} %bitcast.6, s32[8,48]{1,0:T(8,128)S(1)} %bitcast.7, bf16[1,1,8,48,128,128]{5,4,3,2,1,0:T(8,128)(2,1)} %tiles_ref.1), custom_call_target="tpu_custom_call" | custom-call | tf_op jit(solution)/shard_map/densify/pallas_call | solution.py:68
  30.3 1.6 %multiply_theirs.4 = bf16[4,128,384]{2,1,0:T(8,128)(2,1)S(1)} custom-call(bf16[128,384]{1,0:T(8,128)(2,1)S(1)} %get-tuple-element.24.refs_0_.first_ref, bf16[128,384]{1,0:T(8,128)(2,1)S(1)} %collective-permute-done.refs_1_, bf16[128,384]{1,0:T(8,128)(2,1)S(1)} %collective-permute-done.1.refs_2_, bf16[128,384]{1,0:T(8,128)(2,1)S(1)} %collective-permute-done.2.refs_3_, ...), custom_call_target="tpu_custom_call" | custom-call | flops 603979776 | bytes 4718592 | tf_op jit(solution)/shard_map/multiply_theirs/pallas_call | solution.py:105
  32.1 1.6 %multiply_theirs.5 = bf16[4,128,384]{2,1,0:T(8,128)(2,1)S(1)} custom-call(bf16[128,384]{1,0:T(8,128)(2,1)S(1)} %get-tuple-element.30.refs_0_.first_ref, bf16[128,384]{1,0:T(8,128)(2,1)S(1)} %collective-permute-done.7.refs_1_, bf16[128,384]{1,0:T(8,128)(2,1)S(1)} %collective-permute-done.8.refs_2_, bf16[128,384]{1,0:T(8,128)(2,1)S(1)} %collective-permute-done.9.refs_3_, ...), custom_call_target="tpu_custom_call" | custom-call | flops 603979776 | bytes 4718592 | tf_op jit(solution)/shard_map/multiply_theirs/pallas_call | solution.py:105
  33.7 0.5 collective-permute-start.10
  34.3 1.6 %multiply_mine.4.mine_ref = f32[4,128,384]{2,1,0:T(8,128)S(1)} custom-call(bf16[128,384]{1,0:T(8,128)(2,1)S(1)} %get-tuple-element.24.refs_0_.first_ref, bf16[128,384]{1,0:T(8,128)(2,1)S(1)} %collective-permute-done.refs_1_, bf16[128,384]{1,0:T(8,128)(2,1)S(1)} %collective-permute-done.1.refs_2_, bf16[128,384]{1,0:T(8,128)(2,1)S(1)} %collective-permute-done.2.refs_3_, ...), custom_call_target="tpu_custom_call" | custom-call | flops 603979776 | bytes 4718592 | tf_op jit(solution)/shard_map/multiply_mine/pallas_call | solution.py:105
  36.0 1.6 %collective-permute-start.4 = (bf16[128,384]{1,0:T(8,128)(2,1)S(1)}, bf16[128,384]{1,0:T(8,128)(2,1)S(1)}, u32[]{:S(2)}, u32[]{:S(2)}) collective-permute-start(bf16[128,384]{1,0:T(8,128)(2,1)S(1)} %get-tuple-element.26), channel_id=1, source_target_pairs={{0,8},{4,12},{8,0},{12,4},{16,24},{20,28},{24,16},{28,20},{1,9},{5... | collective-permute-start | bytes 294920 | tf_op jit(solution)/shard_map/ppermute | solution.py:183
  37.6 1.5 %collective-permute-start.5 = (bf16[128,384]{1,0:T(8,128)(2,1)S(1)}, bf16[128,384]{1,0:T(8,128)(2,1)S(1)}, u32[]{:S(2)}, u32[]{:S(2)}) collective-permute-start(bf16[128,384]{1,0:T(8,128)(2,1)S(1)} %get-tuple-element.27), channel_id=1, source_target_pairs={{0,16},{4,20},{8,24},{12,28},{16,0},{20,4},{24,8},{28,12},{1,17},{... | collective-permute-start | bytes 294920 | tf_op jit(solution)/shard_map/ppermute | solution.py:183
  39.1 0.5 collective-permute-start.6
  39.6 1.6 %multiply_mine.5.mine_ref = f32[4,128,384]{2,1,0:T(8,128)S(1)} custom-call(bf16[128,384]{1,0:T(8,128)(2,1)S(1)} %get-tuple-element.30.refs_0_.first_ref, bf16[128,384]{1,0:T(8,128)(2,1)S(1)} %collective-permute-done.7.refs_1_, bf16[128,384]{1,0:T(8,128)(2,1)S(1)} %collective-permute-done.8.refs_2_, bf16[128,384]{1,0:T(8,128)(2,1)S(1)} %collective-permute-done.9.refs_3_, ...), custom_call_target="tpu_custom_call" | custom-call | flops 603979776 | bytes 4718592 | tf_op jit(solution)/shard_map/multiply_mine/pallas_call | solution.py:105
  41.3 1.6 %collective-permute-start.11 = (bf16[128,384]{1,0:T(8,128)(2,1)S(1)}, bf16[128,384]{1,0:T(8,128)(2,1)S(1)}, u32[]{:S(2)}, u32[]{:S(2)}) collective-permute-start(bf16[128,384]{1,0:T(8,128)(2,1)S(1)} %get-tuple-element.32), channel_id=1, source_target_pairs={{0,8},{4,12},{8,0},{12,4},{16,24},{20,28},{24,16},{28,20},{1,9},{5... | collective-permute-start | bytes 294920 | tf_op jit(solution)/shard_map/ppermute | solution.py:183
  42.8 1.5 %collective-permute-start.12 = (bf16[128,384]{1,0:T(8,128)(2,1)S(1)}, bf16[128,384]{1,0:T(8,128)(2,1)S(1)}, u32[]{:S(2)}, u32[]{:S(2)}) collective-permute-start(bf16[128,384]{1,0:T(8,128)(2,1)S(1)} %get-tuple-element.33), channel_id=1, source_target_pairs={{0,16},{4,20},{8,24},{12,28},{16,0},{20,4},{24,8},{28,12},{1,17},{... | collective-permute-start | bytes 294920 | tf_op jit(solution)/shard_map/ppermute | solution.py:183
  44.4 0.5 collective-permute-start.13
  44.8 0.3 collective-permute-done.6.refs_3_
  45.4 3.7 %collective-permute-start.15 = (bf16[128,384]{1,0:T(8,128)(2,1)S(1)}, bf16[128,384]{1,0:T(8,128)(2,1)S(1)}, u32[]{:S(2)}, u32[]{:S(2)}) collective-permute-start(bf16[128,384]{1,0:T(8,128)(2,1)S(1)} %get-tuple-element.36.refs_0_.second_ref), channel_id=1, source_target_pairs={{0,2},{1,3},{2,0},{3,1},{4,6},{5,7},{6,4},{7,5},{8,10},{9,11},{10,... | collective-permute-start | bytes 294920 | tf_op jit(solution)/shard_map/ppermute | solution.py:183
  49.1 0.6 collective-permute-start.16
  50.1 3.7 %collective-permute-start.22 = (bf16[128,384]{1,0:T(8,128)(2,1)S(1)}, bf16[128,384]{1,0:T(8,128)(2,1)S(1)}, u32[]{:S(2)}, u32[]{:S(2)}) collective-permute-start(bf16[128,384]{1,0:T(8,128)(2,1)S(1)} %get-tuple-element.41.refs_0_.second_ref), channel_id=1, source_target_pairs={{0,2},{1,3},{2,0},{3,1},{4,6},{5,7},{6,4},{7,5},{8,10},{9,11},{10,... | collective-permute-start | bytes 294920 | tf_op jit(solution)/shard_map/ppermute | solution.py:183
  53.8 0.8 collective-permute-start.23
  54.6 3.0 %collective-permute-done.15.refs_2_ = bf16[128,384]{1,0:T(8,128)(2,1)S(1)} collective-permute-done((bf16[128,384]{1,0:T(8,128)(2,1)S(1)}, bf16[128,384]{1,0:T(8,128)(2,1)S(1)}, u32[]{:S(2)}, u32[]{:S(2)}) %collective-permute-start.15) | collective-permute-done | bytes 98336 | tf_op jit(solution)/shard_map/ppermute | solution.py:183
  57.6 1.6 %multiply_theirs.6 = bf16[4,128,384]{2,1,0:T(8,128)(2,1)S(1)} custom-call(bf16[128,384]{1,0:T(8,128)(2,1)S(1)} %get-tuple-element.36.refs_0_.second_ref, bf16[128,384]{1,0:T(8,128)(2,1)S(1)} %collective-permute-done.14.refs_1_, bf16[128,384]{1,0:T(8,128)(2,1)S(1)} %collective-permute-done.15.refs_2_, bf16[128,384]{1,0:T(8,128)(2,1)S(1)} %collective-permute-done.16.refs_3_, ...), custom_call_target="tpu_custom_call" | custom-call | flops 603979776 | bytes 4718592 | tf_op jit(solution)/shard_map/multiply_theirs/pallas_call | solution.py:105
  59.3 4.2 %collective-permute-done.22.refs_2_ = bf16[128,384]{1,0:T(8,128)(2,1)S(1)} collective-permute-done((bf16[128,384]{1,0:T(8,128)(2,1)S(1)}, bf16[128,384]{1,0:T(8,128)(2,1)S(1)}, u32[]{:S(2)}, u32[]{:S(2)}) %collective-permute-start.22) | collective-permute-done | bytes 98336 | tf_op jit(solution)/shard_map/ppermute | solution.py:183
  63.5 1.6 %multiply_theirs.7 = bf16[4,128,384]{2,1,0:T(8,128)(2,1)S(1)} custom-call(bf16[128,384]{1,0:T(8,128)(2,1)S(1)} %get-tuple-element.41.refs_0_.second_ref, bf16[128,384]{1,0:T(8,128)(2,1)S(1)} %collective-permute-done.21.refs_1_, bf16[128,384]{1,0:T(8,128)(2,1)S(1)} %collective-permute-done.22.refs_2_, bf16[128,384]{1,0:T(8,128)(2,1)S(1)} %collective-permute-done.23.refs_3_, ...), custom_call_target="tpu_custom_call" | custom-call | flops 603979776 | bytes 4718592 | tf_op jit(solution)/shard_map/multiply_theirs/pallas_call | solution.py:105
  65.2 1.6 %multiply_mine.6.mine_ref = f32[4,128,384]{2,1,0:T(8,128)S(1)} custom-call(bf16[128,384]{1,0:T(8,128)(2,1)S(1)} %get-tuple-element.36.refs_0_.second_ref, bf16[128,384]{1,0:T(8,128)(2,1)S(1)} %collective-permute-done.14.refs_1_, bf16[128,384]{1,0:T(8,128)(2,1)S(1)} %collective-permute-done.15.refs_2_, bf16[128,384]{1,0:T(8,128)(2,1)S(1)} %collective-permute-done.16.refs_3_, ...), custom_call_target="tpu_custom_call" | custom-call | flops 603979776 | bytes 4718592 | tf_op jit(solution)/shard_map/multiply_mine/pallas_call | solution.py:105
  67.0 1.6 %collective-permute-start.18 = (bf16[128,384]{1,0:T(8,128)(2,1)S(1)}, bf16[128,384]{1,0:T(8,128)(2,1)S(1)}, u32[]{:S(2)}, u32[]{:S(2)}) collective-permute-start(bf16[128,384]{1,0:T(8,128)(2,1)S(1)} %get-tuple-element.38), channel_id=1, source_target_pairs={{0,8},{4,12},{8,0},{12,4},{16,24},{20,28},{24,16},{28,20},{1,9},{5... | collective-permute-start | bytes 294920 | tf_op jit(solution)/shard_map/ppermute | solution.py:183
  68.5 1.6 %multiply_mine.7.mine_ref = f32[4,128,384]{2,1,0:T(8,128)S(1)} custom-call(bf16[128,384]{1,0:T(8,128)(2,1)S(1)} %get-tuple-element.41.refs_0_.second_ref, bf16[128,384]{1,0:T(8,128)(2,1)S(1)} %collective-permute-done.21.refs_1_, bf16[128,384]{1,0:T(8,128)(2,1)S(1)} %collective-permute-done.22.refs_2_, bf16[128,384]{1,0:T(8,128)(2,1)S(1)} %collective-permute-done.23.refs_3_, ...), custom_call_target="tpu_custom_call" | custom-call | flops 603979776 | bytes 4718592 | tf_op jit(solution)/shard_map/multiply_mine/pallas_call | solution.py:105
  70.2 1.6 %collective-permute-start.19 = (bf16[128,384]{1,0:T(8,128)(2,1)S(1)}, bf16[128,384]{1,0:T(8,128)(2,1)S(1)}, u32[]{:S(2)}, u32[]{:S(2)}) collective-permute-start(bf16[128,384]{1,0:T(8,128)(2,1)S(1)} %get-tuple-element.39), channel_id=1, source_target_pairs={{0,16},{4,20},{8,24},{12,28},{16,0},{20,4},{24,8},{28,12},{1,17},{... | collective-permute-start | bytes 294920 | tf_op jit(solution)/shard_map/ppermute | solution.py:183
  71.7 0.5 collective-permute-start.20
  72.3 1.6 %collective-permute-start.25 = (bf16[128,384]{1,0:T(8,128)(2,1)S(1)}, bf16[128,384]{1,0:T(8,128)(2,1)S(1)}, u32[]{:S(2)}, u32[]{:S(2)}) collective-permute-start(bf16[128,384]{1,0:T(8,128)(2,1)S(1)} %get-tuple-element.43), channel_id=1, source_target_pairs={{0,8},{4,12},{8,0},{12,4},{16,24},{20,28},{24,16},{28,20},{1,9},{5... | collective-permute-start | bytes 294920 | tf_op jit(solution)/shard_map/ppermute | solution.py:183
  73.9 1.5 %collective-permute-start.26 = (bf16[128,384]{1,0:T(8,128)(2,1)S(1)}, bf16[128,384]{1,0:T(8,128)(2,1)S(1)}, u32[]{:S(2)}, u32[]{:S(2)}) collective-permute-start(bf16[128,384]{1,0:T(8,128)(2,1)S(1)} %get-tuple-element.44), channel_id=1, source_target_pairs={{0,16},{4,20},{8,24},{12,28},{16,0},{20,4},{24,8},{28,12},{1,17},{... | collective-permute-start | bytes 294920 | tf_op jit(solution)/shard_map/ppermute | solution.py:183
  75.4 0.5 collective-permute-start.27
  75.9 0.7 pad_maximum_fusion
  76.6 0.3 collective-permute-done.19.refs_2_
  76.8 1.5 %collective-permute-done.20.refs_3_ = bf16[128,384]{1,0:T(8,128)(2,1)S(1)} collective-permute-done((bf16[128,384]{1,0:T(8,128)(2,1)S(1)}, bf16[128,384]{1,0:T(8,128)(2,1)S(1)}, u32[]{:S(2)}, u32[]{:S(2)}) %collective-permute-start.20) | collective-permute-done | bytes 98336 | tf_op jit(solution)/shard_map/ppermute | solution.py:183
  78.3 0.2 label_grad.2
  78.5 1.0 %collective-permute-done.25.refs_1_ = bf16[128,384]{1,0:T(8,128)(2,1)S(1)} collective-permute-done((bf16[128,384]{1,0:T(8,128)(2,1)S(1)}, bf16[128,384]{1,0:T(8,128)(2,1)S(1)}, u32[]{:S(2)}, u32[]{:S(2)}) %collective-permute-start.25) | collective-permute-done | bytes 98336 | tf_op jit(solution)/shard_map/ppermute | solution.py:183
  79.5 1.0 %collective-permute-done.26.refs_2_ = bf16[128,384]{1,0:T(8,128)(2,1)S(1)} collective-permute-done((bf16[128,384]{1,0:T(8,128)(2,1)S(1)}, bf16[128,384]{1,0:T(8,128)(2,1)S(1)}, u32[]{:S(2)}, u32[]{:S(2)}) %collective-permute-start.26) | collective-permute-done | bytes 98336 | tf_op jit(solution)/shard_map/ppermute | solution.py:183
  80.5 1.0 %collective-permute-done.27.refs_3_ = bf16[128,384]{1,0:T(8,128)(2,1)S(1)} collective-permute-done((bf16[128,384]{1,0:T(8,128)(2,1)S(1)}, bf16[128,384]{1,0:T(8,128)(2,1)S(1)}, u32[]{:S(2)}, u32[]{:S(2)}) %collective-permute-start.27) | collective-permute-done | bytes 98336 | tf_op jit(solution)/shard_map/ppermute | solution.py:183
  81.5 0.2 label_grad.3
  81.6 0.7 pad_maximum_fusion.1
  (38 shorter events, 1.3 us)
Async XLA Ops:
  1.3 0.9 %copy-start = (bf16[384,256]{1,0:T(8,128)(2,1)S(1)}, bf16[384,256]{1,0:T(8,128)(2,1)}, u32[]{:S(2)}) copy-start(bf16[384,256]{1,0:T(8,128)(2,1)} %cot_ref.1) | copy-start | bytes 589828
  2.4 10.1 %collective-permute-start = (bf16[128,384]{1,0:T(8,128)(2,1)S(1)}, bf16[128,384]{1,0:T(8,128)(2,1)S(1)}, u32[]{:S(2)}, u32[]{:S(2)}) collective-permute-start(bf16[128,384]{1,0:T(8,128)(2,1)S(1)} %get-tuple-element.24.refs_0_.first_ref), channel_id=1, source_target_pairs={{0,1},{1,0},{2,3},{3,2},{4,5},{5,4},{6,7},{7,6},{8,9},{9,8},{10,11... | collective-permute-start | bytes 294920 | tf_op jit(solution)/shard_map/ppermute | solution.py:183
  5.5 24.8 %collective-permute-start.1 = (bf16[128,384]{1,0:T(8,128)(2,1)S(1)}, bf16[128,384]{1,0:T(8,128)(2,1)S(1)}, u32[]{:S(2)}, u32[]{:S(2)}) collective-permute-start(bf16[128,384]{1,0:T(8,128)(2,1)S(1)} %get-tuple-element.24.refs_0_.first_ref), channel_id=1, source_target_pairs={{0,2},{1,3},{2,0},{3,1},{4,6},{5,7},{6,4},{7,5},{8,10},{9,11},{10,... | collective-permute-start | bytes 294920 | tf_op jit(solution)/shard_map/ppermute | solution.py:183
  8.1 22.2 %collective-permute-start.2 = (bf16[128,384]{1,0:T(8,128)(2,1)S(1)}, bf16[128,384]{1,0:T(8,128)(2,1)S(1)}, u32[]{:S(2)}, u32[]{:S(2)}) collective-permute-start(bf16[128,384]{1,0:T(8,128)(2,1)S(1)} %get-tuple-element.24.refs_0_.first_ref), channel_id=1, source_target_pairs={{0,3},{1,2},{2,1},{3,0},{4,7},{5,6},{6,5},{7,4},{8,11},{9,10},{10,... | collective-permute-start | bytes 294920 | tf_op jit(solution)/shard_map/ppermute | solution.py:183
  8.1 24.0 %collective-permute-start.7 = (bf16[128,384]{1,0:T(8,128)(2,1)S(1)}, bf16[128,384]{1,0:T(8,128)(2,1)S(1)}, u32[]{:S(2)}, u32[]{:S(2)}) collective-permute-start(bf16[128,384]{1,0:T(8,128)(2,1)S(1)} %get-tuple-element.30.refs_0_.first_ref), channel_id=1, source_target_pairs={{0,1},{1,0},{2,3},{3,2},{4,5},{5,4},{6,7},{7,6},{8,9},{9,8},{10,11... | collective-permute-start | bytes 294920 | tf_op jit(solution)/shard_map/ppermute | solution.py:183
  9.0 23.1 %collective-permute-start.8 = (bf16[128,384]{1,0:T(8,128)(2,1)S(1)}, bf16[128,384]{1,0:T(8,128)(2,1)S(1)}, u32[]{:S(2)}, u32[]{:S(2)}) collective-permute-start(bf16[128,384]{1,0:T(8,128)(2,1)S(1)} %get-tuple-element.30.refs_0_.first_ref), channel_id=1, source_target_pairs={{0,2},{1,3},{2,0},{3,1},{4,6},{5,7},{6,4},{7,5},{8,10},{9,11},{10,... | collective-permute-start | bytes 294920 | tf_op jit(solution)/shard_map/ppermute | solution.py:183
  12.5 19.6 %collective-permute-start.9 = (bf16[128,384]{1,0:T(8,128)(2,1)S(1)}, bf16[128,384]{1,0:T(8,128)(2,1)S(1)}, u32[]{:S(2)}, u32[]{:S(2)}) collective-permute-start(bf16[128,384]{1,0:T(8,128)(2,1)S(1)} %get-tuple-element.30.refs_0_.first_ref), channel_id=1, source_target_pairs={{0,3},{1,2},{2,1},{3,0},{4,7},{5,6},{6,5},{7,4},{8,11},{9,10},{10,... | collective-permute-start | bytes 294920 | tf_op jit(solution)/shard_map/ppermute | solution.py:183
  13.2 0.7 copy-start.1
  13.9 0.7 copy-start.2
  14.6 0.7 copy-start.3
  32.0 3.9 %collective-permute-start.3 = (bf16[4,128,384]{2,1,0:T(8,128)(2,1)S(1)}, bf16[4,128,384]{2,1,0:T(8,128)(2,1)S(1)}, u32[]{:S(2)}, u32[]{:S(2)}) collective-permute-start(bf16[4,128,384]{2,1,0:T(8,128)(2,1)S(1)} %multiply_theirs.4), channel_id=1, source_target_pairs={{0,4},{4,0},{8,12},{12,8},{16,20},{20,16},{24,28},{28,24},{1,5},{5... | collective-permute-start | bytes 1179656 | tf_op jit(solution)/shard_map/ppermute | solution.py:183
  33.7 7.5 %collective-permute-start.10 = (bf16[4,128,384]{2,1,0:T(8,128)(2,1)S(1)}, bf16[4,128,384]{2,1,0:T(8,128)(2,1)S(1)}, u32[]{:S(2)}, u32[]{:S(2)}) collective-permute-start(bf16[4,128,384]{2,1,0:T(8,128)(2,1)S(1)} %multiply_theirs.5), channel_id=1, source_target_pairs={{0,4},{4,0},{8,12},{12,8},{16,20},{20,16},{24,28},{28,24},{1,5},{5... | collective-permute-start | bytes 1179656 | tf_op jit(solution)/shard_map/ppermute | solution.py:183
  36.0 8.4 %collective-permute-start.4 = (bf16[128,384]{1,0:T(8,128)(2,1)S(1)}, bf16[128,384]{1,0:T(8,128)(2,1)S(1)}, u32[]{:S(2)}, u32[]{:S(2)}) collective-permute-start(bf16[128,384]{1,0:T(8,128)(2,1)S(1)} %get-tuple-element.26), channel_id=1, source_target_pairs={{0,8},{4,12},{8,0},{12,4},{16,24},{20,28},{24,16},{28,20},{1,9},{5... | collective-permute-start | bytes 294920 | tf_op jit(solution)/shard_map/ppermute | solution.py:183
  37.6 7.3 %collective-permute-start.5 = (bf16[128,384]{1,0:T(8,128)(2,1)S(1)}, bf16[128,384]{1,0:T(8,128)(2,1)S(1)}, u32[]{:S(2)}, u32[]{:S(2)}) collective-permute-start(bf16[128,384]{1,0:T(8,128)(2,1)S(1)} %get-tuple-element.27), channel_id=1, source_target_pairs={{0,16},{4,20},{8,24},{12,28},{16,0},{20,4},{24,8},{28,12},{1,17},{... | collective-permute-start | bytes 294920 | tf_op jit(solution)/shard_map/ppermute | solution.py:183
  39.1 6.1 %collective-permute-start.6 = (bf16[128,384]{1,0:T(8,128)(2,1)S(1)}, bf16[128,384]{1,0:T(8,128)(2,1)S(1)}, u32[]{:S(2)}, u32[]{:S(2)}) collective-permute-start(bf16[128,384]{1,0:T(8,128)(2,1)S(1)} %get-tuple-element.28), channel_id=1, source_target_pairs={{0,24},{4,28},{8,16},{12,20},{16,8},{20,12},{24,0},{28,4},{1,25},{... | collective-permute-start | bytes 294920 | tf_op jit(solution)/shard_map/ppermute | solution.py:183
  41.3 7.8 %collective-permute-start.11 = (bf16[128,384]{1,0:T(8,128)(2,1)S(1)}, bf16[128,384]{1,0:T(8,128)(2,1)S(1)}, u32[]{:S(2)}, u32[]{:S(2)}) collective-permute-start(bf16[128,384]{1,0:T(8,128)(2,1)S(1)} %get-tuple-element.32), channel_id=1, source_target_pairs={{0,8},{4,12},{8,0},{12,4},{16,24},{20,28},{24,16},{28,20},{1,9},{5... | collective-permute-start | bytes 294920 | tf_op jit(solution)/shard_map/ppermute | solution.py:183
  42.8 6.9 %collective-permute-start.12 = (bf16[128,384]{1,0:T(8,128)(2,1)S(1)}, bf16[128,384]{1,0:T(8,128)(2,1)S(1)}, u32[]{:S(2)}, u32[]{:S(2)}) collective-permute-start(bf16[128,384]{1,0:T(8,128)(2,1)S(1)} %get-tuple-element.33), channel_id=1, source_target_pairs={{0,16},{4,20},{8,24},{12,28},{16,0},{20,4},{24,8},{28,12},{1,17},{... | collective-permute-start | bytes 294920 | tf_op jit(solution)/shard_map/ppermute | solution.py:183
  44.4 5.5 %collective-permute-start.13 = (bf16[128,384]{1,0:T(8,128)(2,1)S(1)}, bf16[128,384]{1,0:T(8,128)(2,1)S(1)}, u32[]{:S(2)}, u32[]{:S(2)}) collective-permute-start(bf16[128,384]{1,0:T(8,128)(2,1)S(1)} %get-tuple-element.34), channel_id=1, source_target_pairs={{0,24},{4,28},{8,16},{12,20},{16,8},{20,12},{24,0},{28,4},{1,25},{... | collective-permute-start | bytes 294920 | tf_op jit(solution)/shard_map/ppermute | solution.py:183
  45.3 8.5 %collective-permute-start.14 = (bf16[128,384]{1,0:T(8,128)(2,1)S(1)}, bf16[128,384]{1,0:T(8,128)(2,1)S(1)}, u32[]{:S(2)}, u32[]{:S(2)}) collective-permute-start(bf16[128,384]{1,0:T(8,128)(2,1)S(1)} %get-tuple-element.36.refs_0_.second_ref), channel_id=1, source_target_pairs={{0,1},{1,0},{2,3},{3,2},{4,5},{5,4},{6,7},{7,6},{8,9},{9,8},{10,11... | collective-permute-start | bytes 294920 | tf_op jit(solution)/shard_map/ppermute | solution.py:183
  45.4 12.2 %collective-permute-start.15 = (bf16[128,384]{1,0:T(8,128)(2,1)S(1)}, bf16[128,384]{1,0:T(8,128)(2,1)S(1)}, u32[]{:S(2)}, u32[]{:S(2)}) collective-permute-start(bf16[128,384]{1,0:T(8,128)(2,1)S(1)} %get-tuple-element.36.refs_0_.second_ref), channel_id=1, source_target_pairs={{0,2},{1,3},{2,0},{3,1},{4,6},{5,7},{6,4},{7,5},{8,10},{9,11},{10,... | collective-permute-start | bytes 294920 | tf_op jit(solution)/shard_map/ppermute | solution.py:183
  49.1 8.5 %collective-permute-start.16 = (bf16[128,384]{1,0:T(8,128)(2,1)S(1)}, bf16[128,384]{1,0:T(8,128)(2,1)S(1)}, u32[]{:S(2)}, u32[]{:S(2)}) collective-permute-start(bf16[128,384]{1,0:T(8,128)(2,1)S(1)} %get-tuple-element.36.refs_0_.second_ref), channel_id=1, source_target_pairs={{0,3},{1,2},{2,1},{3,0},{4,7},{5,6},{6,5},{7,4},{8,11},{9,10},{10,... | collective-permute-start | bytes 294920 | tf_op jit(solution)/shard_map/ppermute | solution.py:183
  50.0 9.3 %collective-permute-start.21 = (bf16[128,384]{1,0:T(8,128)(2,1)S(1)}, bf16[128,384]{1,0:T(8,128)(2,1)S(1)}, u32[]{:S(2)}, u32[]{:S(2)}) collective-permute-start(bf16[128,384]{1,0:T(8,128)(2,1)S(1)} %get-tuple-element.41.refs_0_.second_ref), channel_id=1, source_target_pairs={{0,1},{1,0},{2,3},{3,2},{4,5},{5,4},{6,7},{7,6},{8,9},{9,8},{10,11... | collective-permute-start | bytes 294920 | tf_op jit(solution)/shard_map/ppermute | solution.py:183
  50.1 13.4 %collective-permute-start.22 = (bf16[128,384]{1,0:T(8,128)(2,1)S(1)}, bf16[128,384]{1,0:T(8,128)(2,1)S(1)}, u32[]{:S(2)}, u32[]{:S(2)}) collective-permute-start(bf16[128,384]{1,0:T(8,128)(2,1)S(1)} %get-tuple-element.41.refs_0_.second_ref), channel_id=1, source_target_pairs={{0,2},{1,3},{2,0},{3,1},{4,6},{5,7},{6,4},{7,5},{8,10},{9,11},{10,... | collective-permute-start | bytes 294920 | tf_op jit(solution)/shard_map/ppermute | solution.py:183
  53.8 9.7 %collective-permute-start.23 = (bf16[128,384]{1,0:T(8,128)(2,1)S(1)}, bf16[128,384]{1,0:T(8,128)(2,1)S(1)}, u32[]{:S(2)}, u32[]{:S(2)}) collective-permute-start(bf16[128,384]{1,0:T(8,128)(2,1)S(1)} %get-tuple-element.41.refs_0_.second_ref), channel_id=1, source_target_pairs={{0,3},{1,2},{2,1},{3,0},{4,7},{5,6},{6,5},{7,4},{8,11},{9,10},{10,... | collective-permute-start | bytes 294920 | tf_op jit(solution)/shard_map/ppermute | solution.py:183
  59.3 7.6 %collective-permute-start.17 = (bf16[4,128,384]{2,1,0:T(8,128)(2,1)S(1)}, bf16[4,128,384]{2,1,0:T(8,128)(2,1)S(1)}, u32[]{:S(2)}, u32[]{:S(2)}) collective-permute-start(bf16[4,128,384]{2,1,0:T(8,128)(2,1)S(1)} %multiply_theirs.6), channel_id=1, source_target_pairs={{0,4},{4,0},{8,12},{12,8},{16,20},{20,16},{24,28},{28,24},{1,5},{5... | collective-permute-start | bytes 1179656 | tf_op jit(solution)/shard_map/ppermute | solution.py:183
  65.2 7.1 %collective-permute-start.24 = (bf16[4,128,384]{2,1,0:T(8,128)(2,1)S(1)}, bf16[4,128,384]{2,1,0:T(8,128)(2,1)S(1)}, u32[]{:S(2)}, u32[]{:S(2)}) collective-permute-start(bf16[4,128,384]{2,1,0:T(8,128)(2,1)S(1)} %multiply_theirs.7), channel_id=1, source_target_pairs={{0,4},{4,0},{8,12},{12,8},{16,20},{20,16},{24,28},{28,24},{1,5},{5... | collective-permute-start | bytes 1179656 | tf_op jit(solution)/shard_map/ppermute | solution.py:183
  67.0 8.4 %collective-permute-start.18 = (bf16[128,384]{1,0:T(8,128)(2,1)S(1)}, bf16[128,384]{1,0:T(8,128)(2,1)S(1)}, u32[]{:S(2)}, u32[]{:S(2)}) collective-permute-start(bf16[128,384]{1,0:T(8,128)(2,1)S(1)} %get-tuple-element.38), channel_id=1, source_target_pairs={{0,8},{4,12},{8,0},{12,4},{16,24},{20,28},{24,16},{28,20},{1,9},{5... | collective-permute-start | bytes 294920 | tf_op jit(solution)/shard_map/ppermute | solution.py:183
  70.2 6.7 %collective-permute-start.19 = (bf16[128,384]{1,0:T(8,128)(2,1)S(1)}, bf16[128,384]{1,0:T(8,128)(2,1)S(1)}, u32[]{:S(2)}, u32[]{:S(2)}) collective-permute-start(bf16[128,384]{1,0:T(8,128)(2,1)S(1)} %get-tuple-element.39), channel_id=1, source_target_pairs={{0,16},{4,20},{8,24},{12,28},{16,0},{20,4},{24,8},{28,12},{1,17},{... | collective-permute-start | bytes 294920 | tf_op jit(solution)/shard_map/ppermute | solution.py:183
  71.7 6.6 %collective-permute-start.20 = (bf16[128,384]{1,0:T(8,128)(2,1)S(1)}, bf16[128,384]{1,0:T(8,128)(2,1)S(1)}, u32[]{:S(2)}, u32[]{:S(2)}) collective-permute-start(bf16[128,384]{1,0:T(8,128)(2,1)S(1)} %get-tuple-element.40), channel_id=1, source_target_pairs={{0,24},{4,28},{8,16},{12,20},{16,8},{20,12},{24,0},{28,4},{1,25},{... | collective-permute-start | bytes 294920 | tf_op jit(solution)/shard_map/ppermute | solution.py:183
  72.3 7.2 %collective-permute-start.25 = (bf16[128,384]{1,0:T(8,128)(2,1)S(1)}, bf16[128,384]{1,0:T(8,128)(2,1)S(1)}, u32[]{:S(2)}, u32[]{:S(2)}) collective-permute-start(bf16[128,384]{1,0:T(8,128)(2,1)S(1)} %get-tuple-element.43), channel_id=1, source_target_pairs={{0,8},{4,12},{8,0},{12,4},{16,24},{20,28},{24,16},{28,20},{1,9},{5... | collective-permute-start | bytes 294920 | tf_op jit(solution)/shard_map/ppermute | solution.py:183
  73.9 6.6 %collective-permute-start.26 = (bf16[128,384]{1,0:T(8,128)(2,1)S(1)}, bf16[128,384]{1,0:T(8,128)(2,1)S(1)}, u32[]{:S(2)}, u32[]{:S(2)}) collective-permute-start(bf16[128,384]{1,0:T(8,128)(2,1)S(1)} %get-tuple-element.44), channel_id=1, source_target_pairs={{0,16},{4,20},{8,24},{12,28},{16,0},{20,4},{24,8},{28,12},{1,17},{... | collective-permute-start | bytes 294920 | tf_op jit(solution)/shard_map/ppermute | solution.py:183
  75.4 6.1 %collective-permute-start.27 = (bf16[128,384]{1,0:T(8,128)(2,1)S(1)}, bf16[128,384]{1,0:T(8,128)(2,1)S(1)}, u32[]{:S(2)}, u32[]{:S(2)}) collective-permute-start(bf16[128,384]{1,0:T(8,128)(2,1)S(1)} %get-tuple-element.45), channel_id=1, source_target_pairs={{0,24},{4,28},{8,16},{12,20},{16,8},{20,12},{24,0},{28,4},{1,25},{... | collective-permute-start | bytes 294920 | tf_op jit(solution)/shard_map/ppermute | solution.py:183

commit v2 on v0

v2 whole, which is shorter than its diff:
```python
import functools

import jax
import jax.numpy as jnp
from jax import lax
from jax.experimental import pallas as pl
from jax.experimental.pallas import tpu as pltpu
from jax.sharding import PartitionSpec as P

ALPHA = 0.9
CHUNKS = 2
VMEM_LIMIT = 40 * 1024 * 1024
CHEAP = pl.CostEstimate(flops=1, bytes_accessed=1, transcendentals=0)


def params():
    return pltpu.CompilerParams(vmem_limit_bytes=VMEM_LIMIT)


def after(arrays, *others):
    return lax.optimization_barrier((arrays, others))[0]


def keep_of(seed_row, first_class, classes):
    ids = lax.broadcasted_iota(jnp.int32, (classes, seed_row.shape[1]), 0) + first_class
    return ids != seed_row


def prepare_kernel(cot_ref, seed_ref, out_ref, cot, seed, semaphores):
    copies = [
        pltpu.make_async_copy(cot_ref, cot, semaphores.at[0]),
        pltpu.make_async_copy(seed_ref, seed, semaphores.at[1]),
    ]
    for copy in copies:
        copy.start()
    for copy in copies:
        copy.wait()
    part = cot[...].astype(jnp.float32).T
    keep = keep_of(seed[...][None, :], 0, part.shape[0])
    out_ref[...] = jnp.where(keep, part, 0.0).astype(out_ref.dtype)


def prepare(cotangent, seed_label):
    segment, classes = cotangent.shape
    cotangent, seed_label = (
        pltpu.with_memory_space_constraint(array, pltpu.HBM) for array in (cotangent, seed_label)
    )
    return pl.pallas_call(
        prepare_kernel,
        in_specs=[pl.BlockSpec(memory_space=pltpu.HBM)] * 2,
        out_shape=jax.ShapeDtypeStruct((classes, segment), jnp.bfloat16),
        scratch_shapes=[
            pltpu.VMEM(cotangent.shape, cotangent.dtype),
            pltpu.VMEM(seed_label.shape, seed_label.dtype),
            pltpu.SemaphoreType.DMA((2,)),
        ],
        name="prepare",
        compiler_params=params(),
        cost_estimate=CHEAP,
    )(cotangent, seed_label)


def slot_codes(col_place, blocks, tile_rows, tile_cols, tile_scale):
    slots = tile_rows.shape[1]
    ids = jnp.arange(slots, dtype=jnp.int32)
    place = ((tile_rows // blocks) ^ col_place) * blocks + tile_rows % blocks
    codes = (((place << 4) | tile_cols) << 16) | (ids[None, :] << 8) | tile_scale
    position = jnp.sum((codes[:, None, :] < codes[:, :, None]).astype(jnp.int32), axis=-1)
    return jnp.sum(jnp.where(position[:, :, None] == ids, codes[:, :, None], 0), axis=1)


def densify_kernel(odd, place_ref, codes_ref, tiles_ref, out_ref):
    slots, tile = tiles_ref.shape[3], tiles_ref.shape[4]
    depth, segment = out_ref.shape[0], out_ref.shape[1] // pl.num_programs(0)
    step = pl.program_id(0)
    target = jnp.bitwise_xor(place_ref[0], 2 * step + odd)
    base = step * segment
    out_ref[:, pl.ds(pl.multiple_of(base, tile), segment)] = jnp.zeros(
        (depth, segment), out_ref.dtype
    )

    def add(position, carry):
        total, before = carry
        code = codes_ref[target, position]
        block, slot, scale = code >> 16, (code >> 8) & 255, code & 255
        term = tiles_ref[0, 0, 0, slot].astype(jnp.float32) * scale.astype(jnp.float32)
        total = total * (block == before).astype(jnp.float32) + term
        row, col = (block >> 4) * tile, base + (block & 15) * tile
        out_ref[
            pl.ds(pl.multiple_of(row, tile), tile), pl.ds(pl.multiple_of(col, tile), tile)
        ] = total.astype(out_ref.dtype)
        return total, block

    start = (jnp.zeros((tile, tile), jnp.float32), jnp.int32(-1))
    lax.fori_loop(0, slots, add, start, unroll=4)


def densify(place, codes, tile_values, odd, depth, segment):
    _, _, targets, slots, tile, _ = tile_values.shape
    half = targets // 2
    return pl.pallas_call(
        functools.partial(densify_kernel, odd),
        grid_spec=pltpu.PrefetchScalarGridSpec(
            num_scalar_prefetch=2,
            grid=(half,),
            in_specs=[
                pl.BlockSpec(
                    (1, 1, 1, slots, tile, tile),
                    lambda m, place, _: (0, 0, jnp.bitwise_xor(place[0], 2 * m + odd), 0, 0, 0),
                )
            ],
            out_specs=pl.BlockSpec(memory_space=pltpu.VMEM),
        ),
        out_shape=jax.ShapeDtypeStruct((depth, half * segment), jnp.bfloat16),
        name="densify_theirs" if odd else "densify_mine",
        compiler_params=params(),
        cost_estimate=CHEAP,
    )(place, codes, tile_values)


def multiply_kernel(groups, first, rows, start, *refs):
    label_refs, matrix_ref, out_ref = refs[:-2], refs[-2], refs[-1]
    half, _, segment = out_ref.shape
    each = len(label_refs) // groups
    labels = jnp.concatenate(
        [
            jnp.concatenate(
                [ref[first : first + rows, :] for ref in label_refs[i * each : (i + 1) * each]],
                axis=1,
            )
            for i in range(groups)
        ],
        axis=0,
    )
    for i in range(0, half, 2):
        part = jnp.dot(
            labels,
            matrix_ref[:, (start + i) * segment : (start + i + 2) * segment],
            preferred_element_type=jnp.float32,
        )
        out_ref[i] = part[:, :segment].astype(out_ref.dtype)
        out_ref[i + 1] = part[:, segment:].astype(out_ref.dtype)


def multiply(groups, first, rows, matrix, dtype, name, start=0, count=None, weight=0):
    segment = groups[0][0].shape[1]
    depth, width = matrix.shape
    count = width // segment if count is None else count
    total = len(groups) * rows
    return pl.pallas_call(
        functools.partial(multiply_kernel, len(groups), first, rows, start),
        out_shape=jax.ShapeDtypeStruct((count, total, segment), dtype),
        name=name,
        compiler_params=params(),
        cost_estimate=pl.CostEstimate(
            flops=2 * weight * depth * width * rows, bytes_accessed=1, transcendentals=0
        ),
    )(*[label for group in groups for label in group], matrix)


def pair_kernel(mine_ref, *refs):
    count = mine_ref.shape[0]
    theirs_refs, out_refs = refs[:-count], refs[-count:]
    theirs = [ref.at[i] for ref in theirs_refs for i in range(ref.shape[0])]
    for i, out_ref in enumerate(out_refs):
        total = mine_ref[i] + theirs[i][...].astype(jnp.float32)
        out_ref[...] = total.astype(out_ref.dtype)


def pair(mine, theirs):
    count, rows, segment = mine.shape
    return pl.pallas_call(
        pair_kernel,
        out_shape=[jax.ShapeDtypeStruct((rows, segment), jnp.float32)]
        + [jax.ShapeDtypeStruct((rows, segment), jnp.bfloat16)] * (count - 1),
        name="pair_sum",
        compiler_params=params(),
        cost_estimate=CHEAP,
    )(mine, *theirs)


def add_pieces(pieces):
    total = pieces[0][...]
    for piece in pieces[1:]:
        total = total + piece[...].astype(jnp.float32)
    return total


def middle_kernel(first_class, seed_ref, *refs):
    pieces, (grad_ref, next_ref) = refs[:-2], refs[-2:]
    grad = (ALPHA * add_pieces(pieces)).astype(jnp.bfloat16)
    grad_ref[...] = grad
    keep = keep_of(seed_ref[...][None, :], first_class, grad.shape[0])
    next_ref[...] = jnp.where(keep, grad.astype(jnp.float32), 0.0).astype(jnp.bfloat16)


def middle(seed_label, pieces, first_class):
    shape = jax.ShapeDtypeStruct(pieces[0].shape, jnp.bfloat16)
    return pl.pallas_call(
        functools.partial(middle_kernel, first_class),
        out_shape=[shape, shape],
        name="first_grad",
        compiler_params=params(),
        cost_estimate=CHEAP,
    )(seed_label, *pieces)


def transposed_kernel(*refs):
    part_refs, out_ref = refs[:-1], refs[-1]
    rows = part_refs[0].shape[0]
    for i, ref in enumerate(part_refs):
        part = ref[...].astype(jnp.float32).T.astype(out_ref.dtype)
        out_ref[:, i * rows : (i + 1) * rows] = part


def transposed(parts):
    rows, segment = parts[0].shape
    return pl.pallas_call(
        transposed_kernel,
        out_shape=jax.ShapeDtypeStruct((segment, len(parts) * rows), jnp.bfloat16),
        name="first_grad_out",
        compiler_params=params(),
        cost_estimate=CHEAP,
    )(*parts)


def label_part(first, first_ref, second_ref, pieces):
    rows = second_ref.shape[0]
    kept = first_ref[first : first + rows, :].astype(jnp.float32)
    kept = kept + second_ref[...].astype(jnp.float32)
    return (ALPHA * add_pieces(pieces) + (1.0 - ALPHA) * kept).T.astype(jnp.bfloat16)


def label_kernel(first, first_ref, second_ref, *refs):
    refs[-1][...] = label_part(first, first_ref, second_ref, refs[:-1])


def label(first_in, second_in, pieces, first):
    rows, segment = second_in.shape
    return pl.pallas_call(
        functools.partial(label_kernel, first),
        out_shape=jax.ShapeDtypeStruct((segment, rows), jnp.bfloat16),
        name="label_grad",
        compiler_params=params(),
        cost_estimate=CHEAP,
    )(first_in, second_in, *pieces)


def last_label_kernel(first, count, first_ref, second_ref, *refs):
    ready, pieces, out_ref = refs[:count], refs[count:-1], refs[-1]
    rows = second_ref.shape[0]
    for i, ref in enumerate(ready):
        out_ref[:, i * rows : (i + 1) * rows] = ref[...]
    out_ref[:, first : first + rows] = label_part(first, first_ref, second_ref, pieces)


def last_label(first_in, second_in, pieces, first, ready):
    classes, segment = first_in.shape
    return pl.pallas_call(
        functools.partial(last_label_kernel, first, len(ready)),
        out_shape=jax.ShapeDtypeStruct((segment, classes), jnp.bfloat16),
        name="label_grad_out",
        compiler_params=params(),
        cost_estimate=CHEAP,
    )(first_in, second_in, *ready, *pieces)


def flip(array, axis, size, bits):
    return lax.ppermute(array, axis, [(i, i ^ bits) for i in range(size)])


def gather(labels, n_col):
    others = {k: flip(labels, "col", n_col, k) for k in reversed(range(1, n_col))}
    return [labels] + [others[k] for k in range(1, n_col)]


def spread(own_and_others, n_row):
    own, *others = own_and_others
    return [own] + [flip(part, "row", n_row, 2 * (j + 1)) for j, part in enumerate(others)]


def local(n_row, n_col, cotangent, seed_label, tile_values, tile_rows, tile_cols, tile_scale):
    segment, classes = cotangent.shape
    rows, depth = classes // CHUNKS, n_col * segment
    blocks = segment // tile_values.shape[-1]
    firsts = [i * rows for i in range(CHUNKS)]
    col_place = lax.axis_index("col").astype(jnp.int32)
    place = jnp.stack([lax.axis_index("row").astype(jnp.int32), col_place])
    first_in = prepare(cotangent, seed_label)
    codes = slot_codes(col_place, blocks, tile_rows[0, 0], tile_cols[0, 0], tile_scale[0, 0])
    to_theirs = densify(place, codes, tile_values, 1, depth, segment)
    codes = after(codes, to_theirs)
    to_mine = densify(place, codes, tile_values, 0, depth, segment)

    arrived = after(gather(first_in, n_col), to_mine)
    theirs, mines, swapped, pieces = [], [], [], []
    done = to_mine
    for i, first in enumerate(firsts):
        labels = after(arrived, done)
        done = multiply([labels], first, rows, to_theirs, jnp.bfloat16, "multiply_theirs")
        swapped.append(flip(done, "row", n_row, 1))
        if i + 1 < CHUNKS:
            labels = after(arrived, done)
            done = multiply([labels], first, rows, to_mine, jnp.float32, "multiply_mine")
            mines.append(done)
    for i, first in enumerate(firsts):
        if i + 1 == CHUNKS:
            labels = after(arrived, done)
            done = multiply([labels], first, rows, to_mine, jnp.float32, "multiply_mine")
            mines.append(done)
        done = pair(after(mines[i], done), swapped[i : i + 1])
        pieces.append(spread(done, n_row))
    grads, seconds, sources = [], [], []
    for i, first in enumerate(firsts):
        grad, second_in = middle(seed_label, after(pieces[i], done), first)
        done = [grad, second_in]
        grads.append(grad)
        seconds.append(second_in)
        sources.append(gather(second_in, n_col))

    pieces = []
    for i in range(CHUNKS):
        labels = after(sources[i], done)
        theirs = multiply([labels], 0, rows, to_theirs, jnp.bfloat16, "multiply_theirs")
        swapped = flip(theirs, "row", n_row, 1)
        labels = after(sources[i], theirs)
        mine = multiply(
            [labels], 0, rows, to_mine, jnp.float32, "multiply_mine", weight=20
        )
        done = pair(mine, [swapped])
        pieces.append(spread(done, n_row))
    results = []
    for i in range(CHUNKS - 1):
        done = label(first_in, seconds[i], after(pieces[i], done), firsts[i])
        results.append(done)
    first_grad = transposed(after(grads, done))
    pieces = after(pieces[-1], first_grad)
    return first_grad, last_label(first_in, seconds[-1], pieces, firsts[-1], results)


def solution(mesh):
    return jax.shard_map(
        functools.partial(local, mesh.shape["row"], mesh.shape["col"]),
        mesh=mesh,
        in_specs=(
            P(("row", "col"), None),
            P(("row", "col")),
            P("row", "col", None, None, None, None),
            P("row", "col", None, None),
            P("row", "col", None, None),
            P("row", "col", None, None),
        ),
        out_specs=(P(("row", "col"), None), P(("row", "col"), None)),
        check_vma=False,
    )
```

time: 361 us -> 68.5 us (0.19)
  matrix products: 159 us -> 0 us
  waiting for transfers between devices: 75 us -> 12.9 us
  local copies, waits for them, and re-layouts: 42.9 us -> 0.01 us
  blocking collectives: 41 us -> 0 us
  starting transfers between devices: 0.08 us -> 31.5 us
  other arithmetic: 26.6 us -> 1.31 us
  Pallas kernels: 0 us -> 21.7 us
  between operations: 14.1 us -> 0.83 us
    dot_general x32 -> x0, matrix products: 159 us -> none  [the longest x16 104 us: group_term(): jnp.einsum('tb,tjc->bjc', weights, products, precision=lax.Precision.HIGH...]
    reduce_scatter x2 -> x0, waiting for transfers between devices: 75 us -> none  [propagate(): lax.psum_scatter(flat_terms.astype(jnp.bfloat16), 'row', scatter_dimensio...]
    all_gather x2 -> x0, blocking collectives: 41 us -> none  [propagate(): gathered = lax.all_gather(labels, 'col', axis=0, tiled=True)]
    gather x16 -> x0, local copies, waits for them, and re-layouts: 39.7 us -> none  [group_term(): picked = jnp.take(sources, row_ids, axis=0)]
    ppermute x0 -> x25, starting transfers between devices: none -> 31.5 us  [flip(): return lax.ppermute(array, axis, [(i, i ^ bits) for i in range(size)])]
    pallas_call x0 -> x20, Pallas kernels: none -> 21.7 us  [the longest x2 12.1 us: densify(): pl.pallas_call(functools.partial(densify_kernel, odd), grid_spec=pltpu.Pr...]
    ppermute x0 -> x25, waiting for transfers between devices: none -> 12.9 us  [flip(): return lax.ppermute(array, axis, [(i, i ^ bits) for i in range(size)])]
    eq x16 -> x0, other arithmetic: 11.5 us -> none  [group_term(): col_ids[:, None] == jnp.arange(blocks, dtype=jnp.int32)[None, :]]
  transfers between devices with their start and end apart: 2 -> 25, of which waited for: 2 -> 8; matrix products, arithmetic and copies ran while one was open for 0% -> 2% of each run, Pallas kernels for 0% -> 28%
where the time goes in v2:
time: 68.5 us; the launch traced here: 68.2 us
  starting transfers between devices  31.5 us (46%)
  Pallas kernels  21.7 us (32%)
  waiting for transfers between devices  12.9 us (19%)
  other arithmetic  1.31 us (2%)
  between operations  0.83 us (1%)
    ppermute x25, starting transfers between devices, flip(): return lax.ppermute(array, axis, [(i, i ^ bits) for i in range(size)])  31.5 us
    ppermute x25, waiting for transfers between devices, flip(): return lax.ppermute(array, axis, [(i, i ^ bits) for i in range(size)])  12.9 us
    pallas_call x2, Pallas kernels, densify(): pl.pallas_call(functools.partial(densify_kernel, odd), grid_spec=pltpu.Pr...  12.1 us
    pallas_call x8, Pallas kernels, multiply(): pl.pallas_call(functools.partial(multiply_kernel, len(groups), first, row...  6.22 us
  transfers between devices with their start and end apart: 25, of which 8 were waited for; matrix products, arithmetic and copies ran while one was open for 2% of the time, Pallas kernels for 28%

profile of v2, /device:TPU:0, one launch (start us, length us, event | category | flops | bytes accessed | tf_op | source)
XLA Modules:
  0.0 68.2 jit_solution(15419617516738262624)
XLA Ops:
  0.6 1.1 %prepare.1.refs_0_.first_ref = bf16[256,384]{1,0:T(8,128)(2,1)S(1)} custom-call(bf16[384,256]{1,0:T(8,128)(2,1)} %cot_ref.1, s32[384]{0:T(512)} %seed_ref.5), custom_call_target="tpu_custom_call" | custom-call | flops 1 | bytes 1 | tf_op jit(solution)/shard_map/prepare/pallas_call | solution.py:48
  1.7 5.1 %collective-permute-start.2 = (bf16[256,384]{1,0:T(8,128)(2,1)S(1)}, bf16[256,384]{1,0:T(8,128)(2,1)S(1)}, u32[]{:S(2)}, u32[]{:S(2)}) collective-permute-start(bf16[256,384]{1,0:T(8,128)(2,1)S(1)} %prepare.1.refs_0_.first_ref), channel_id=1, source_target_pairs={{0,3},{1,2},{2,1},{3,0},{4,7},{5,6},{6,5},{7,4},{8,11},{9,10},{10,... | collective-permute-start | bytes 589832 | tf_op jit(solution)/shard_map/ppermute | solution.py:269
  6.8 0.6 collective-permute-start
  7.5 0.7 %fusion.7 = s32[8,48]{1,0:T(8,128)S(1)} fusion(s32[1,1,8,48]{3,2,1,0:T(8,128)} %param.11, s32[1,1,8,48]{3,2,1,0:T(8,128)} %param.10, s32[1,1,8,48]{3,2,1,0:T(8,128)} %param.9, s32[48]{0:T(128)S(1)} %iota_shift-left_fusion, s32[]{:T(128)} %axis_index.25), kind=kLoop, calls=%fused_computation.12 | loop fusion | flops 7680 | bytes 6340 | tf_op jit(solution)/shard_map/or | solution.py:67
  8.2 0.3 convert_reduce_fusion
  8.5 0.1 pad_add_fusion.place_ref
  8.6 0.2 select_reduce_fusion.codes_ref
  8.8 6.1 %densify_theirs.1.refs_4_ = bf16[1536,1536]{1,0:T(8,128)(2,1)S(1)} custom-call(s32[2]{0:T(128)S(1)} %pad_add_fusion.place_ref, s32[8,48]{1,0:T(8,128)S(1)} %select_reduce_fusion.codes_ref, bf16[1,1,8,48,128,128]{5,4,3,2,1,0:T(8,128)(2,1)} %tiles_ref.3), custom_call_target="tpu_custom_call" | custom-call | flops 1 | bytes 1 | tf_op jit(solution)/shard_map/densify_theirs/pallas_call | solution.py:101
  14.9 6.1 %densify_mine.1.refs_4_ = bf16[1536,1536]{1,0:T(8,128)(2,1)S(1)} custom-call(s32[2]{0:T(128)S(1)} %pad_add_fusion.place_ref, s32[8,48]{1,0:T(8,128)S(1)} %select_reduce_fusion.codes_ref, bf16[1,1,8,48,128,128]{5,4,3,2,1,0:T(8,128)(2,1)} %tiles_ref.3), custom_call_target="tpu_custom_call" | custom-call | flops 1 | bytes 1 | tf_op jit(solution)/shard_map/densify_mine/pallas_call | solution.py:101
  20.9 2.6 %collective-permute-done.1.refs_2_ = bf16[256,384]{1,0:T(8,128)(2,1)S(1)} collective-permute-done((bf16[256,384]{1,0:T(8,128)(2,1)S(1)}, bf16[256,384]{1,0:T(8,128)(2,1)S(1)}, u32[]{:S(2)}, u32[]{:S(2)}) %collective-permute-start.1) | collective-permute-done | bytes 196640 | tf_op jit(solution)/shard_map/ppermute | solution.py:269
  23.5 0.8 %multiply_theirs.4 = bf16[4,128,384]{2,1,0:T(8,128)(2,1)S(1)} custom-call(bf16[256,384]{1,0:T(8,128)(2,1)S(1)} %prepare.1.refs_0_.first_ref, bf16[256,384]{1,0:T(8,128)(2,1)S(1)} %collective-permute-done.refs_1_, bf16[256,384]{1,0:T(8,128)(2,1)S(1)} %collective-permute-done.1.refs_2_, bf16[256,384]{1,0:T(8,128)(2,1)S(1)} %collective-permute-done.2.refs_3_, ...), custom_call_target="tpu_custom_call" | custom-call | bytes 1 | tf_op jit(solution)/shard_map/multiply_theirs/pallas_call | solution.py:150
  24.4 0.8 %multiply_mine.4.mine_ref = f32[4,128,384]{2,1,0:T(8,128)S(1)} custom-call(bf16[256,384]{1,0:T(8,128)(2,1)S(1)} %prepare.1.refs_0_.first_ref, bf16[256,384]{1,0:T(8,128)(2,1)S(1)} %collective-permute-done.refs_1_, bf16[256,384]{1,0:T(8,128)(2,1)S(1)} %collective-permute-done.1.refs_2_, bf16[256,384]{1,0:T(8,128)(2,1)S(1)} %collective-permute-done.2.refs_3_, ...), custom_call_target="tpu_custom_call" | custom-call | bytes 1 | tf_op jit(solution)/shard_map/multiply_mine/pallas_call | solution.py:150
  25.2 0.8 %multiply_theirs.5 = bf16[4,128,384]{2,1,0:T(8,128)(2,1)S(1)} custom-call(bf16[256,384]{1,0:T(8,128)(2,1)S(1)} %prepare.1.refs_0_.first_ref, bf16[256,384]{1,0:T(8,128)(2,1)S(1)} %collective-permute-done.refs_1_, bf16[256,384]{1,0:T(8,128)(2,1)S(1)} %collective-permute-done.1.refs_2_, bf16[256,384]{1,0:T(8,128)(2,1)S(1)} %collective-permute-done.2.refs_3_, ...), custom_call_target="tpu_custom_call" | custom-call | bytes 1 | tf_op jit(solution)/shard_map/multiply_theirs/pallas_call | solution.py:150
  26.0 0.6 collective-permute-start.7
  26.6 1.6 %collective-permute-start.4 = (bf16[128,384]{1,0:T(8,128)(2,1)S(1)}, bf16[128,384]{1,0:T(8,128)(2,1)S(1)}, u32[]{:S(2)}, u32[]{:S(2)}) collective-permute-start(bf16[128,384]{1,0:T(8,128)(2,1)S(1)} %get-tuple-element.97), channel_id=1, source_target_pairs={{0,8},{4,12},{8,0},{12,4},{16,24},{20,28},{24,16},{28,20},{1,9},{5... | collective-permute-start | bytes 294920 | tf_op jit(solution)/shard_map/ppermute | solution.py:269
  28.2 1.5 %collective-permute-start.5 = (bf16[128,384]{1,0:T(8,128)(2,1)S(1)}, bf16[128,384]{1,0:T(8,128)(2,1)S(1)}, u32[]{:S(2)}, u32[]{:S(2)}) collective-permute-start(bf16[128,384]{1,0:T(8,128)(2,1)S(1)} %get-tuple-element.98), channel_id=1, source_target_pairs={{0,16},{4,20},{8,24},{12,28},{16,0},{20,4},{24,8},{28,12},{1,17},{... | collective-permute-start | bytes 294920 | tf_op jit(solution)/shard_map/ppermute | solution.py:269
  29.7 0.5 collective-permute-start.6
  30.2 0.8 %multiply_mine.5.mine_ref = f32[4,128,384]{2,1,0:T(8,128)S(1)} custom-call(bf16[256,384]{1,0:T(8,128)(2,1)S(1)} %prepare.1.refs_0_.first_ref, bf16[256,384]{1,0:T(8,128)(2,1)S(1)} %collective-permute-done.refs_1_, bf16[256,384]{1,0:T(8,128)(2,1)S(1)} %collective-permute-done.1.refs_2_, bf16[256,384]{1,0:T(8,128)(2,1)S(1)} %collective-permute-done.2.refs_3_, ...), custom_call_target="tpu_custom_call" | custom-call | bytes 1 | tf_op jit(solution)/shard_map/multiply_mine/pallas_call | solution.py:150
  31.0 0.1 pair_sum.5
  31.0 1.6 %collective-permute-start.8 = (bf16[128,384]{1,0:T(8,128)(2,1)S(1)}, bf16[128,384]{1,0:T(8,128)(2,1)S(1)}, u32[]{:S(2)}, u32[]{:S(2)}) collective-permute-start(bf16[128,384]{1,0:T(8,128)(2,1)S(1)} %get-tuple-element.105), channel_id=1, source_target_pairs={{0,8},{4,12},{8,0},{12,4},{16,24},{20,28},{24,16},{28,20},{1,9},{5... | collective-permute-start | bytes 294920 | tf_op jit(solution)/shard_map/ppermute | solution.py:269
  32.6 1.5 %collective-permute-start.9 = (bf16[128,384]{1,0:T(8,128)(2,1)S(1)}, bf16[128,384]{1,0:T(8,128)(2,1)S(1)}, u32[]{:S(2)}, u32[]{:S(2)}) collective-permute-start(bf16[128,384]{1,0:T(8,128)(2,1)S(1)} %get-tuple-element.106), channel_id=1, source_target_pairs={{0,16},{4,20},{8,24},{12,28},{16,0},{20,4},{24,8},{28,12},{1,17},{... | collective-permute-start | bytes 294920 | tf_op jit(solution)/shard_map/ppermute | solution.py:269
  34.1 0.5 collective-permute-start.10
  34.6 1.4 %collective-permute-done.6.refs_3_ = bf16[128,384]{1,0:T(8,128)(2,1)S(1)} collective-permute-done((bf16[128,384]{1,0:T(8,128)(2,1)S(1)}, bf16[128,384]{1,0:T(8,128)(2,1)S(1)}, u32[]{:S(2)}, u32[]{:S(2)}) %collective-permute-start.6) | collective-permute-done | bytes 98336 | tf_op jit(solution)/shard_map/ppermute | solution.py:269
  36.0 0.1 first_grad.2
  36.1 2.5 %collective-permute-start.13 = (bf16[128,384]{1,0:T(8,128)(2,1)S(1)}, bf16[128,384]{1,0:T(8,128)(2,1)S(1)}, u32[]{:S(2)}, u32[]{:S(2)}) collective-permute-start(bf16[128,384]{1,0:T(8,128)(2,1)S(1)} %get-tuple-element.124.refs_0_.second_ref), channel_id=1, source_target_pairs={{0,3},{1,2},{2,1},{3,0},{4,7},{5,6},{6,5},{7,4},{8,11},{9,10},{10,... | collective-permute-start | bytes 294920 | tf_op jit(solution)/shard_map/ppermute | solution.py:269
  38.6 1.9 %collective-permute-start.11 = (bf16[128,384]{1,0:T(8,128)(2,1)S(1)}, bf16[128,384]{1,0:T(8,128)(2,1)S(1)}, u32[]{:S(2)}, u32[]{:S(2)}) collective-permute-start(bf16[128,384]{1,0:T(8,128)(2,1)S(1)} %get-tuple-element.124.refs_0_.second_ref), channel_id=1, source_target_pairs={{0,1},{1,0},{2,3},{3,2},{4,5},{5,4},{6,7},{7,6},{8,9},{9,8},{10,11... | collective-permute-start | bytes 294920 | tf_op jit(solution)/shard_map/ppermute | solution.py:269
  40.5 0.1 first_grad.3
  40.6 2.5 %collective-permute-start.20 = (bf16[128,384]{1,0:T(8,128)(2,1)S(1)}, bf16[128,384]{1,0:T(8,128)(2,1)S(1)}, u32[]{:S(2)}, u32[]{:S(2)}) collective-permute-start(bf16[128,384]{1,0:T(8,128)(2,1)S(1)} %get-tuple-element.136.refs_0_.second_ref), channel_id=1, source_target_pairs={{0,3},{1,2},{2,1},{3,0},{4,7},{5,6},{6,5},{7,4},{8,11},{9,10},{10,... | collective-permute-start | bytes 294920 | tf_op jit(solution)/shard_map/ppermute | solution.py:269
  43.2 3.8 %collective-permute-start.18 = (bf16[128,384]{1,0:T(8,128)(2,1)S(1)}, bf16[128,384]{1,0:T(8,128)(2,1)S(1)}, u32[]{:S(2)}, u32[]{:S(2)}) collective-permute-start(bf16[128,384]{1,0:T(8,128)(2,1)S(1)} %get-tuple-element.136.refs_0_.second_ref), channel_id=1, source_target_pairs={{0,1},{1,0},{2,3},{3,2},{4,5},{5,4},{6,7},{7,6},{8,9},{9,8},{10,11... | collective-permute-start | bytes 294920 | tf_op jit(solution)/shard_map/ppermute | solution.py:269
  47.0 3.8 %collective-permute-done.12.refs_2_ = bf16[128,384]{1,0:T(8,128)(2,1)S(1)} collective-permute-done((bf16[128,384]{1,0:T(8,128)(2,1)S(1)}, bf16[128,384]{1,0:T(8,128)(2,1)S(1)}, u32[]{:S(2)}, u32[]{:S(2)}) %collective-permute-start.12) | collective-permute-done | bytes 98336 | tf_op jit(solution)/shard_map/ppermute | solution.py:269
  50.8 0.8 %multiply_theirs.6 = bf16[4,128,384]{2,1,0:T(8,128)(2,1)S(1)} custom-call(bf16[128,384]{1,0:T(8,128)(2,1)S(1)} %get-tuple-element.124.refs_0_.second_ref, bf16[128,384]{1,0:T(8,128)(2,1)S(1)} %collective-permute-done.11.refs_1_, bf16[128,384]{1,0:T(8,128)(2,1)S(1)} %collective-permute-done.12.refs_2_, bf16[128,384]{1,0:T(8,128)(2,1)S(1)} %collective-permute-done.13.refs_3_, ...), custom_call_target="tpu_custom_call" | custom-call | bytes 1 | tf_op jit(solution)/shard_map/multiply_theirs/pallas_call | solution.py:150
  51.6 0.8 %multiply_mine.6.mine_ref = f32[4,128,384]{2,1,0:T(8,128)S(1)} custom-call(bf16[128,384]{1,0:T(8,128)(2,1)S(1)} %get-tuple-element.124.refs_0_.second_ref, bf16[128,384]{1,0:T(8,128)(2,1)S(1)} %collective-permute-done.11.refs_1_, bf16[128,384]{1,0:T(8,128)(2,1)S(1)} %collective-permute-done.12.refs_2_, bf16[128,384]{1,0:T(8,128)(2,1)S(1)} %collective-permute-done.13.refs_3_, ...), custom_call_target="tpu_custom_call" | custom-call | flops 12079595520 | bytes 1 | tf_op jit(solution)/shard_map/multiply_mine/pallas_call | solution.py:150
  52.4 0.9 %collective-permute-done.14.refs_0_ = bf16[4,128,384]{2,1,0:T(8,128)(2,1)S(1)} collective-permute-done((bf16[4,128,384]{2,1,0:T(8,128)(2,1)S(1)}, bf16[4,128,384]{2,1,0:T(8,128)(2,1)S(1)}, u32[]{:S(2)}, u32[]{:S(2)}) %collective-permute-start.14) | collective-permute-done | bytes 393248 | tf_op jit(solution)/shard_map/ppermute | solution.py:269
  53.4 1.0 %collective-permute-start.15 = (bf16[128,384]{1,0:T(8,128)(2,1)S(1)}, bf16[128,384]{1,0:T(8,128)(2,1)S(1)}, u32[]{:S(2)}, u32[]{:S(2)}) collective-permute-start(bf16[128,384]{1,0:T(8,128)(2,1)S(1)} %get-tuple-element.129), channel_id=1, source_target_pairs={{0,8},{4,12},{8,0},{12,4},{16,24},{20,28},{24,16},{28,20},{1,9},{5... | collective-permute-start | bytes 294920 | tf_op jit(solution)/shard_map/ppermute | solution.py:269
  54.4 1.2 %collective-permute-start.16 = (bf16[128,384]{1,0:T(8,128)(2,1)S(1)}, bf16[128,384]{1,0:T(8,128)(2,1)S(1)}, u32[]{:S(2)}, u32[]{:S(2)}) collective-permute-start(bf16[128,384]{1,0:T(8,128)(2,1)S(1)} %get-tuple-element.130), channel_id=1, source_target_pairs={{0,16},{4,20},{8,24},{12,28},{16,0},{20,4},{24,8},{28,12},{1,17},{... | collective-permute-start | bytes 294920 | tf_op jit(solution)/shard_map/ppermute | solution.py:269
  55.7 1.3 %collective-permute-start.17 = (bf16[128,384]{1,0:T(8,128)(2,1)S(1)}, bf16[128,384]{1,0:T(8,128)(2,1)S(1)}, u32[]{:S(2)}, u32[]{:S(2)}) collective-permute-start(bf16[128,384]{1,0:T(8,128)(2,1)S(1)} %get-tuple-element.131), channel_id=1, source_target_pairs={{0,24},{4,28},{8,16},{12,20},{16,8},{20,12},{24,0},{28,4},{1,25},{... | collective-permute-start | bytes 294920 | tf_op jit(solution)/shard_map/ppermute | solution.py:269
  57.0 0.8 %multiply_theirs.7 = bf16[4,128,384]{2,1,0:T(8,128)(2,1)S(1)} custom-call(bf16[128,384]{1,0:T(8,128)(2,1)S(1)} %get-tuple-element.136.refs_0_.second_ref, bf16[128,384]{1,0:T(8,128)(2,1)S(1)} %collective-permute-done.18.refs_1_, bf16[128,384]{1,0:T(8,128)(2,1)S(1)} %collective-permute-done.19.refs_2_, bf16[128,384]{1,0:T(8,128)(2,1)S(1)} %collective-permute-done.20.refs_3_, ...), custom_call_target="tpu_custom_call" | custom-call | bytes 1 | tf_op jit(solution)/shard_map/multiply_theirs/pallas_call | solution.py:150
  57.8 0.8 %multiply_mine.7.mine_ref = f32[4,128,384]{2,1,0:T(8,128)S(1)} custom-call(bf16[128,384]{1,0:T(8,128)(2,1)S(1)} %get-tuple-element.136.refs_0_.second_ref, bf16[128,384]{1,0:T(8,128)(2,1)S(1)} %collective-permute-done.18.refs_1_, bf16[128,384]{1,0:T(8,128)(2,1)S(1)} %collective-permute-done.19.refs_2_, bf16[128,384]{1,0:T(8,128)(2,1)S(1)} %collective-permute-done.20.refs_3_, ...), custom_call_target="tpu_custom_call" | custom-call | flops 12079595520 | bytes 1 | tf_op jit(solution)/shard_map/multiply_mine/pallas_call | solution.py:150
  58.6 0.9 %collective-permute-done.21.refs_0_ = bf16[4,128,384]{2,1,0:T(8,128)(2,1)S(1)} collective-permute-done((bf16[4,128,384]{2,1,0:T(8,128)(2,1)S(1)}, bf16[4,128,384]{2,1,0:T(8,128)(2,1)S(1)}, u32[]{:S(2)}, u32[]{:S(2)}) %collective-permute-start.21) | collective-permute-done | bytes 393248 | tf_op jit(solution)/shard_map/ppermute | solution.py:269
  59.6 1.0 %collective-permute-start.22 = (bf16[128,384]{1,0:T(8,128)(2,1)S(1)}, bf16[128,384]{1,0:T(8,128)(2,1)S(1)}, u32[]{:S(2)}, u32[]{:S(2)}) collective-permute-start(bf16[128,384]{1,0:T(8,128)(2,1)S(1)} %get-tuple-element.141), channel_id=1, source_target_pairs={{0,8},{4,12},{8,0},{12,4},{16,24},{20,28},{24,16},{28,20},{1,9},{5... | collective-permute-start | bytes 294920 | tf_op jit(solution)/shard_map/ppermute | solution.py:269
  60.6 1.2 %collective-permute-start.23 = (bf16[128,384]{1,0:T(8,128)(2,1)S(1)}, bf16[128,384]{1,0:T(8,128)(2,1)S(1)}, u32[]{:S(2)}, u32[]{:S(2)}) collective-permute-start(bf16[128,384]{1,0:T(8,128)(2,1)S(1)} %get-tuple-element.142), channel_id=1, source_target_pairs={{0,16},{4,20},{8,24},{12,28},{16,0},{20,4},{24,8},{28,12},{1,17},{... | collective-permute-start | bytes 294920 | tf_op jit(solution)/shard_map/ppermute | solution.py:269
  61.9 1.3 %collective-permute-start.24 = (bf16[128,384]{1,0:T(8,128)(2,1)S(1)}, bf16[128,384]{1,0:T(8,128)(2,1)S(1)}, u32[]{:S(2)}, u32[]{:S(2)}) collective-permute-start(bf16[128,384]{1,0:T(8,128)(2,1)S(1)} %get-tuple-element.143), channel_id=1, source_target_pairs={{0,24},{4,28},{8,16},{12,20},{16,8},{20,12},{24,0},{28,4},{1,25},{... | collective-permute-start | bytes 294920 | tf_op jit(solution)/shard_map/ppermute | solution.py:269
  63.2 0.2 label_grad.1.refs_0_
  63.3 0.8 %first_grad_out.1 = bf16[384,256]{1,0:T(8,128)(2,1)} custom-call(bf16[128,384]{1,0:T(8,128)(2,1)S(1)} %get-tuple-element.148.refs_0_, bf16[128,384]{1,0:T(8,128)(2,1)S(1)} %get-tuple-element.149.refs_1_), custom_call_target="tpu_custom_call" | custom-call | flops 1 | bytes 1 | tf_op jit(solution)/shard_map/first_grad_out/pallas_call | solution.py:218
  64.2 0.6 collective-permute-done.22.refs_2_
  64.8 1.5 %collective-permute-done.23.refs_3_ = bf16[128,384]{1,0:T(8,128)(2,1)S(1)} collective-permute-done((bf16[128,384]{1,0:T(8,128)(2,1)S(1)}, bf16[128,384]{1,0:T(8,128)(2,1)S(1)}, u32[]{:S(2)}, u32[]{:S(2)}) %collective-permute-start.23) | collective-permute-done | bytes 98336 | tf_op jit(solution)/shard_map/ppermute | solution.py:269
  66.3 1.1 %collective-permute-done.24.refs_4_ = bf16[128,384]{1,0:T(8,128)(2,1)S(1)} collective-permute-done((bf16[128,384]{1,0:T(8,128)(2,1)S(1)}, bf16[128,384]{1,0:T(8,128)(2,1)S(1)}, u32[]{:S(2)}, u32[]{:S(2)}) %collective-permute-start.24) | collective-permute-done | bytes 98336 | tf_op jit(solution)/shard_map/ppermute | solution.py:269
  67.4 0.8 %label_grad_out.1 = bf16[384,256]{1,0:T(8,128)(2,1)} custom-call(bf16[256,384]{1,0:T(8,128)(2,1)S(1)} %prepare.1.refs_0_.first_ref, bf16[128,384]{1,0:T(8,128)(2,1)S(1)} %get-tuple-element.136.refs_0_.second_ref, bf16[384,128]{1,0:T(8,128)(2,1)S(1)} %label_grad.1.refs_0_, f32[128,384]{1,0:T(8,128)S(1)} %get-tuple-element.150.refs_1_, ...), custom_call_target="tpu_custom_call" | custom-call | flops 1 | bytes 1 | tf_op jit(solution)/shard_map/label_grad_out/pallas_call | solution.py:259
  (29 shorter events, 0.5 us)
Async XLA Ops:
  1.7 19.2 %collective-permute-start.2 = (bf16[256,384]{1,0:T(8,128)(2,1)S(1)}, bf16[256,384]{1,0:T(8,128)(2,1)S(1)}, u32[]{:S(2)}, u32[]{:S(2)}) collective-permute-start(bf16[256,384]{1,0:T(8,128)(2,1)S(1)} %prepare.1.refs_0_.first_ref), channel_id=1, source_target_pairs={{0,3},{1,2},{2,1},{3,0},{4,7},{5,6},{6,5},{7,4},{8,11},{9,10},{10,... | collective-permute-start | bytes 589832 | tf_op jit(solution)/shard_map/ppermute | solution.py:269
  6.8 16.7 %collective-permute-start.1 = (bf16[256,384]{1,0:T(8,128)(2,1)S(1)}, bf16[256,384]{1,0:T(8,128)(2,1)S(1)}, u32[]{:S(2)}, u32[]{:S(2)}) collective-permute-start(bf16[256,384]{1,0:T(8,128)(2,1)S(1)} %prepare.1.refs_0_.first_ref), channel_id=1, source_target_pairs={{0,2},{1,3},{2,0},{3,1},{4,6},{5,7},{6,4},{7,5},{8,10},{9,11},{10,... | collective-permute-start | bytes 589832 | tf_op jit(solution)/shard_map/ppermute | solution.py:269
  6.8 16.7 %collective-permute-start = (bf16[256,384]{1,0:T(8,128)(2,1)S(1)}, bf16[256,384]{1,0:T(8,128)(2,1)S(1)}, u32[]{:S(2)}, u32[]{:S(2)}) collective-permute-start(bf16[256,384]{1,0:T(8,128)(2,1)S(1)} %prepare.1.refs_0_.first_ref), channel_id=1, source_target_pairs={{0,1},{1,0},{2,3},{3,2},{4,5},{5,4},{6,7},{7,6},{8,9},{9,8},{10,11... | collective-permute-start | bytes 589832 | tf_op jit(solution)/shard_map/ppermute | solution.py:269
  24.3 2.2 %collective-permute-start.3 = (bf16[4,128,384]{2,1,0:T(8,128)(2,1)S(1)}, bf16[4,128,384]{2,1,0:T(8,128)(2,1)S(1)}, u32[]{:S(2)}, u32[]{:S(2)}) collective-permute-start(bf16[4,128,384]{2,1,0:T(8,128)(2,1)S(1)} %multiply_theirs.4), channel_id=1, source_target_pairs={{0,4},{4,0},{8,12},{12,8},{16,20},{20,16},{24,28},{28,24},{1,5},{5... | collective-permute-start | bytes 1179656 | tf_op jit(solution)/shard_map/ppermute | solution.py:269
  26.0 10.0 %copy-start = (s32[384]{0:T(512)S(1)}, s32[384]{0:T(512)}, u32[]{:S(2)}) copy-start(s32[384]{0:T(512)} %seed_ref.5) | copy-start | bytes 4612
  26.0 5.0 %collective-permute-start.7 = (bf16[4,128,384]{2,1,0:T(8,128)(2,1)S(1)}, bf16[4,128,384]{2,1,0:T(8,128)(2,1)S(1)}, u32[]{:S(2)}, u32[]{:S(2)}) collective-permute-start(bf16[4,128,384]{2,1,0:T(8,128)(2,1)S(1)} %multiply_theirs.5), channel_id=1, source_target_pairs={{0,4},{4,0},{8,12},{12,8},{16,20},{20,16},{24,28},{28,24},{1,5},{5... | collective-permute-start | bytes 1179656 | tf_op jit(solution)/shard_map/ppermute | solution.py:269
  26.6 7.5 %collective-permute-start.4 = (bf16[128,384]{1,0:T(8,128)(2,1)S(1)}, bf16[128,384]{1,0:T(8,128)(2,1)S(1)}, u32[]{:S(2)}, u32[]{:S(2)}) collective-permute-start(bf16[128,384]{1,0:T(8,128)(2,1)S(1)} %get-tuple-element.97), channel_id=1, source_target_pairs={{0,8},{4,12},{8,0},{12,4},{16,24},{20,28},{24,16},{28,20},{1,9},{5... | collective-permute-start | bytes 294920 | tf_op jit(solution)/shard_map/ppermute | solution.py:269
  28.2 6.4 %collective-permute-start.5 = (bf16[128,384]{1,0:T(8,128)(2,1)S(1)}, bf16[128,384]{1,0:T(8,128)(2,1)S(1)}, u32[]{:S(2)}, u32[]{:S(2)}) collective-permute-start(bf16[128,384]{1,0:T(8,128)(2,1)S(1)} %get-tuple-element.98), channel_id=1, source_target_pairs={{0,16},{4,20},{8,24},{12,28},{16,0},{20,4},{24,8},{28,12},{1,17},{... | collective-permute-start | bytes 294920 | tf_op jit(solution)/shard_map/ppermute | solution.py:269
  29.7 6.3 %collective-permute-start.6 = (bf16[128,384]{1,0:T(8,128)(2,1)S(1)}, bf16[128,384]{1,0:T(8,128)(2,1)S(1)}, u32[]{:S(2)}, u32[]{:S(2)}) collective-permute-start(bf16[128,384]{1,0:T(8,128)(2,1)S(1)} %get-tuple-element.99), channel_id=1, source_target_pairs={{0,24},{4,28},{8,16},{12,20},{16,8},{20,12},{24,0},{28,4},{1,25},{... | collective-permute-start | bytes 294920 | tf_op jit(solution)/shard_map/ppermute | solution.py:269
  31.0 7.6 %collective-permute-start.8 = (bf16[128,384]{1,0:T(8,128)(2,1)S(1)}, bf16[128,384]{1,0:T(8,128)(2,1)S(1)}, u32[]{:S(2)}, u32[]{:S(2)}) collective-permute-start(bf16[128,384]{1,0:T(8,128)(2,1)S(1)} %get-tuple-element.105), channel_id=1, source_target_pairs={{0,8},{4,12},{8,0},{12,4},{16,24},{20,28},{24,16},{28,20},{1,9},{5... | collective-permute-start | bytes 294920 | tf_op jit(solution)/shard_map/ppermute | solution.py:269
  32.6 7.9 %collective-permute-start.9 = (bf16[128,384]{1,0:T(8,128)(2,1)S(1)}, bf16[128,384]{1,0:T(8,128)(2,1)S(1)}, u32[]{:S(2)}, u32[]{:S(2)}) collective-permute-start(bf16[128,384]{1,0:T(8,128)(2,1)S(1)} %get-tuple-element.106), channel_id=1, source_target_pairs={{0,16},{4,20},{8,24},{12,28},{16,0},{20,4},{24,8},{28,12},{1,17},{... | collective-permute-start | bytes 294920 | tf_op jit(solution)/shard_map/ppermute | solution.py:269
  34.1 6.4 %collective-permute-start.10 = (bf16[128,384]{1,0:T(8,128)(2,1)S(1)}, bf16[128,384]{1,0:T(8,128)(2,1)S(1)}, u32[]{:S(2)}, u32[]{:S(2)}) collective-permute-start(bf16[128,384]{1,0:T(8,128)(2,1)S(1)} %get-tuple-element.107), channel_id=1, source_target_pairs={{0,24},{4,28},{8,16},{12,20},{16,8},{20,12},{24,0},{28,4},{1,25},{... | collective-permute-start | bytes 294920 | tf_op jit(solution)/shard_map/ppermute | solution.py:269
  36.1 7.1 %collective-permute-start.13 = (bf16[128,384]{1,0:T(8,128)(2,1)S(1)}, bf16[128,384]{1,0:T(8,128)(2,1)S(1)}, u32[]{:S(2)}, u32[]{:S(2)}) collective-permute-start(bf16[128,384]{1,0:T(8,128)(2,1)S(1)} %get-tuple-element.124.refs_0_.second_ref), channel_id=1, source_target_pairs={{0,3},{1,2},{2,1},{3,0},{4,7},{5,6},{6,5},{7,4},{8,11},{9,10},{10,... | collective-permute-start | bytes 294920 | tf_op jit(solution)/shard_map/ppermute | solution.py:269
  38.6 12.1 %collective-permute-start.12 = (bf16[128,384]{1,0:T(8,128)(2,1)S(1)}, bf16[128,384]{1,0:T(8,128)(2,1)S(1)}, u32[]{:S(2)}, u32[]{:S(2)}) collective-permute-start(bf16[128,384]{1,0:T(8,128)(2,1)S(1)} %get-tuple-element.124.refs_0_.second_ref), channel_id=1, source_target_pairs={{0,2},{1,3},{2,0},{3,1},{4,6},{5,7},{6,4},{7,5},{8,10},{9,11},{10,... | collective-permute-start | bytes 294920 | tf_op jit(solution)/shard_map/ppermute | solution.py:269
  38.6 12.1 %collective-permute-start.11 = (bf16[128,384]{1,0:T(8,128)(2,1)S(1)}, bf16[128,384]{1,0:T(8,128)(2,1)S(1)}, u32[]{:S(2)}, u32[]{:S(2)}) collective-permute-start(bf16[128,384]{1,0:T(8,128)(2,1)S(1)} %get-tuple-element.124.refs_0_.second_ref), channel_id=1, source_target_pairs={{0,1},{1,0},{2,3},{3,2},{4,5},{5,4},{6,7},{7,6},{8,9},{9,8},{10,11... | collective-permute-start | bytes 294920 | tf_op jit(solution)/shard_map/ppermute | solution.py:269
  40.6 15.0 %collective-permute-start.20 = (bf16[128,384]{1,0:T(8,128)(2,1)S(1)}, bf16[128,384]{1,0:T(8,128)(2,1)S(1)}, u32[]{:S(2)}, u32[]{:S(2)}) collective-permute-start(bf16[128,384]{1,0:T(8,128)(2,1)S(1)} %get-tuple-element.136.refs_0_.second_ref), channel_id=1, source_target_pairs={{0,3},{1,2},{2,1},{3,0},{4,7},{5,6},{6,5},{7,4},{8,11},{9,10},{10,... | collective-permute-start | bytes 294920 | tf_op jit(solution)/shard_map/ppermute | solution.py:269
  43.2 13.8 %collective-permute-start.19 = (bf16[128,384]{1,0:T(8,128)(2,1)S(1)}, bf16[128,384]{1,0:T(8,128)(2,1)S(1)}, u32[]{:S(2)}, u32[]{:S(2)}) collective-permute-start(bf16[128,384]{1,0:T(8,128)(2,1)S(1)} %get-tuple-element.136.refs_0_.second_ref), channel_id=1, source_target_pairs={{0,2},{1,3},{2,0},{3,1},{4,6},{5,7},{6,4},{7,5},{8,10},{9,11},{10,... | collective-permute-start | bytes 294920 | tf_op jit(solution)/shard_map/ppermute | solution.py:269
  43.2 13.8 %collective-permute-start.18 = (bf16[128,384]{1,0:T(8,128)(2,1)S(1)}, bf16[128,384]{1,0:T(8,128)(2,1)S(1)}, u32[]{:S(2)}, u32[]{:S(2)}) collective-permute-start(bf16[128,384]{1,0:T(8,128)(2,1)S(1)} %get-tuple-element.136.refs_0_.second_ref), channel_id=1, source_target_pairs={{0,1},{1,0},{2,3},{3,2},{4,5},{5,4},{6,7},{7,6},{8,9},{9,8},{10,11... | collective-permute-start | bytes 294920 | tf_op jit(solution)/shard_map/ppermute | solution.py:269
  51.5 1.8 %collective-permute-start.14 = (bf16[4,128,384]{2,1,0:T(8,128)(2,1)S(1)}, bf16[4,128,384]{2,1,0:T(8,128)(2,1)S(1)}, u32[]{:S(2)}, u32[]{:S(2)}) collective-permute-start(bf16[4,128,384]{2,1,0:T(8,128)(2,1)S(1)} %multiply_theirs.6), channel_id=1, source_target_pairs={{0,4},{4,0},{8,12},{12,8},{16,20},{20,16},{24,28},{28,24},{1,5},{5... | collective-permute-start | bytes 1179656 | tf_op jit(solution)/shard_map/ppermute | solution.py:269
  53.4 8.5 %collective-permute-start.15 = (bf16[128,384]{1,0:T(8,128)(2,1)S(1)}, bf16[128,384]{1,0:T(8,128)(2,1)S(1)}, u32[]{:S(2)}, u32[]{:S(2)}) collective-permute-start(bf16[128,384]{1,0:T(8,128)(2,1)S(1)} %get-tuple-element.129), channel_id=1, source_target_pairs={{0,8},{4,12},{8,0},{12,4},{16,24},{20,28},{24,16},{28,20},{1,9},{5... | collective-permute-start | bytes 294920 | tf_op jit(solution)/shard_map/ppermute | solution.py:269
  54.4 8.8 %collective-permute-start.16 = (bf16[128,384]{1,0:T(8,128)(2,1)S(1)}, bf16[128,384]{1,0:T(8,128)(2,1)S(1)}, u32[]{:S(2)}, u32[]{:S(2)}) collective-permute-start(bf16[128,384]{1,0:T(8,128)(2,1)S(1)} %get-tuple-element.130), channel_id=1, source_target_pairs={{0,16},{4,20},{8,24},{12,28},{16,0},{20,4},{24,8},{28,12},{1,17},{... | collective-permute-start | bytes 294920 | tf_op jit(solution)/shard_map/ppermute | solution.py:269
  55.7 7.5 %collective-permute-start.17 = (bf16[128,384]{1,0:T(8,128)(2,1)S(1)}, bf16[128,384]{1,0:T(8,128)(2,1)S(1)}, u32[]{:S(2)}, u32[]{:S(2)}) collective-permute-start(bf16[128,384]{1,0:T(8,128)(2,1)S(1)} %get-tuple-element.131), channel_id=1, source_target_pairs={{0,24},{4,28},{8,16},{12,20},{16,8},{20,12},{24,0},{28,4},{1,25},{... | collective-permute-start | bytes 294920 | tf_op jit(solution)/shard_map/ppermute | solution.py:269
  57.8 1.8 %collective-permute-start.21 = (bf16[4,128,384]{2,1,0:T(8,128)(2,1)S(1)}, bf16[4,128,384]{2,1,0:T(8,128)(2,1)S(1)}, u32[]{:S(2)}, u32[]{:S(2)}) collective-permute-start(bf16[4,128,384]{2,1,0:T(8,128)(2,1)S(1)} %multiply_theirs.7), channel_id=1, source_target_pairs={{0,4},{4,0},{8,12},{12,8},{16,20},{20,16},{24,28},{28,24},{1,5},{5... | collective-permute-start | bytes 1179656 | tf_op jit(solution)/shard_map/ppermute | solution.py:269
  59.6 5.2 %collective-permute-start.22 = (bf16[128,384]{1,0:T(8,128)(2,1)S(1)}, bf16[128,384]{1,0:T(8,128)(2,1)S(1)}, u32[]{:S(2)}, u32[]{:S(2)}) collective-permute-start(bf16[128,384]{1,0:T(8,128)(2,1)S(1)} %get-tuple-element.141), channel_id=1, source_target_pairs={{0,8},{4,12},{8,0},{12,4},{16,24},{20,28},{24,16},{28,20},{1,9},{5... | collective-permute-start | bytes 294920 | tf_op jit(solution)/shard_map/ppermute | solution.py:269
  60.6 5.7 %collective-permute-start.23 = (bf16[128,384]{1,0:T(8,128)(2,1)S(1)}, bf16[128,384]{1,0:T(8,128)(2,1)S(1)}, u32[]{:S(2)}, u32[]{:S(2)}) collective-permute-start(bf16[128,384]{1,0:T(8,128)(2,1)S(1)} %get-tuple-element.142), channel_id=1, source_target_pairs={{0,16},{4,20},{8,24},{12,28},{16,0},{20,4},{24,8},{28,12},{1,17},{... | collective-permute-start | bytes 294920 | tf_op jit(solution)/shard_map/ppermute | solution.py:269
  61.9 5.5 %collective-permute-start.24 = (bf16[128,384]{1,0:T(8,128)(2,1)S(1)}, bf16[128,384]{1,0:T(8,128)(2,1)S(1)}, u32[]{:S(2)}, u32[]{:S(2)}) collective-permute-start(bf16[128,384]{1,0:T(8,128)(2,1)S(1)} %get-tuple-element.143), channel_id=1, source_target_pairs={{0,24},{4,28},{8,16},{12,20},{16,8},{20,12},{24,0},{28,4},{1,25},{... | collective-permute-start | bytes 294920 | tf_op jit(solution)/shard_map/ppermute | solution.py:269

commit v3 on v2

--- a/solution.py
+++ b/solution.py
@@ -8,7 +8,6 @@
 from jax.sharding import PartitionSpec as P
 
 ALPHA = 0.9
-CHUNKS = 2
 VMEM_LIMIT = 40 * 1024 * 1024
 CHEAP = pl.CostEstimate(flops=1, bytes_accessed=1, transcendentals=0)
 
@@ -179,10 +178,34 @@
     )(mine, *theirs)
 
 
+def halve_kernel(kept_ref, arrived_ref, stay_ref, send_ref):
+    for i in range(kept_ref.shape[0]):
+        total = kept_ref[i] + arrived_ref[i].astype(jnp.float32)
+        if i % 2:
+            send_ref[i // 2] = total.astype(send_ref.dtype)
+        else:
+            stay_ref[i // 2] = total
+
+
+def halve(kept, arrived):
+    count, rows, segment = kept.shape
+    shape = (count // 2, rows, segment)
+    return pl.pallas_call(
+        halve_kernel,
+        out_shape=[
+            jax.ShapeDtypeStruct(shape, jnp.float32),
+            jax.ShapeDtypeStruct(shape, jnp.bfloat16),
+        ],
+        name="halve_sum",
+        compiler_params=params(),
+        cost_estimate=CHEAP,
+    )(kept, arrived)
+
+
 def add_pieces(pieces):
-    total = pieces[0][...]
+    total = pieces[0][...].reshape(pieces[0].shape[-2:])
     for piece in pieces[1:]:
-        total = total + piece[...].astype(jnp.float32)
+        total = total + piece[...].reshape(total.shape).astype(jnp.float32)
     return total
 
 
@@ -195,33 +218,51 @@
 
 
 def middle(seed_label, pieces, first_class):
-    shape = jax.ShapeDtypeStruct(pieces[0].shape, jnp.bfloat16)
+    shape = jax.ShapeDtypeStruct(pieces[0].shape[-2:], jnp.bfloat16)
     return pl.pallas_call(
         functools.partial(middle_kernel, first_class),
         out_shape=[shape, shape],
         name="first_grad",
         compiler_params=params(),
-        cost_estimate=CHEAP,
+        cost_estimate=pl.CostEstimate(
+            flops=10**10 if first_class == 0 else 1, bytes_accessed=1, transcendentals=0
+        ),
     )(seed_label, *pieces)
 
 
-def transposed_kernel(*refs):
-    part_refs, out_ref = refs[:-1], refs[-1]
-    rows = part_refs[0].shape[0]
-    for i, ref in enumerate(part_refs):
-        part = ref[...].astype(jnp.float32).T.astype(out_ref.dtype)
-        out_ref[:, i * rows : (i + 1) * rows] = part
-
-
-def transposed(parts):
-    rows, segment = parts[0].shape
-    return pl.pallas_call(
-        transposed_kernel,
-        out_shape=jax.ShapeDtypeStruct((segment, len(parts) * rows), jnp.bfloat16),
+def turn_kernel(part_ref, out_ref):
+    out_ref[...] = part_ref[...].astype(jnp.float32).T.astype(out_ref.dtype)
+
+
+def turn(part):
+    rows, segment = part.shape
+    return pl.pallas_call(
+        turn_kernel,
+        out_shape=jax.ShapeDtypeStruct((segment, rows), part.dtype),
+        name="turn_grad",
+        compiler_params=params(),
+        cost_estimate=pl.CostEstimate(flops=10**10, bytes_accessed=1, transcendentals=0),
+    )(part)
+
+
+def first_out_kernel(*refs):
+    ready, last_ref, out_ref = refs[:-2], refs[-2], refs[-1]
+    rows = last_ref.shape[0]
+    for i, ref in enumerate(ready):
+        out_ref[:, i * rows : (i + 1) * rows] = ref[...]
+    turned = last_ref[...].astype(jnp.float32).T.astype(out_ref.dtype)
+    out_ref[:, len(ready) * rows :] = turned
+
+
+def first_out(ready, last):
+    rows, segment = last.shape
+    return pl.pallas_call(
+        first_out_kernel,
+        out_shape=jax.ShapeDtypeStruct((segment, (len(ready) + 1) * rows), jnp.bfloat16),
         name="first_grad_out",
         compiler_params=params(),
         cost_estimate=CHEAP,
-    )(*parts)
+    )(*ready, last)
 
 
 def label_part(first, first_ref, second_ref, pieces):
@@ -269,73 +310,78 @@
     return lax.ppermute(array, axis, [(i, i ^ bits) for i in range(size)])
 
 
-def gather(labels, n_col):
-    others = {k: flip(labels, "col", n_col, k) for k in reversed(range(1, n_col))}
-    return [labels] + [others[k] for k in range(1, n_col)]
-
-
-def spread(own_and_others, n_row):
-    own, *others = own_and_others
-    return [own] + [flip(part, "row", n_row, 2 * (j + 1)) for j, part in enumerate(others)]
+def gather(labels, n_col, late=(), waits=()):
+    held = after(labels, waits) if late else labels
+    return [labels] + [
+        flip(held if k in late else labels, "col", n_col, k) for k in range(1, n_col)
+    ]
+
+
+def spread(parts, n_row, late=(), waits=()):
+    own, *others = parts
+    sent = []
+    for j, part in enumerate(others, 1):
+        part = after(part, waits) if j in late else part
+        sent.append(flip(part, "row", n_row, 2 * j))
+    return [own] + sent
 
 
 def local(n_row, n_col, cotangent, seed_label, tile_values, tile_rows, tile_cols, tile_scale):
     segment, classes = cotangent.shape
-    rows, depth = classes // CHUNKS, n_col * segment
-    blocks = segment // tile_values.shape[-1]
-    firsts = [i * rows for i in range(CHUNKS)]
+    rows, depth = classes // 2, n_col * segment
+    blocks, chips = segment // tile_values.shape[-1], n_row // 2
     col_place = lax.axis_index("col").astype(jnp.int32)
     place = jnp.stack([lax.axis_index("row").astype(jnp.int32), col_place])
     first_in = prepare(cotangent, seed_label)
     codes = slot_codes(col_place, blocks, tile_rows[0, 0], tile_cols[0, 0], tile_scale[0, 0])
     to_theirs = densify(place, codes, tile_values, 1, depth, segment)
-    codes = after(codes, to_theirs)
-    to_mine = densify(place, codes, tile_values, 0, depth, segment)
-
-    arrived = after(gather(first_in, n_col), to_mine)
-    theirs, mines, swapped, pieces = [], [], [], []
-    done = to_mine
-    for i, first in enumerate(firsts):
-        labels = after(arrived, done)
-        done = multiply([labels], first, rows, to_theirs, jnp.bfloat16, "multiply_theirs")
-        swapped.append(flip(done, "row", n_row, 1))
-        if i + 1 < CHUNKS:
-            labels = after(arrived, done)
-            done = multiply([labels], first, rows, to_mine, jnp.float32, "multiply_mine")
-            mines.append(done)
-    for i, first in enumerate(firsts):
-        if i + 1 == CHUNKS:
-            labels = after(arrived, done)
-            done = multiply([labels], first, rows, to_mine, jnp.float32, "multiply_mine")
-            mines.append(done)
-        done = pair(after(mines[i], done), swapped[i : i + 1])
-        pieces.append(spread(done, n_row))
-    grads, seconds, sources = [], [], []
-    for i, first in enumerate(firsts):
-        grad, second_in = middle(seed_label, after(pieces[i], done), first)
-        done = [grad, second_in]
-        grads.append(grad)
-        seconds.append(second_in)
-        sources.append(gather(second_in, n_col))
-
-    pieces = []
-    for i in range(CHUNKS):
-        labels = after(sources[i], done)
-        theirs = multiply([labels], 0, rows, to_theirs, jnp.bfloat16, "multiply_theirs")
-        swapped = flip(theirs, "row", n_row, 1)
-        labels = after(sources[i], theirs)
-        mine = multiply(
-            [labels], 0, rows, to_mine, jnp.float32, "multiply_mine", weight=20
+    to_mine = densify(place, after(codes, to_theirs), tile_values, 0, depth, segment)
+
+    def for_theirs(labels, first, waits):
+        labels = after(labels, waits)
+        part = multiply([labels], first, rows, to_theirs, jnp.bfloat16, "multiply_theirs")
+        return part, flip(part, "row", n_row, 1)
+
+    def for_mine(labels, first, waits, weight=0):
+        labels = after(labels, waits)
+        return multiply(
+            [labels], first, rows, to_mine, jnp.float32, "multiply_mine", weight=weight
         )
-        done = pair(mine, [swapped])
-        pieces.append(spread(done, n_row))
-    results = []
-    for i in range(CHUNKS - 1):
-        done = label(first_in, seconds[i], after(pieces[i], done), firsts[i])
-        results.append(done)
-    first_grad = transposed(after(grads, done))
-    pieces = after(pieces[-1], first_grad)
-    return first_grad, last_label(first_in, seconds[-1], pieces, firsts[-1], results)
+
+    arrived = gather(first_in, n_col)
+    theirs, swapped_a = for_theirs(arrived, 0, to_mine)
+    mine = for_mine(arrived, 0, theirs)
+    theirs, swapped_b = for_theirs(arrived, rows, mine)
+    parts_a = pair(after(mine, theirs), [swapped_a])
+    mine = for_mine(arrived, rows, parts_a, 20)
+    pieces_a = spread(parts_a, n_row)
+    done = halve(mine, swapped_b)
+    pieces_b = [done[0], flip(done[1], "row", n_row, 2)]
+
+    grad_a, second_a = middle(seed_label, after(pieces_a, done), 0)
+    done, step = [grad_a, second_a], 4
+    while step < n_row:
+        done = halve(*after(pieces_b, done))
+        pieces_b = [done[0], flip(done[1], "row", n_row, step)]
+        step *= 2
+    sources_a = gather(second_a, n_col, (1,), done)
+    turned_a = turn(after(grad_a, done))
+    grad_b, second_b = middle(seed_label, after(pieces_b, turned_a), rows)
+
+    theirs, swapped_a = for_theirs(sources_a, 0, [grad_b, second_b])
+    mine = for_mine(sources_a, 0, theirs, 20)
+    sources_b = gather(second_b, n_col)
+    parts_a = pair(mine, [swapped_a])
+    theirs, swapped_b = for_theirs(sources_b, 0, parts_a)
+    mine = for_mine(sources_b, 0, theirs, 20)
+    pieces_a = spread(parts_a, n_row)
+    parts_b = pair(mine, [swapped_b])
+    pieces_b = spread(parts_b, n_row)
+
+    label_a = label(first_in, second_a, after(pieces_a, parts_b), 0)
+    first_grad = first_out([turned_a], after(grad_b, label_a))
+    pieces_b = after(pieces_b, first_grad)
+    return first_grad, last_label(first_in, second_b, pieces_b, rows, [label_a])
 
 
 def solution(mesh):

time: 68.5 us -> 66.4 us (0.969)
  starting transfers between devices: 31.5 us -> 28.2 us
  waiting for transfers between devices: 12.9 us -> 14.1 us
    ppermute x25 -> x24, starting transfers between devices: 31.5 us -> 28.2 us  [flip(): return lax.ppermute(array, axis, [(i, i ^ bits) for i in range(size)])]
    ppermute x25 -> x24, waiting for transfers between devices: 12.9 us -> 14.1 us  [flip(): return lax.ppermute(array, axis, [(i, i ^ bits) for i in range(size)])]
  transfers between devices with their start and end apart: 25 -> 24, of which waited for: 8 -> 9; matrix products, arithmetic and copies ran while one was open for 2% -> 2% of each run, Pallas kernels for 28% -> 29%
where the time goes in v3:
time: 66.4 us; the launch traced here: 66.2 us
  starting transfers between devices  28.2 us (42%)
  Pallas kernels  21.7 us (33%)
  waiting for transfers between devices  14.1 us (21%)
  other arithmetic  1.31 us (2%)
  between operations  0.83 us (1%)
    ppermute x24, starting transfers between devices, flip(): return lax.ppermute(array, axis, [(i, i ^ bits) for i in range(size)])  28.2 us
    ppermute x24, waiting for transfers between devices, flip(): return lax.ppermute(array, axis, [(i, i ^ bits) for i in range(size)])  14.1 us
    pallas_call x2, Pallas kernels, densify(): pl.pallas_call(functools.partial(densify_kernel, odd), grid_spec=pltpu.Pr...  12.1 us
    pallas_call x8, Pallas kernels, multiply(): pl.pallas_call(functools.partial(multiply_kernel, len(groups), first, row...  6.22 us
  transfers between devices with their start and end apart: 24, of which 9 were waited for; matrix products, arithmetic and copies ran while one was open for 2% of the time, Pallas kernels for 29%

profile of v3, /device:TPU:0, one launch (start us, length us, event | category | flops | bytes accessed | tf_op | source)
XLA Modules:
  0.0 66.2 jit_solution(15148941370934012029)
XLA Ops:
  0.6 1.1 %prepare.1.refs_0_.first_ref = bf16[256,384]{1,0:T(8,128)(2,1)S(1)} custom-call(bf16[384,256]{1,0:T(8,128)(2,1)} %cot_ref.1, s32[384]{0:T(512)} %seed_ref.5), custom_call_target="tpu_custom_call" | custom-call | flops 1 | bytes 1 | tf_op jit(solution)/shard_map/prepare/pallas_call | solution.py:47
  1.7 5.1 %collective-permute-start.2 = (bf16[256,384]{1,0:T(8,128)(2,1)S(1)}, bf16[256,384]{1,0:T(8,128)(2,1)S(1)}, u32[]{:S(2)}, u32[]{:S(2)}) collective-permute-start(bf16[256,384]{1,0:T(8,128)(2,1)S(1)} %prepare.1.refs_0_.first_ref), channel_id=1, source_target_pairs={{0,3},{1,2},{2,1},{3,0},{4,7},{5,6},{6,5},{7,4},{8,11},{9,10},{10,... | collective-permute-start | bytes 589832 | tf_op jit(solution)/shard_map/ppermute | solution.py:310
  6.8 0.6 collective-permute-start
  7.5 0.7 %fusion.7 = s32[8,48]{1,0:T(8,128)S(1)} fusion(s32[1,1,8,48]{3,2,1,0:T(8,128)} %param.11, s32[1,1,8,48]{3,2,1,0:T(8,128)} %param.10, s32[1,1,8,48]{3,2,1,0:T(8,128)} %param.9, s32[48]{0:T(128)S(1)} %iota_shift-left_fusion, s32[]{:T(128)} %axis_index.25), kind=kLoop, calls=%fused_computation.12 | loop fusion | flops 7680 | bytes 6340 | tf_op jit(solution)/shard_map/or | solution.py:66
  8.2 0.3 convert_reduce_fusion
  8.5 0.1 pad_add_fusion.place_ref
  8.6 0.2 select_reduce_fusion.codes_ref
  8.8 6.1 %densify_theirs.1.refs_4_ = bf16[1536,1536]{1,0:T(8,128)(2,1)S(1)} custom-call(s32[2]{0:T(128)S(1)} %pad_add_fusion.place_ref, s32[8,48]{1,0:T(8,128)S(1)} %select_reduce_fusion.codes_ref, bf16[1,1,8,48,128,128]{5,4,3,2,1,0:T(8,128)(2,1)} %tiles_ref.3), custom_call_target="tpu_custom_call" | custom-call | flops 1 | bytes 1 | tf_op jit(solution)/shard_map/densify_theirs/pallas_call | solution.py:100
  14.9 6.1 %densify_mine.1.refs_4_ = bf16[1536,1536]{1,0:T(8,128)(2,1)S(1)} custom-call(s32[2]{0:T(128)S(1)} %pad_add_fusion.place_ref, s32[8,48]{1,0:T(8,128)S(1)} %select_reduce_fusion.codes_ref, bf16[1,1,8,48,128,128]{5,4,3,2,1,0:T(8,128)(2,1)} %tiles_ref.3), custom_call_target="tpu_custom_call" | custom-call | flops 1 | bytes 1 | tf_op jit(solution)/shard_map/densify_mine/pallas_call | solution.py:100
  20.9 2.6 %collective-permute-done.1.refs_2_ = bf16[256,384]{1,0:T(8,128)(2,1)S(1)} collective-permute-done((bf16[256,384]{1,0:T(8,128)(2,1)S(1)}, bf16[256,384]{1,0:T(8,128)(2,1)S(1)}, u32[]{:S(2)}, u32[]{:S(2)}) %collective-permute-start.1) | collective-permute-done | bytes 196640 | tf_op jit(solution)/shard_map/ppermute | solution.py:310
  23.5 0.8 %multiply_theirs.4 = bf16[4,128,384]{2,1,0:T(8,128)(2,1)S(1)} custom-call(bf16[256,384]{1,0:T(8,128)(2,1)S(1)} %prepare.1.refs_0_.first_ref, bf16[256,384]{1,0:T(8,128)(2,1)S(1)} %collective-permute-done.refs_1_, bf16[256,384]{1,0:T(8,128)(2,1)S(1)} %collective-permute-done.1.refs_2_, bf16[256,384]{1,0:T(8,128)(2,1)S(1)} %collective-permute-done.2.refs_3_, ...), custom_call_target="tpu_custom_call" | custom-call | bytes 1 | tf_op jit(solution)/shard_map/multiply_theirs/pallas_call | solution.py:149
  24.4 0.8 %multiply_mine.4.mine_ref = f32[4,128,384]{2,1,0:T(8,128)S(1)} custom-call(bf16[256,384]{1,0:T(8,128)(2,1)S(1)} %prepare.1.refs_0_.first_ref, bf16[256,384]{1,0:T(8,128)(2,1)S(1)} %collective-permute-done.refs_1_, bf16[256,384]{1,0:T(8,128)(2,1)S(1)} %collective-permute-done.1.refs_2_, bf16[256,384]{1,0:T(8,128)(2,1)S(1)} %collective-permute-done.2.refs_3_, ...), custom_call_target="tpu_custom_call" | custom-call | bytes 1 | tf_op jit(solution)/shard_map/multiply_mine/pallas_call | solution.py:149
  25.2 0.8 %multiply_theirs.5 = bf16[4,128,384]{2,1,0:T(8,128)(2,1)S(1)} custom-call(bf16[256,384]{1,0:T(8,128)(2,1)S(1)} %prepare.1.refs_0_.first_ref, bf16[256,384]{1,0:T(8,128)(2,1)S(1)} %collective-permute-done.refs_1_, bf16[256,384]{1,0:T(8,128)(2,1)S(1)} %collective-permute-done.1.refs_2_, bf16[256,384]{1,0:T(8,128)(2,1)S(1)} %collective-permute-done.2.refs_3_, ...), custom_call_target="tpu_custom_call" | custom-call | bytes 1 | tf_op jit(solution)/shard_map/multiply_theirs/pallas_call | solution.py:149
  26.0 0.6 collective-permute-start.7
  26.6 1.6 %collective-permute-start.4 = (bf16[128,384]{1,0:T(8,128)(2,1)S(1)}, bf16[128,384]{1,0:T(8,128)(2,1)S(1)}, u32[]{:S(2)}, u32[]{:S(2)}) collective-permute-start(bf16[128,384]{1,0:T(8,128)(2,1)S(1)} %get-tuple-element.90), channel_id=1, source_target_pairs={{0,8},{4,12},{8,0},{12,4},{16,24},{20,28},{24,16},{28,20},{1,9},{5... | collective-permute-start | bytes 294920 | tf_op jit(solution)/shard_map/ppermute | solution.py:310
  28.2 1.5 %collective-permute-start.5 = (bf16[128,384]{1,0:T(8,128)(2,1)S(1)}, bf16[128,384]{1,0:T(8,128)(2,1)S(1)}, u32[]{:S(2)}, u32[]{:S(2)}) collective-permute-start(bf16[128,384]{1,0:T(8,128)(2,1)S(1)} %get-tuple-element.91), channel_id=1, source_target_pairs={{0,16},{4,20},{8,24},{12,28},{16,0},{20,4},{24,8},{28,12},{1,17},{... | collective-permute-start | bytes 294920 | tf_op jit(solution)/shard_map/ppermute | solution.py:310
  29.7 0.5 collective-permute-start.6
  30.2 0.8 %multiply_mine.5.kept_ref = f32[4,128,384]{2,1,0:T(8,128)S(1)} custom-call(bf16[256,384]{1,0:T(8,128)(2,1)S(1)} %prepare.1.refs_0_.first_ref, bf16[256,384]{1,0:T(8,128)(2,1)S(1)} %collective-permute-done.refs_1_, bf16[256,384]{1,0:T(8,128)(2,1)S(1)} %collective-permute-done.1.refs_2_, bf16[256,384]{1,0:T(8,128)(2,1)S(1)} %collective-permute-done.2.refs_3_, ...), custom_call_target="tpu_custom_call" | custom-call | flops 12079595520 | bytes 1 | tf_op jit(solution)/shard_map/multiply_mine/pallas_call | solution.py:149
  31.0 1.6 %collective-permute-start.8 = (bf16[2,128,384]{2,1,0:T(8,128)(2,1)S(1)}, bf16[2,128,384]{2,1,0:T(8,128)(2,1)S(1)}, u32[]{:S(2)}, u32[]{:S(2)}) collective-permute-start(bf16[2,128,384]{2,1,0:T(8,128)(2,1)S(1)} %get-tuple-element.98), channel_id=1, source_target_pairs={{0,8},{4,12},{8,0},{12,4},{16,24},{20,28},{24,16},{28,20},{1,9},{5... | collective-permute-start | bytes 589832 | tf_op jit(solution)/shard_map/ppermute | solution.py:310
  32.6 1.2 %collective-permute-done.5.refs_2_ = bf16[128,384]{1,0:T(8,128)(2,1)S(1)} collective-permute-done((bf16[128,384]{1,0:T(8,128)(2,1)S(1)}, bf16[128,384]{1,0:T(8,128)(2,1)S(1)}, u32[]{:S(2)}, u32[]{:S(2)}) %collective-permute-start.5) | collective-permute-done | bytes 98336 | tf_op jit(solution)/shard_map/ppermute | solution.py:310
  33.8 2.4 %collective-permute-done.6.refs_3_ = bf16[128,384]{1,0:T(8,128)(2,1)S(1)} collective-permute-done((bf16[128,384]{1,0:T(8,128)(2,1)S(1)}, bf16[128,384]{1,0:T(8,128)(2,1)S(1)}, u32[]{:S(2)}, u32[]{:S(2)}) %collective-permute-start.6) | collective-permute-done | bytes 98336 | tf_op jit(solution)/shard_map/ppermute | solution.py:310
  36.3 0.1 first_grad.2
  36.3 2.5 %collective-permute-start.12 = (bf16[128,384]{1,0:T(8,128)(2,1)S(1)}, bf16[128,384]{1,0:T(8,128)(2,1)S(1)}, u32[]{:S(2)}, u32[]{:S(2)}) collective-permute-start(bf16[128,384]{1,0:T(8,128)(2,1)S(1)} %get-tuple-element.119.refs_0_.second_ref), channel_id=1, source_target_pairs={{0,3},{1,2},{2,1},{3,0},{4,7},{5,6},{6,5},{7,4},{8,11},{9,10},{10,... | collective-permute-start | bytes 294920 | tf_op jit(solution)/shard_map/ppermute | solution.py:310
  38.9 0.8 %collective-permute-start.9 = (bf16[1,128,384]{2,1,0:T(8,128)(2,1)S(1)}, bf16[1,128,384]{2,1,0:T(8,128)(2,1)S(1)}, u32[]{:S(2)}, u32[]{:S(2)}) collective-permute-start(bf16[1,128,384]{2,1,0:T(8,128)(2,1)S(1)} %get-tuple-element.108), channel_id=1, source_target_pairs={{0,16},{4,20},{8,24},{12,28},{16,0},{20,4},{24,8},{28,12},{1,17},{... | collective-permute-start | bytes 294920 | tf_op jit(solution)/shard_map/ppermute | solution.py:310
  39.8 1.6 %collective-permute-start.10 = (bf16[128,384]{1,0:T(8,128)(2,1)S(1)}, bf16[128,384]{1,0:T(8,128)(2,1)S(1)}, u32[]{:S(2)}, u32[]{:S(2)}) collective-permute-start(bf16[128,384]{1,0:T(8,128)(2,1)S(1)} %get-tuple-element.119.refs_0_.second_ref), channel_id=1, source_target_pairs={{0,1},{1,0},{2,3},{3,2},{4,5},{5,4},{6,7},{7,6},{8,9},{9,8},{10,11... | collective-permute-start | bytes 294920 | tf_op jit(solution)/shard_map/ppermute | solution.py:310
  41.4 0.1 turn_grad.1.refs_0_
  41.5 2.1 %collective-permute-done.9.refs_1_ = bf16[1,128,384]{2,1,0:T(8,128)(2,1)S(1)} collective-permute-done((bf16[1,128,384]{2,1,0:T(8,128)(2,1)S(1)}, bf16[1,128,384]{2,1,0:T(8,128)(2,1)S(1)}, u32[]{:S(2)}, u32[]{:S(2)}) %collective-permute-start.9) | collective-permute-done | bytes 98336 | tf_op jit(solution)/shard_map/ppermute | solution.py:310
  43.7 1.8 %collective-permute-start.19 = (bf16[128,384]{1,0:T(8,128)(2,1)S(1)}, bf16[128,384]{1,0:T(8,128)(2,1)S(1)}, u32[]{:S(2)}, u32[]{:S(2)}) collective-permute-start(bf16[128,384]{1,0:T(8,128)(2,1)S(1)} %get-tuple-element.131.refs_0_.second_ref), channel_id=1, source_target_pairs={{0,3},{1,2},{2,1},{3,0},{4,7},{5,6},{6,5},{7,4},{8,11},{9,10},{10,... | collective-permute-start | bytes 294920 | tf_op jit(solution)/shard_map/ppermute | solution.py:310
  45.5 1.6 %collective-permute-start.18 = (bf16[128,384]{1,0:T(8,128)(2,1)S(1)}, bf16[128,384]{1,0:T(8,128)(2,1)S(1)}, u32[]{:S(2)}, u32[]{:S(2)}) collective-permute-start(bf16[128,384]{1,0:T(8,128)(2,1)S(1)} %get-tuple-element.131.refs_0_.second_ref), channel_id=1, source_target_pairs={{0,2},{1,3},{2,0},{3,1},{4,6},{5,7},{6,4},{7,5},{8,10},{9,11},{10,... | collective-permute-start | bytes 294920 | tf_op jit(solution)/shard_map/ppermute | solution.py:310
  47.1 1.0 %collective-permute-start.17 = (bf16[128,384]{1,0:T(8,128)(2,1)S(1)}, bf16[128,384]{1,0:T(8,128)(2,1)S(1)}, u32[]{:S(2)}, u32[]{:S(2)}) collective-permute-start(bf16[128,384]{1,0:T(8,128)(2,1)S(1)} %get-tuple-element.131.refs_0_.second_ref), channel_id=1, source_target_pairs={{0,1},{1,0},{2,3},{3,2},{4,5},{5,4},{6,7},{7,6},{8,9},{9,8},{10,11... | collective-permute-start | bytes 294920 | tf_op jit(solution)/shard_map/ppermute | solution.py:310
  48.1 0.6 collective-permute-done.11.refs_2_
  48.7 0.8 %multiply_theirs.6 = bf16[4,128,384]{2,1,0:T(8,128)(2,1)S(1)} custom-call(bf16[128,384]{1,0:T(8,128)(2,1)S(1)} %get-tuple-element.119.refs_0_.second_ref, bf16[128,384]{1,0:T(8,128)(2,1)S(1)} %collective-permute-done.10.refs_1_, bf16[128,384]{1,0:T(8,128)(2,1)S(1)} %collective-permute-done.11.refs_2_, bf16[128,384]{1,0:T(8,128)(2,1)S(1)} %collective-permute-done.12.refs_3_, ...), custom_call_target="tpu_custom_call" | custom-call | bytes 1 | tf_op jit(solution)/shard_map/multiply_theirs/pallas_call | solution.py:149
  49.6 0.8 %multiply_mine.6.mine_ref = f32[4,128,384]{2,1,0:T(8,128)S(1)} custom-call(bf16[128,384]{1,0:T(8,128)(2,1)S(1)} %get-tuple-element.119.refs_0_.second_ref, bf16[128,384]{1,0:T(8,128)(2,1)S(1)} %collective-permute-done.10.refs_1_, bf16[128,384]{1,0:T(8,128)(2,1)S(1)} %collective-permute-done.11.refs_2_, bf16[128,384]{1,0:T(8,128)(2,1)S(1)} %collective-permute-done.12.refs_3_, ...), custom_call_target="tpu_custom_call" | custom-call | flops 12079595520 | bytes 1 | tf_op jit(solution)/shard_map/multiply_mine/pallas_call | solution.py:149
  50.4 0.9 %collective-permute-done.13.refs_0_ = bf16[4,128,384]{2,1,0:T(8,128)(2,1)S(1)} collective-permute-done((bf16[4,128,384]{2,1,0:T(8,128)(2,1)S(1)}, bf16[4,128,384]{2,1,0:T(8,128)(2,1)S(1)}, u32[]{:S(2)}, u32[]{:S(2)}) %collective-permute-start.13) | collective-permute-done | bytes 393248 | tf_op jit(solution)/shard_map/ppermute | solution.py:310
  51.4 1.1 %collective-permute-start.14 = (bf16[128,384]{1,0:T(8,128)(2,1)S(1)}, bf16[128,384]{1,0:T(8,128)(2,1)S(1)}, u32[]{:S(2)}, u32[]{:S(2)}) collective-permute-start(bf16[128,384]{1,0:T(8,128)(2,1)S(1)} %get-tuple-element.124), channel_id=1, source_target_pairs={{0,8},{4,12},{8,0},{12,4},{16,24},{20,28},{24,16},{28,20},{1,9},{5... | collective-permute-start | bytes 294920 | tf_op jit(solution)/shard_map/ppermute | solution.py:310
  52.5 0.2 collective-permute-start.15
  52.7 2.2 %collective-permute-start.16 = (bf16[128,384]{1,0:T(8,128)(2,1)S(1)}, bf16[128,384]{1,0:T(8,128)(2,1)S(1)}, u32[]{:S(2)}, u32[]{:S(2)}) collective-permute-start(bf16[128,384]{1,0:T(8,128)(2,1)S(1)} %get-tuple-element.126), channel_id=1, source_target_pairs={{0,24},{4,28},{8,16},{12,20},{16,8},{20,12},{24,0},{28,4},{1,25},{... | collective-permute-start | bytes 294920 | tf_op jit(solution)/shard_map/ppermute | solution.py:310
  54.9 0.8 %multiply_theirs.7 = bf16[4,128,384]{2,1,0:T(8,128)(2,1)S(1)} custom-call(bf16[128,384]{1,0:T(8,128)(2,1)S(1)} %get-tuple-element.131.refs_0_.second_ref, bf16[128,384]{1,0:T(8,128)(2,1)S(1)} %collective-permute-done.17.refs_1_, bf16[128,384]{1,0:T(8,128)(2,1)S(1)} %collective-permute-done.18.refs_2_, bf16[128,384]{1,0:T(8,128)(2,1)S(1)} %collective-permute-done.19.refs_3_, ...), custom_call_target="tpu_custom_call" | custom-call | bytes 1 | tf_op jit(solution)/shard_map/multiply_theirs/pallas_call | solution.py:149
  55.8 0.8 %multiply_mine.7.mine_ref = f32[4,128,384]{2,1,0:T(8,128)S(1)} custom-call(bf16[128,384]{1,0:T(8,128)(2,1)S(1)} %get-tuple-element.131.refs_0_.second_ref, bf16[128,384]{1,0:T(8,128)(2,1)S(1)} %collective-permute-done.17.refs_1_, bf16[128,384]{1,0:T(8,128)(2,1)S(1)} %collective-permute-done.18.refs_2_, bf16[128,384]{1,0:T(8,128)(2,1)S(1)} %collective-permute-done.19.refs_3_, ...), custom_call_target="tpu_custom_call" | custom-call | flops 12079595520 | bytes 1 | tf_op jit(solution)/shard_map/multiply_mine/pallas_call | solution.py:149
  56.6 0.9 %collective-permute-done.20.refs_0_ = bf16[4,128,384]{2,1,0:T(8,128)(2,1)S(1)} collective-permute-done((bf16[4,128,384]{2,1,0:T(8,128)(2,1)S(1)}, bf16[4,128,384]{2,1,0:T(8,128)(2,1)S(1)}, u32[]{:S(2)}, u32[]{:S(2)}) %collective-permute-start.20) | collective-permute-done | bytes 393248 | tf_op jit(solution)/shard_map/ppermute | solution.py:310
  57.6 1.1 %collective-permute-start.21 = (bf16[128,384]{1,0:T(8,128)(2,1)S(1)}, bf16[128,384]{1,0:T(8,128)(2,1)S(1)}, u32[]{:S(2)}, u32[]{:S(2)}) collective-permute-start(bf16[128,384]{1,0:T(8,128)(2,1)S(1)} %get-tuple-element.136), channel_id=1, source_target_pairs={{0,8},{4,12},{8,0},{12,4},{16,24},{20,28},{24,16},{28,20},{1,9},{5... | collective-permute-start | bytes 294920 | tf_op jit(solution)/shard_map/ppermute | solution.py:310
  58.7 0.2 collective-permute-start.22
  58.9 2.2 %collective-permute-start.23 = (bf16[128,384]{1,0:T(8,128)(2,1)S(1)}, bf16[128,384]{1,0:T(8,128)(2,1)S(1)}, u32[]{:S(2)}, u32[]{:S(2)}) collective-permute-start(bf16[128,384]{1,0:T(8,128)(2,1)S(1)} %get-tuple-element.138), channel_id=1, source_target_pairs={{0,24},{4,28},{8,16},{12,20},{16,8},{20,12},{24,0},{28,4},{1,25},{... | collective-permute-start | bytes 294920 | tf_op jit(solution)/shard_map/ppermute | solution.py:310
  61.1 0.2 label_grad.1.refs_0_
  61.3 0.8 %first_grad_out.1 = bf16[384,256]{1,0:T(8,128)(2,1)} custom-call(bf16[384,128]{1,0:T(8,128)(2,1)S(1)} %turn_grad.1.refs_0_, bf16[128,384]{1,0:T(8,128)(2,1)S(1)} %get-tuple-element.143.refs_1_), custom_call_target="tpu_custom_call" | custom-call | flops 1 | bytes 1 | tf_op jit(solution)/shard_map/first_grad_out/pallas_call | solution.py:259
  62.1 0.5 collective-permute-done.21.refs_2_
  62.6 2.7 %collective-permute-done.22.refs_3_ = bf16[128,384]{1,0:T(8,128)(2,1)S(1)} collective-permute-done((bf16[128,384]{1,0:T(8,128)(2,1)S(1)}, bf16[128,384]{1,0:T(8,128)(2,1)S(1)}, u32[]{:S(2)}, u32[]{:S(2)}) %collective-permute-start.22) | collective-permute-done | bytes 98336 | tf_op jit(solution)/shard_map/ppermute | solution.py:310
  65.3 0.8 %label_grad_out.1 = bf16[384,256]{1,0:T(8,128)(2,1)} custom-call(bf16[256,384]{1,0:T(8,128)(2,1)S(1)} %prepare.1.refs_0_.first_ref, bf16[128,384]{1,0:T(8,128)(2,1)S(1)} %get-tuple-element.131.refs_0_.second_ref, bf16[384,128]{1,0:T(8,128)(2,1)S(1)} %label_grad.1.refs_0_, f32[128,384]{1,0:T(8,128)S(1)} %get-tuple-element.144.refs_1_, ...), custom_call_target="tpu_custom_call" | custom-call | flops 1 | bytes 1 | tf_op jit(solution)/shard_map/label_grad_out/pallas_call | solution.py:300
  (29 shorter events, 0.6 us)
Async XLA Ops:
  1.7 19.2 %collective-permute-start.2 = (bf16[256,384]{1,0:T(8,128)(2,1)S(1)}, bf16[256,384]{1,0:T(8,128)(2,1)S(1)}, u32[]{:S(2)}, u32[]{:S(2)}) collective-permute-start(bf16[256,384]{1,0:T(8,128)(2,1)S(1)} %prepare.1.refs_0_.first_ref), channel_id=1, source_target_pairs={{0,3},{1,2},{2,1},{3,0},{4,7},{5,6},{6,5},{7,4},{8,11},{9,10},{10,... | collective-permute-start | bytes 589832 | tf_op jit(solution)/shard_map/ppermute | solution.py:310
  6.8 16.7 %collective-permute-start.1 = (bf16[256,384]{1,0:T(8,128)(2,1)S(1)}, bf16[256,384]{1,0:T(8,128)(2,1)S(1)}, u32[]{:S(2)}, u32[]{:S(2)}) collective-permute-start(bf16[256,384]{1,0:T(8,128)(2,1)S(1)} %prepare.1.refs_0_.first_ref), channel_id=1, source_target_pairs={{0,2},{1,3},{2,0},{3,1},{4,6},{5,7},{6,4},{7,5},{8,10},{9,11},{10,... | collective-permute-start | bytes 589832 | tf_op jit(solution)/shard_map/ppermute | solution.py:310
  6.8 16.7 %collective-permute-start = (bf16[256,384]{1,0:T(8,128)(2,1)S(1)}, bf16[256,384]{1,0:T(8,128)(2,1)S(1)}, u32[]{:S(2)}, u32[]{:S(2)}) collective-permute-start(bf16[256,384]{1,0:T(8,128)(2,1)S(1)} %prepare.1.refs_0_.first_ref), channel_id=1, source_target_pairs={{0,1},{1,0},{2,3},{3,2},{4,5},{5,4},{6,7},{7,6},{8,9},{9,8},{10,11... | collective-permute-start | bytes 589832 | tf_op jit(solution)/shard_map/ppermute | solution.py:310
  24.3 2.2 %collective-permute-start.3 = (bf16[4,128,384]{2,1,0:T(8,128)(2,1)S(1)}, bf16[4,128,384]{2,1,0:T(8,128)(2,1)S(1)}, u32[]{:S(2)}, u32[]{:S(2)}) collective-permute-start(bf16[4,128,384]{2,1,0:T(8,128)(2,1)S(1)} %multiply_theirs.4), channel_id=1, source_target_pairs={{0,4},{4,0},{8,12},{12,8},{16,20},{20,16},{24,28},{28,24},{1,5},{5... | collective-permute-start | bytes 1179656 | tf_op jit(solution)/shard_map/ppermute | solution.py:310
  26.0 5.0 %collective-permute-start.7 = (bf16[4,128,384]{2,1,0:T(8,128)(2,1)S(1)}, bf16[4,128,384]{2,1,0:T(8,128)(2,1)S(1)}, u32[]{:S(2)}, u32[]{:S(2)}) collective-permute-start(bf16[4,128,384]{2,1,0:T(8,128)(2,1)S(1)} %multiply_theirs.5), channel_id=1, source_target_pairs={{0,4},{4,0},{8,12},{12,8},{16,20},{20,16},{24,28},{28,24},{1,5},{5... | collective-permute-start | bytes 1179656 | tf_op jit(solution)/shard_map/ppermute | solution.py:310
  26.6 6.0 %collective-permute-start.4 = (bf16[128,384]{1,0:T(8,128)(2,1)S(1)}, bf16[128,384]{1,0:T(8,128)(2,1)S(1)}, u32[]{:S(2)}, u32[]{:S(2)}) collective-permute-start(bf16[128,384]{1,0:T(8,128)(2,1)S(1)} %get-tuple-element.90), channel_id=1, source_target_pairs={{0,8},{4,12},{8,0},{12,4},{16,24},{20,28},{24,16},{28,20},{1,9},{5... | collective-permute-start | bytes 294920 | tf_op jit(solution)/shard_map/ppermute | solution.py:310
  28.2 5.7 %collective-permute-start.5 = (bf16[128,384]{1,0:T(8,128)(2,1)S(1)}, bf16[128,384]{1,0:T(8,128)(2,1)S(1)}, u32[]{:S(2)}, u32[]{:S(2)}) collective-permute-start(bf16[128,384]{1,0:T(8,128)(2,1)S(1)} %get-tuple-element.91), channel_id=1, source_target_pairs={{0,16},{4,20},{8,24},{12,28},{16,0},{20,4},{24,8},{28,12},{1,17},{... | collective-permute-start | bytes 294920 | tf_op jit(solution)/shard_map/ppermute | solution.py:310
  29.7 6.6 %collective-permute-start.6 = (bf16[128,384]{1,0:T(8,128)(2,1)S(1)}, bf16[128,384]{1,0:T(8,128)(2,1)S(1)}, u32[]{:S(2)}, u32[]{:S(2)}) collective-permute-start(bf16[128,384]{1,0:T(8,128)(2,1)S(1)} %get-tuple-element.92), channel_id=1, source_target_pairs={{0,24},{4,28},{8,16},{12,20},{16,8},{20,12},{24,0},{28,4},{1,25},{... | collective-permute-start | bytes 294920 | tf_op jit(solution)/shard_map/ppermute | solution.py:310
  30.2 6.1 %copy-start = (s32[384]{0:T(512)S(1)}, s32[384]{0:T(512)}, u32[]{:S(2)}) copy-start(s32[384]{0:T(512)} %seed_ref.5) | copy-start | bytes 4612
  31.0 7.8 %collective-permute-start.8 = (bf16[2,128,384]{2,1,0:T(8,128)(2,1)S(1)}, bf16[2,128,384]{2,1,0:T(8,128)(2,1)S(1)}, u32[]{:S(2)}, u32[]{:S(2)}) collective-permute-start(bf16[2,128,384]{2,1,0:T(8,128)(2,1)S(1)} %get-tuple-element.98), channel_id=1, source_target_pairs={{0,8},{4,12},{8,0},{12,4},{16,24},{20,28},{24,16},{28,20},{1,9},{5... | collective-permute-start | bytes 589832 | tf_op jit(solution)/shard_map/ppermute | solution.py:310
  36.3 10.8 %collective-permute-start.12 = (bf16[128,384]{1,0:T(8,128)(2,1)S(1)}, bf16[128,384]{1,0:T(8,128)(2,1)S(1)}, u32[]{:S(2)}, u32[]{:S(2)}) collective-permute-start(bf16[128,384]{1,0:T(8,128)(2,1)S(1)} %get-tuple-element.119.refs_0_.second_ref), channel_id=1, source_target_pairs={{0,3},{1,2},{2,1},{3,0},{4,7},{5,6},{6,5},{7,4},{8,11},{9,10},{10,... | collective-permute-start | bytes 294920 | tf_op jit(solution)/shard_map/ppermute | solution.py:310
  38.9 9.8 %collective-permute-start.11 = (bf16[128,384]{1,0:T(8,128)(2,1)S(1)}, bf16[128,384]{1,0:T(8,128)(2,1)S(1)}, u32[]{:S(2)}, u32[]{:S(2)}) collective-permute-start(bf16[128,384]{1,0:T(8,128)(2,1)S(1)} %get-tuple-element.119.refs_0_.second_ref), channel_id=1, source_target_pairs={{0,2},{1,3},{2,0},{3,1},{4,6},{5,7},{6,4},{7,5},{8,10},{9,11},{10,... | collective-permute-start | bytes 294920 | tf_op jit(solution)/shard_map/ppermute | solution.py:310
  38.9 4.7 %collective-permute-start.9 = (bf16[1,128,384]{2,1,0:T(8,128)(2,1)S(1)}, bf16[1,128,384]{2,1,0:T(8,128)(2,1)S(1)}, u32[]{:S(2)}, u32[]{:S(2)}) collective-permute-start(bf16[1,128,384]{2,1,0:T(8,128)(2,1)S(1)} %get-tuple-element.108), channel_id=1, source_target_pairs={{0,16},{4,20},{8,24},{12,28},{16,0},{20,4},{24,8},{28,12},{1,17},{... | collective-permute-start | bytes 294920 | tf_op jit(solution)/shard_map/ppermute | solution.py:310
  39.8 8.9 %collective-permute-start.10 = (bf16[128,384]{1,0:T(8,128)(2,1)S(1)}, bf16[128,384]{1,0:T(8,128)(2,1)S(1)}, u32[]{:S(2)}, u32[]{:S(2)}) collective-permute-start(bf16[128,384]{1,0:T(8,128)(2,1)S(1)} %get-tuple-element.119.refs_0_.second_ref), channel_id=1, source_target_pairs={{0,1},{1,0},{2,3},{3,2},{4,5},{5,4},{6,7},{7,6},{8,9},{9,8},{10,11... | collective-permute-start | bytes 294920 | tf_op jit(solution)/shard_map/ppermute | solution.py:310
  43.7 9.0 %collective-permute-start.19 = (bf16[128,384]{1,0:T(8,128)(2,1)S(1)}, bf16[128,384]{1,0:T(8,128)(2,1)S(1)}, u32[]{:S(2)}, u32[]{:S(2)}) collective-permute-start(bf16[128,384]{1,0:T(8,128)(2,1)S(1)} %get-tuple-element.131.refs_0_.second_ref), channel_id=1, source_target_pairs={{0,3},{1,2},{2,1},{3,0},{4,7},{5,6},{6,5},{7,4},{8,11},{9,10},{10,... | collective-permute-start | bytes 294920 | tf_op jit(solution)/shard_map/ppermute | solution.py:310
  45.5 9.5 %collective-permute-start.18 = (bf16[128,384]{1,0:T(8,128)(2,1)S(1)}, bf16[128,384]{1,0:T(8,128)(2,1)S(1)}, u32[]{:S(2)}, u32[]{:S(2)}) collective-permute-start(bf16[128,384]{1,0:T(8,128)(2,1)S(1)} %get-tuple-element.131.refs_0_.second_ref), channel_id=1, source_target_pairs={{0,2},{1,3},{2,0},{3,1},{4,6},{5,7},{6,4},{7,5},{8,10},{9,11},{10,... | collective-permute-start | bytes 294920 | tf_op jit(solution)/shard_map/ppermute | solution.py:310
  47.1 7.8 %collective-permute-start.17 = (bf16[128,384]{1,0:T(8,128)(2,1)S(1)}, bf16[128,384]{1,0:T(8,128)(2,1)S(1)}, u32[]{:S(2)}, u32[]{:S(2)}) collective-permute-start(bf16[128,384]{1,0:T(8,128)(2,1)S(1)} %get-tuple-element.131.refs_0_.second_ref), channel_id=1, source_target_pairs={{0,1},{1,0},{2,3},{3,2},{4,5},{5,4},{6,7},{7,6},{8,9},{9,8},{10,11... | collective-permute-start | bytes 294920 | tf_op jit(solution)/shard_map/ppermute | solution.py:310
  49.5 1.8 %collective-permute-start.13 = (bf16[4,128,384]{2,1,0:T(8,128)(2,1)S(1)}, bf16[4,128,384]{2,1,0:T(8,128)(2,1)S(1)}, u32[]{:S(2)}, u32[]{:S(2)}) collective-permute-start(bf16[4,128,384]{2,1,0:T(8,128)(2,1)S(1)} %multiply_theirs.6), channel_id=1, source_target_pairs={{0,4},{4,0},{8,12},{12,8},{16,20},{20,16},{24,28},{28,24},{1,5},{5... | collective-permute-start | bytes 1179656 | tf_op jit(solution)/shard_map/ppermute | solution.py:310
  51.4 7.6 %collective-permute-start.14 = (bf16[128,384]{1,0:T(8,128)(2,1)S(1)}, bf16[128,384]{1,0:T(8,128)(2,1)S(1)}, u32[]{:S(2)}, u32[]{:S(2)}) collective-permute-start(bf16[128,384]{1,0:T(8,128)(2,1)S(1)} %get-tuple-element.124), channel_id=1, source_target_pairs={{0,8},{4,12},{8,0},{12,4},{16,24},{20,28},{24,16},{28,20},{1,9},{5... | collective-permute-start | bytes 294920 | tf_op jit(solution)/shard_map/ppermute | solution.py:310
  52.5 8.7 %collective-permute-start.15 = (bf16[128,384]{1,0:T(8,128)(2,1)S(1)}, bf16[128,384]{1,0:T(8,128)(2,1)S(1)}, u32[]{:S(2)}, u32[]{:S(2)}) collective-permute-start(bf16[128,384]{1,0:T(8,128)(2,1)S(1)} %get-tuple-element.125), channel_id=1, source_target_pairs={{0,16},{4,20},{8,24},{12,28},{16,0},{20,4},{24,8},{28,12},{1,17},{... | collective-permute-start | bytes 294920 | tf_op jit(solution)/shard_map/ppermute | solution.py:310
  52.7 8.4 %collective-permute-start.16 = (bf16[128,384]{1,0:T(8,128)(2,1)S(1)}, bf16[128,384]{1,0:T(8,128)(2,1)S(1)}, u32[]{:S(2)}, u32[]{:S(2)}) collective-permute-start(bf16[128,384]{1,0:T(8,128)(2,1)S(1)} %get-tuple-element.126), channel_id=1, source_target_pairs={{0,24},{4,28},{8,16},{12,20},{16,8},{20,12},{24,0},{28,4},{1,25},{... | collective-permute-start | bytes 294920 | tf_op jit(solution)/shard_map/ppermute | solution.py:310
  55.7 1.8 %collective-permute-start.20 = (bf16[4,128,384]{2,1,0:T(8,128)(2,1)S(1)}, bf16[4,128,384]{2,1,0:T(8,128)(2,1)S(1)}, u32[]{:S(2)}, u32[]{:S(2)}) collective-permute-start(bf16[4,128,384]{2,1,0:T(8,128)(2,1)S(1)} %multiply_theirs.7), channel_id=1, source_target_pairs={{0,4},{4,0},{8,12},{12,8},{16,20},{20,16},{24,28},{28,24},{1,5},{5... | collective-permute-start | bytes 1179656 | tf_op jit(solution)/shard_map/ppermute | solution.py:310
  57.6 5.0 %collective-permute-start.21 = (bf16[128,384]{1,0:T(8,128)(2,1)S(1)}, bf16[128,384]{1,0:T(8,128)(2,1)S(1)}, u32[]{:S(2)}, u32[]{:S(2)}) collective-permute-start(bf16[128,384]{1,0:T(8,128)(2,1)S(1)} %get-tuple-element.136), channel_id=1, source_target_pairs={{0,8},{4,12},{8,0},{12,4},{16,24},{20,28},{24,16},{28,20},{1,9},{5... | collective-permute-start | bytes 294920 | tf_op jit(solution)/shard_map/ppermute | solution.py:310
  58.7 6.7 %collective-permute-start.22 = (bf16[128,384]{1,0:T(8,128)(2,1)S(1)}, bf16[128,384]{1,0:T(8,128)(2,1)S(1)}, u32[]{:S(2)}, u32[]{:S(2)}) collective-permute-start(bf16[128,384]{1,0:T(8,128)(2,1)S(1)} %get-tuple-element.137), channel_id=1, source_target_pairs={{0,16},{4,20},{8,24},{12,28},{16,0},{20,4},{24,8},{28,12},{1,17},{... | collective-permute-start | bytes 294920 | tf_op jit(solution)/shard_map/ppermute | solution.py:310
  58.9 6.4 %collective-permute-start.23 = (bf16[128,384]{1,0:T(8,128)(2,1)S(1)}, bf16[128,384]{1,0:T(8,128)(2,1)S(1)}, u32[]{:S(2)}, u32[]{:S(2)}) collective-permute-start(bf16[128,384]{1,0:T(8,128)(2,1)S(1)} %get-tuple-element.138), channel_id=1, source_target_pairs={{0,24},{4,28},{8,16},{12,20},{16,8},{20,12},{24,0},{28,4},{1,25},{... | collective-permute-start | bytes 294920 | tf_op jit(solution)/shard_map/ppermute | solution.py:310

commit v4 on v3

--- a/solution.py
+++ b/solution.py
@@ -68,11 +68,16 @@
     return jnp.sum(jnp.where(position[:, :, None] == ids, codes[:, :, None], 0), axis=1)
 
 
+def chip_offset(position, chips):
+    return jnp.where(position == 0, 0, (position + chips - 3) % (chips - 1) + 1)
+
+
 def densify_kernel(odd, place_ref, codes_ref, tiles_ref, out_ref):
     slots, tile = tiles_ref.shape[3], tiles_ref.shape[4]
     depth, segment = out_ref.shape[0], out_ref.shape[1] // pl.num_programs(0)
     step = pl.program_id(0)
-    target = jnp.bitwise_xor(place_ref[0], 2 * step + odd)
+    chip = chip_offset(step, pl.num_programs(0))
+    target = jnp.bitwise_xor(place_ref[0], 2 * chip + odd)
     base = step * segment
     out_ref[:, pl.ds(pl.multiple_of(base, tile), segment)] = jnp.zeros(
         (depth, segment), out_ref.dtype
@@ -105,7 +110,9 @@
             in_specs=[
                 pl.BlockSpec(
                     (1, 1, 1, slots, tile, tile),
-                    lambda m, place, _: (0, 0, jnp.bitwise_xor(place[0], 2 * m + odd), 0, 0, 0),
+                    lambda m, place, _: (
+                        0, 0, jnp.bitwise_xor(place[0], 2 * chip_offset(m, half) + odd), 0, 0, 0
+                    ),
                 )
             ],
             out_specs=pl.BlockSpec(memory_space=pltpu.VMEM),
@@ -117,21 +124,12 @@
     )(place, codes, tile_values)
 
 
-def multiply_kernel(groups, first, rows, start, *refs):
+def multiply_kernel(offsets, first, rows, start, *refs):
     label_refs, matrix_ref, out_ref = refs[:-2], refs[-2], refs[-1]
-    half, _, segment = out_ref.shape
-    each = len(label_refs) // groups
-    labels = jnp.concatenate(
-        [
-            jnp.concatenate(
-                [ref[first : first + rows, :] for ref in label_refs[i * each : (i + 1) * each]],
-                axis=1,
-            )
-            for i in range(groups)
-        ],
-        axis=0,
-    )
-    for i in range(0, half, 2):
+    count, _, segment = out_ref.shape
+    label_refs = [label_refs[offsets.index(k)] for k in range(len(offsets))]
+    labels = jnp.concatenate([ref[first : first + rows, :] for ref in label_refs], axis=1)
+    for i in range(0, count, 2):
         part = jnp.dot(
             labels,
             matrix_ref[:, (start + i) * segment : (start + i + 2) * segment],
@@ -141,57 +139,53 @@
         out_ref[i + 1] = part[:, segment:].astype(out_ref.dtype)
 
 
-def multiply(groups, first, rows, matrix, dtype, name, start=0, count=None, weight=0):
-    segment = groups[0][0].shape[1]
+def multiply(sources, first, rows, matrix, dtype, name, start, count, weight):
+    offsets, labels = sources
+    segment = labels[0].shape[1]
     depth, width = matrix.shape
-    count = width // segment if count is None else count
-    total = len(groups) * rows
-    return pl.pallas_call(
-        functools.partial(multiply_kernel, len(groups), first, rows, start),
-        out_shape=jax.ShapeDtypeStruct((count, total, segment), dtype),
+    return pl.pallas_call(
+        functools.partial(multiply_kernel, tuple(offsets), first, rows, start),
+        out_shape=jax.ShapeDtypeStruct((count, rows, segment), dtype),
         name=name,
         compiler_params=params(),
         cost_estimate=pl.CostEstimate(
             flops=2 * weight * depth * width * rows, bytes_accessed=1, transcendentals=0
         ),
-    )(*[label for group in groups for label in group], matrix)
-
-
-def pair_kernel(mine_ref, *refs):
-    count = mine_ref.shape[0]
-    theirs_refs, out_refs = refs[:-count], refs[-count:]
-    theirs = [ref.at[i] for ref in theirs_refs for i in range(ref.shape[0])]
+    )(*labels, matrix)
+
+
+def pair_kernel(start, mine_ref, theirs_ref, *out_refs):
     for i, out_ref in enumerate(out_refs):
-        total = mine_ref[i] + theirs[i][...].astype(jnp.float32)
+        total = mine_ref[start + i] + theirs_ref[i].astype(jnp.float32)
         out_ref[...] = total.astype(out_ref.dtype)
 
 
-def pair(mine, theirs):
-    count, rows, segment = mine.shape
-    return pl.pallas_call(
-        pair_kernel,
-        out_shape=[jax.ShapeDtypeStruct((rows, segment), jnp.float32)]
-        + [jax.ShapeDtypeStruct((rows, segment), jnp.bfloat16)] * (count - 1),
+def pair(mine, theirs, start=0):
+    count, rows, segment = theirs.shape
+    types = [jnp.bfloat16 if start + i else jnp.float32 for i in range(count)]
+    return pl.pallas_call(
+        functools.partial(pair_kernel, start),
+        out_shape=[jax.ShapeDtypeStruct((rows, segment), dtype) for dtype in types],
         name="pair_sum",
         compiler_params=params(),
         cost_estimate=CHEAP,
-    )(mine, *theirs)
-
-
-def halve_kernel(kept_ref, arrived_ref, stay_ref, send_ref):
+    )(mine, theirs)
+
+
+def halve_kernel(order, kept_ref, arrived_ref, stay_ref, send_ref):
     for i in range(kept_ref.shape[0]):
-        total = kept_ref[i] + arrived_ref[i].astype(jnp.float32)
+        total = kept_ref[order[i]] + arrived_ref[order[i]].astype(jnp.float32)
         if i % 2:
             send_ref[i // 2] = total.astype(send_ref.dtype)
         else:
             stay_ref[i // 2] = total
 
 
-def halve(kept, arrived):
+def halve(kept, arrived, order):
     count, rows, segment = kept.shape
     shape = (count // 2, rows, segment)
     return pl.pallas_call(
-        halve_kernel,
+        functools.partial(halve_kernel, order),
         out_shape=[
             jax.ShapeDtypeStruct(shape, jnp.float32),
             jax.ShapeDtypeStruct(shape, jnp.bfloat16),
@@ -310,26 +304,24 @@
     return lax.ppermute(array, axis, [(i, i ^ bits) for i in range(size)])
 
 
-def gather(labels, n_col, late=(), waits=()):
+def gather(labels, n_col, order, late=(), waits=()):
     held = after(labels, waits) if late else labels
-    return [labels] + [
-        flip(held if k in late else labels, "col", n_col, k) for k in range(1, n_col)
+    offsets = [k % n_col for k in order if k < n_col] + list(range(len(order) + 1, n_col))
+    parts = [flip(held if k in late else labels, "col", n_col, k) for k in offsets]
+    return [0] + offsets, [labels] + parts
+
+
+def spread(parts, offsets, n_row):
+    return parts[:1] + [
+        flip(part, "row", n_row, 2 * j) for j, part in zip(offsets[1:], parts[1:])
     ]
-
-
-def spread(parts, n_row, late=(), waits=()):
-    own, *others = parts
-    sent = []
-    for j, part in enumerate(others, 1):
-        part = after(part, waits) if j in late else part
-        sent.append(flip(part, "row", n_row, 2 * j))
-    return [own] + sent
 
 
 def local(n_row, n_col, cotangent, seed_label, tile_values, tile_rows, tile_cols, tile_scale):
     segment, classes = cotangent.shape
     rows, depth = classes // 2, n_col * segment
     blocks, chips = segment // tile_values.shape[-1], n_row // 2
+    offsets = [0, chips - 1, *range(1, chips - 1)]
     col_place = lax.axis_index("col").astype(jnp.int32)
     place = jnp.stack([lax.axis_index("row").astype(jnp.int32), col_place])
     first_in = prepare(cotangent, seed_label)
@@ -337,46 +329,58 @@
     to_theirs = densify(place, codes, tile_values, 1, depth, segment)
     to_mine = densify(place, after(codes, to_theirs), tile_values, 0, depth, segment)
 
-    def for_theirs(labels, first, waits):
-        labels = after(labels, waits)
-        part = multiply([labels], first, rows, to_theirs, jnp.bfloat16, "multiply_theirs")
-        return part, flip(part, "row", n_row, 1)
+    def for_theirs(labels, first, waits, splits=1, weight=0):
+        parts, count = [], chips // splits
+        for start in range(0, chips, count):
+            labels = labels[0], after(labels[1], waits)
+            waits = multiply(
+                labels, first, rows, to_theirs, jnp.bfloat16, "multiply_theirs",
+                start, count, weight,
+            )
+            parts.append(flip(waits, "row", n_row, 1))
+        return waits, parts
 
     def for_mine(labels, first, waits, weight=0):
-        labels = after(labels, waits)
+        labels = labels[0], after(labels[1], waits)
         return multiply(
-            [labels], first, rows, to_mine, jnp.float32, "multiply_mine", weight=weight
+            labels, first, rows, to_mine, jnp.float32, "multiply_mine", 0, chips, weight
         )
 
-    arrived = gather(first_in, n_col)
-    theirs, swapped_a = for_theirs(arrived, 0, to_mine)
+    def add_pairs(mine, swapped):
+        parts = []
+        for part in swapped:
+            parts += pair(after(mine, parts), part, len(parts))
+        return parts
+
+    arrived = gather(first_in, n_col, (2, 1, 3))
+    theirs, swapped_a = for_theirs(arrived, 0, to_mine, 2)
     mine = for_mine(arrived, 0, theirs)
-    theirs, swapped_b = for_theirs(arrived, rows, mine)
-    parts_a = pair(after(mine, theirs), [swapped_a])
-    mine = for_mine(arrived, rows, parts_a, 20)
-    pieces_a = spread(parts_a, n_row)
-    done = halve(mine, swapped_b)
+    parts_a = add_pairs(mine, swapped_a)
+    theirs, swapped_b = for_theirs(arrived, rows, parts_a)
+    mine = for_mine(arrived, rows, theirs, 20)
+    pieces_a = spread(parts_a, offsets, n_row)
+    done = halve(mine, swapped_b[0], [offsets.index(j) for j in range(chips)])
     pieces_b = [done[0], flip(done[1], "row", n_row, 2)]
 
     grad_a, second_a = middle(seed_label, after(pieces_a, done), 0)
     done, step = [grad_a, second_a], 4
     while step < n_row:
-        done = halve(*after(pieces_b, done))
+        done = halve(*after(pieces_b, done), range(chips))
         pieces_b = [done[0], flip(done[1], "row", n_row, step)]
         step *= 2
-    sources_a = gather(second_a, n_col, (1,), done)
+    sources_a = gather(second_a, n_col, (3, 2, 1), (1,), done)
     turned_a = turn(after(grad_a, done))
     grad_b, second_b = middle(seed_label, after(pieces_b, turned_a), rows)
 
     theirs, swapped_a = for_theirs(sources_a, 0, [grad_b, second_b])
     mine = for_mine(sources_a, 0, theirs, 20)
-    sources_b = gather(second_b, n_col)
-    parts_a = pair(mine, [swapped_a])
-    theirs, swapped_b = for_theirs(sources_b, 0, parts_a)
+    sources_b = gather(second_b, n_col, (3, 2, 1))
+    parts_a = add_pairs(mine, swapped_a)
+    theirs, swapped_b = for_theirs(sources_b, 0, parts_a, 1)
     mine = for_mine(sources_b, 0, theirs, 20)
-    pieces_a = spread(parts_a, n_row)
-    parts_b = pair(mine, [swapped_b])
-    pieces_b = spread(parts_b, n_row)
+    pieces_a = spread(parts_a, offsets, n_row)
+    parts_b = add_pairs(mine, swapped_b)
+    pieces_b = spread(parts_b, offsets, n_row)
 
     label_a = label(first_in, second_a, after(pieces_a, parts_b), 0)
     first_grad = first_out([turned_a], after(grad_b, label_a))

time: 66.4 us -> 65.6 us (0.988)
  waiting for transfers between devices: 14.1 us -> 6.83 us
  starting transfers between devices: 28.2 us -> 34.3 us
    ppermute x24 -> x25, waiting for transfers between devices: 14.1 us -> 6.83 us  [flip(): return lax.ppermute(array, axis, [(i, i ^ bits) for i in range(size)])]
    ppermute x24 -> x25, starting transfers between devices: 28.2 us -> 34.3 us  [flip(): return lax.ppermute(array, axis, [(i, i ^ bits) for i in range(size)])]
    pallas_call x13 -> x15, Pallas kernels: 6.54 us -> 6.72 us  [the longest x9 6.4 us: multiply(): pl.pallas_call(functools.partial(multiply_kernel, tuple(offsets), first,...]
  transfers between devices with their start and end apart: 24 -> 25, of which waited for: 9 -> 8; matrix products, arithmetic and copies ran while one was open for 2% -> 2% of each run, Pallas kernels for 29% -> 30%
where the time goes in v4:
time: 65.6 us; the launch traced here: 65.3 us
  starting transfers between devices  34.3 us (52%)
  Pallas kernels  22 us (34%)
  waiting for transfers between devices  6.83 us (10%)
  other arithmetic  1.3 us (2%)
  between operations  0.9 us (1%)
    ppermute x25, starting transfers between devices, flip(): return lax.ppermute(array, axis, [(i, i ^ bits) for i in range(size)])  34.3 us
    pallas_call x2, Pallas kernels, densify(): pl.pallas_call(functools.partial(densify_kernel, odd), grid_spec=pltpu.Pr...  12.2 us
    ppermute x25, waiting for transfers between devices, flip(): return lax.ppermute(array, axis, [(i, i ^ bits) for i in range(size)])  6.83 us
    pallas_call x9, Pallas kernels, multiply(): pl.pallas_call(functools.partial(multiply_kernel, tuple(offsets), first,...  6.4 us
  transfers between devices with their start and end apart: 25, of which 8 were waited for; matrix products, arithmetic and copies ran while one was open for 2% of the time, Pallas kernels for 30%

profile of v4, /device:TPU:0, one launch (start us, length us, event | category | flops | bytes accessed | tf_op | source)
XLA Modules:
  0.0 65.3 jit_solution(7499952906863700710)
XLA Ops:
  0.6 1.1 %prepare.1.refs_0_.first_ref = bf16[256,384]{1,0:T(8,128)(2,1)S(1)} custom-call(bf16[384,256]{1,0:T(8,128)(2,1)} %cot_ref.1, s32[384]{0:T(512)} %seed_ref.5), custom_call_target="tpu_custom_call" | custom-call | flops 1 | bytes 1 | tf_op jit(solution)/shard_map/prepare/pallas_call | solution.py:47
  1.7 4.1 %collective-permute-start = (bf16[256,384]{1,0:T(8,128)(2,1)S(1)}, bf16[256,384]{1,0:T(8,128)(2,1)S(1)}, u32[]{:S(2)}, u32[]{:S(2)}) collective-permute-start(bf16[256,384]{1,0:T(8,128)(2,1)S(1)} %prepare.1.refs_0_.first_ref), channel_id=1, source_target_pairs={{0,2},{1,3},{2,0},{3,1},{4,6},{5,7},{6,4},{7,5},{8,10},{9,11},{10,... | collective-permute-start | bytes 589832 | tf_op jit(solution)/shard_map/ppermute | solution.py:304
  5.8 1.6 %collective-permute-start.1 = (bf16[256,384]{1,0:T(8,128)(2,1)S(1)}, bf16[256,384]{1,0:T(8,128)(2,1)S(1)}, u32[]{:S(2)}, u32[]{:S(2)}) collective-permute-start(bf16[256,384]{1,0:T(8,128)(2,1)S(1)} %prepare.1.refs_0_.first_ref), channel_id=1, source_target_pairs={{0,1},{1,0},{2,3},{3,2},{4,5},{5,4},{6,7},{7,6},{8,9},{9,8},{10,11... | collective-permute-start | bytes 589832 | tf_op jit(solution)/shard_map/ppermute | solution.py:304
  7.4 0.7 %fusion.7 = s32[8,48]{1,0:T(8,128)S(1)} fusion(s32[1,1,8,48]{3,2,1,0:T(8,128)} %param.11, s32[1,1,8,48]{3,2,1,0:T(8,128)} %param.10, s32[1,1,8,48]{3,2,1,0:T(8,128)} %param.9, s32[48]{0:T(128)S(1)} %iota_shift-left_fusion, s32[]{:T(128)} %axis_index.25), kind=kLoop, calls=%fused_computation.12 | loop fusion | flops 7680 | bytes 6340 | tf_op jit(solution)/shard_map/or | solution.py:66
  8.1 0.3 convert_reduce_fusion
  8.5 0.2 select_reduce_fusion.codes_ref
  8.7 6.1 %densify_theirs.1.refs_4_ = bf16[1536,1536]{1,0:T(8,128)(2,1)S(1)} custom-call(s32[2]{0:T(128)S(1)} %pad_add_fusion.place_ref, s32[8,48]{1,0:T(8,128)S(1)} %select_reduce_fusion.codes_ref, bf16[1,1,8,48,128,128]{5,4,3,2,1,0:T(8,128)(2,1)} %tiles_ref.3), custom_call_target="tpu_custom_call" | custom-call | flops 1 | bytes 1 | tf_op jit(solution)/shard_map/densify_theirs/pallas_call | solution.py:105
  14.8 6.1 %densify_mine.1.refs_4_ = bf16[1536,1536]{1,0:T(8,128)(2,1)S(1)} custom-call(s32[2]{0:T(128)S(1)} %pad_add_fusion.place_ref, s32[8,48]{1,0:T(8,128)S(1)} %select_reduce_fusion.codes_ref, bf16[1,1,8,48,128,128]{5,4,3,2,1,0:T(8,128)(2,1)} %tiles_ref.3), custom_call_target="tpu_custom_call" | custom-call | flops 1 | bytes 1 | tf_op jit(solution)/shard_map/densify_mine/pallas_call | solution.py:105
  20.9 0.5 multiply_theirs.5
  21.5 0.5 multiply_theirs.6
  22.0 0.6 collective-permute-start.5
  22.5 0.8 %multiply_mine.4.mine_ref = f32[4,128,384]{2,1,0:T(8,128)S(1)} custom-call(bf16[256,384]{1,0:T(8,128)(2,1)S(1)} %prepare.1.refs_0_.first_ref, bf16[256,384]{1,0:T(8,128)(2,1)S(1)} %collective-permute-done.refs_1_, bf16[256,384]{1,0:T(8,128)(2,1)S(1)} %collective-permute-done.1.refs_2_, bf16[256,384]{1,0:T(8,128)(2,1)S(1)} %collective-permute-done.2.refs_3_, ...), custom_call_target="tpu_custom_call" | custom-call | bytes 1 | tf_op jit(solution)/shard_map/multiply_mine/pallas_call | solution.py:146
  23.4 2.7 %collective-permute-start.4 = (bf16[128,384]{1,0:T(8,128)(2,1)S(1)}, bf16[128,384]{1,0:T(8,128)(2,1)S(1)}, u32[]{:S(2)}, u32[]{:S(2)}) collective-permute-start(bf16[128,384]{1,0:T(8,128)(2,1)S(1)} %get-tuple-element.93), channel_id=1, source_target_pairs={{0,24},{4,28},{8,16},{12,20},{16,8},{20,12},{24,0},{28,4},{1,25},{... | collective-permute-start | bytes 294920 | tf_op jit(solution)/shard_map/ppermute | solution.py:304
  26.2 0.6 collective-permute-start.6
  26.8 0.3 collective-permute-start.7
  27.1 0.8 %multiply_theirs.7 = bf16[4,128,384]{2,1,0:T(8,128)(2,1)S(1)} custom-call(bf16[256,384]{1,0:T(8,128)(2,1)S(1)} %prepare.1.refs_0_.first_ref, bf16[256,384]{1,0:T(8,128)(2,1)S(1)} %collective-permute-done.refs_1_, bf16[256,384]{1,0:T(8,128)(2,1)S(1)} %collective-permute-done.1.refs_2_, bf16[256,384]{1,0:T(8,128)(2,1)S(1)} %collective-permute-done.2.refs_3_, ...), custom_call_target="tpu_custom_call" | custom-call | bytes 1 | tf_op jit(solution)/shard_map/multiply_theirs/pallas_call | solution.py:146
  27.9 0.8 %multiply_mine.5.kept_ref = f32[4,128,384]{2,1,0:T(8,128)S(1)} custom-call(bf16[256,384]{1,0:T(8,128)(2,1)S(1)} %prepare.1.refs_0_.first_ref, bf16[256,384]{1,0:T(8,128)(2,1)S(1)} %collective-permute-done.refs_1_, bf16[256,384]{1,0:T(8,128)(2,1)S(1)} %collective-permute-done.1.refs_2_, bf16[256,384]{1,0:T(8,128)(2,1)S(1)} %collective-permute-done.2.refs_3_, ...), custom_call_target="tpu_custom_call" | custom-call | flops 12079595520 | bytes 1 | tf_op jit(solution)/shard_map/multiply_mine/pallas_call | solution.py:146
  28.7 0.9 %collective-permute-done.8.arrived_ref = bf16[4,128,384]{2,1,0:T(8,128)(2,1)S(1)} collective-permute-done((bf16[4,128,384]{2,1,0:T(8,128)(2,1)S(1)}, bf16[4,128,384]{2,1,0:T(8,128)(2,1)S(1)}, u32[]{:S(2)}, u32[]{:S(2)}) %collective-permute-start.8) | collective-permute-done | bytes 393248 | tf_op jit(solution)/shard_map/ppermute | solution.py:304
  29.7 1.8 %collective-permute-start.9 = (bf16[2,128,384]{2,1,0:T(8,128)(2,1)S(1)}, bf16[2,128,384]{2,1,0:T(8,128)(2,1)S(1)}, u32[]{:S(2)}, u32[]{:S(2)}) collective-permute-start(bf16[2,128,384]{2,1,0:T(8,128)(2,1)S(1)} %get-tuple-element.106), channel_id=1, source_target_pairs={{0,8},{4,12},{8,0},{12,4},{16,24},{20,28},{24,16},{28,20},{1,9},{5... | collective-permute-start | bytes 589832 | tf_op jit(solution)/shard_map/ppermute | solution.py:304
  31.5 0.1 first_grad.2
  31.6 3.7 %collective-permute-start.11 = (bf16[128,384]{1,0:T(8,128)(2,1)S(1)}, bf16[128,384]{1,0:T(8,128)(2,1)S(1)}, u32[]{:S(2)}, u32[]{:S(2)}) collective-permute-start(bf16[128,384]{1,0:T(8,128)(2,1)S(1)} %get-tuple-element.127.refs_0_.second_ref), channel_id=1, source_target_pairs={{0,3},{1,2},{2,1},{3,0},{4,7},{5,6},{6,5},{7,4},{8,11},{9,10},{10,... | collective-permute-start | bytes 294920 | tf_op jit(solution)/shard_map/ppermute | solution.py:304
  35.3 1.3 %collective-permute-start.12 = (bf16[128,384]{1,0:T(8,128)(2,1)S(1)}, bf16[128,384]{1,0:T(8,128)(2,1)S(1)}, u32[]{:S(2)}, u32[]{:S(2)}) collective-permute-start(bf16[128,384]{1,0:T(8,128)(2,1)S(1)} %get-tuple-element.127.refs_0_.second_ref), channel_id=1, source_target_pairs={{0,2},{1,3},{2,0},{3,1},{4,6},{5,7},{6,4},{7,5},{8,10},{9,11},{10,... | collective-permute-start | bytes 294920 | tf_op jit(solution)/shard_map/ppermute | solution.py:304
  36.6 0.1 collective-permute-done.9.arrived_ref
  36.8 1.8 %collective-permute-start.10 = (bf16[1,128,384]{2,1,0:T(8,128)(2,1)S(1)}, bf16[1,128,384]{2,1,0:T(8,128)(2,1)S(1)}, u32[]{:S(2)}, u32[]{:S(2)}) collective-permute-start(bf16[1,128,384]{2,1,0:T(8,128)(2,1)S(1)} %get-tuple-element.116), channel_id=1, source_target_pairs={{0,16},{4,20},{8,24},{12,28},{16,0},{20,4},{24,8},{28,12},{1,17},{... | collective-permute-start | bytes 294920 | tf_op jit(solution)/shard_map/ppermute | solution.py:304
  38.6 2.9 %collective-permute-start.13 = (bf16[128,384]{1,0:T(8,128)(2,1)S(1)}, bf16[128,384]{1,0:T(8,128)(2,1)S(1)}, u32[]{:S(2)}, u32[]{:S(2)}) collective-permute-start(bf16[128,384]{1,0:T(8,128)(2,1)S(1)} %get-tuple-element.127.refs_0_.second_ref), channel_id=1, source_target_pairs={{0,1},{1,0},{2,3},{3,2},{4,5},{5,4},{6,7},{7,6},{8,9},{9,8},{10,11... | collective-permute-start | bytes 294920 | tf_op jit(solution)/shard_map/ppermute | solution.py:304
  41.5 0.1 turn_grad.1.refs_0_
  41.7 3.7 %collective-permute-start.18 = (bf16[128,384]{1,0:T(8,128)(2,1)S(1)}, bf16[128,384]{1,0:T(8,128)(2,1)S(1)}, u32[]{:S(2)}, u32[]{:S(2)}) collective-permute-start(bf16[128,384]{1,0:T(8,128)(2,1)S(1)} %get-tuple-element.139.refs_0_.second_ref), channel_id=1, source_target_pairs={{0,3},{1,2},{2,1},{3,0},{4,7},{5,6},{6,5},{7,4},{8,11},{9,10},{10,... | collective-permute-start | bytes 294920 | tf_op jit(solution)/shard_map/ppermute | solution.py:304
  45.4 1.3 %collective-permute-start.19 = (bf16[128,384]{1,0:T(8,128)(2,1)S(1)}, bf16[128,384]{1,0:T(8,128)(2,1)S(1)}, u32[]{:S(2)}, u32[]{:S(2)}) collective-permute-start(bf16[128,384]{1,0:T(8,128)(2,1)S(1)} %get-tuple-element.139.refs_0_.second_ref), channel_id=1, source_target_pairs={{0,2},{1,3},{2,0},{3,1},{4,6},{5,7},{6,4},{7,5},{8,10},{9,11},{10,... | collective-permute-start | bytes 294920 | tf_op jit(solution)/shard_map/ppermute | solution.py:304
  46.7 0.5 collective-permute-start.20
  47.2 0.8 %multiply_theirs.8 = bf16[4,128,384]{2,1,0:T(8,128)(2,1)S(1)} custom-call(bf16[128,384]{1,0:T(8,128)(2,1)S(1)} %get-tuple-element.127.refs_0_.second_ref, bf16[128,384]{1,0:T(8,128)(2,1)S(1)} %collective-permute-done.11.refs_1_, bf16[128,384]{1,0:T(8,128)(2,1)S(1)} %collective-permute-done.12.refs_2_, bf16[128,384]{1,0:T(8,128)(2,1)S(1)} %collective-permute-done.13.refs_3_, ...), custom_call_target="tpu_custom_call" | custom-call | bytes 1 | tf_op jit(solution)/shard_map/multiply_theirs/pallas_call | solution.py:146
  48.1 0.8 %multiply_mine.6.mine_ref = f32[4,128,384]{2,1,0:T(8,128)S(1)} custom-call(bf16[128,384]{1,0:T(8,128)(2,1)S(1)} %get-tuple-element.127.refs_0_.second_ref, bf16[128,384]{1,0:T(8,128)(2,1)S(1)} %collective-permute-done.11.refs_1_, bf16[128,384]{1,0:T(8,128)(2,1)S(1)} %collective-permute-done.12.refs_2_, bf16[128,384]{1,0:T(8,128)(2,1)S(1)} %collective-permute-done.13.refs_3_, ...), custom_call_target="tpu_custom_call" | custom-call | flops 12079595520 | bytes 1 | tf_op jit(solution)/shard_map/multiply_mine/pallas_call | solution.py:146
  48.9 0.9 %collective-permute-done.14.theirs_ref = bf16[4,128,384]{2,1,0:T(8,128)(2,1)S(1)} collective-permute-done((bf16[4,128,384]{2,1,0:T(8,128)(2,1)S(1)}, bf16[4,128,384]{2,1,0:T(8,128)(2,1)S(1)}, u32[]{:S(2)}, u32[]{:S(2)}) %collective-permute-start.14) | collective-permute-done | bytes 393248 | tf_op jit(solution)/shard_map/ppermute | solution.py:304
  49.9 2.5 %collective-permute-start.15 = (bf16[128,384]{1,0:T(8,128)(2,1)S(1)}, bf16[128,384]{1,0:T(8,128)(2,1)S(1)}, u32[]{:S(2)}, u32[]{:S(2)}) collective-permute-start(bf16[128,384]{1,0:T(8,128)(2,1)S(1)} %get-tuple-element.132), channel_id=1, source_target_pairs={{0,24},{4,28},{8,16},{12,20},{16,8},{20,12},{24,0},{28,4},{1,25},{... | collective-permute-start | bytes 294920 | tf_op jit(solution)/shard_map/ppermute | solution.py:304
  52.4 0.5 collective-permute-start.16
  52.9 0.5 collective-permute-start.17
  53.4 0.5 collective-permute-done.19.refs_2_
  53.9 0.8 %multiply_theirs.9 = bf16[4,128,384]{2,1,0:T(8,128)(2,1)S(1)} custom-call(bf16[128,384]{1,0:T(8,128)(2,1)S(1)} %get-tuple-element.139.refs_0_.second_ref, bf16[128,384]{1,0:T(8,128)(2,1)S(1)} %collective-permute-done.18.refs_1_, bf16[128,384]{1,0:T(8,128)(2,1)S(1)} %collective-permute-done.19.refs_2_, bf16[128,384]{1,0:T(8,128)(2,1)S(1)} %collective-permute-done.20.refs_3_, ...), custom_call_target="tpu_custom_call" | custom-call | bytes 1 | tf_op jit(solution)/shard_map/multiply_theirs/pallas_call | solution.py:146
  54.8 0.8 %multiply_mine.7.mine_ref = f32[4,128,384]{2,1,0:T(8,128)S(1)} custom-call(bf16[128,384]{1,0:T(8,128)(2,1)S(1)} %get-tuple-element.139.refs_0_.second_ref, bf16[128,384]{1,0:T(8,128)(2,1)S(1)} %collective-permute-done.18.refs_1_, bf16[128,384]{1,0:T(8,128)(2,1)S(1)} %collective-permute-done.19.refs_2_, bf16[128,384]{1,0:T(8,128)(2,1)S(1)} %collective-permute-done.20.refs_3_, ...), custom_call_target="tpu_custom_call" | custom-call | flops 12079595520 | bytes 1 | tf_op jit(solution)/shard_map/multiply_mine/pallas_call | solution.py:146
  55.6 0.9 %collective-permute-done.21.theirs_ref = bf16[4,128,384]{2,1,0:T(8,128)(2,1)S(1)} collective-permute-done((bf16[4,128,384]{2,1,0:T(8,128)(2,1)S(1)}, bf16[4,128,384]{2,1,0:T(8,128)(2,1)S(1)}, u32[]{:S(2)}, u32[]{:S(2)}) %collective-permute-start.21) | collective-permute-done | bytes 393248 | tf_op jit(solution)/shard_map/ppermute | solution.py:304
  56.6 2.0 %collective-permute-start.22 = (bf16[128,384]{1,0:T(8,128)(2,1)S(1)}, bf16[128,384]{1,0:T(8,128)(2,1)S(1)}, u32[]{:S(2)}, u32[]{:S(2)}) collective-permute-start(bf16[128,384]{1,0:T(8,128)(2,1)S(1)} %get-tuple-element.144), channel_id=1, source_target_pairs={{0,24},{4,28},{8,16},{12,20},{16,8},{20,12},{24,0},{28,4},{1,25},{... | collective-permute-start | bytes 294920 | tf_op jit(solution)/shard_map/ppermute | solution.py:304
  58.6 0.5 collective-permute-start.23
  59.1 1.0 %collective-permute-start.24 = (bf16[128,384]{1,0:T(8,128)(2,1)S(1)}, bf16[128,384]{1,0:T(8,128)(2,1)S(1)}, u32[]{:S(2)}, u32[]{:S(2)}) collective-permute-start(bf16[128,384]{1,0:T(8,128)(2,1)S(1)} %get-tuple-element.146), channel_id=1, source_target_pairs={{0,16},{4,20},{8,24},{12,28},{16,0},{20,4},{24,8},{28,12},{1,17},{... | collective-permute-start | bytes 294920 | tf_op jit(solution)/shard_map/ppermute | solution.py:304
  60.2 0.2 label_grad.1.refs_0_
  60.3 0.8 %first_grad_out.1 = bf16[384,256]{1,0:T(8,128)(2,1)} custom-call(bf16[384,128]{1,0:T(8,128)(2,1)S(1)} %turn_grad.1.refs_0_, bf16[128,384]{1,0:T(8,128)(2,1)S(1)} %get-tuple-element.151.refs_1_), custom_call_target="tpu_custom_call" | custom-call | flops 1 | bytes 1 | tf_op jit(solution)/shard_map/first_grad_out/pallas_call | solution.py:253
  61.1 2.1 %collective-permute-done.22.refs_2_ = bf16[128,384]{1,0:T(8,128)(2,1)S(1)} collective-permute-done((bf16[128,384]{1,0:T(8,128)(2,1)S(1)}, bf16[128,384]{1,0:T(8,128)(2,1)S(1)}, u32[]{:S(2)}, u32[]{:S(2)}) %collective-permute-start.22) | collective-permute-done | bytes 98336 | tf_op jit(solution)/shard_map/ppermute | solution.py:304
  63.2 0.8 %collective-permute-done.23.refs_3_ = bf16[128,384]{1,0:T(8,128)(2,1)S(1)} collective-permute-done((bf16[128,384]{1,0:T(8,128)(2,1)S(1)}, bf16[128,384]{1,0:T(8,128)(2,1)S(1)}, u32[]{:S(2)}, u32[]{:S(2)}) %collective-permute-start.23) | collective-permute-done | bytes 98336 | tf_op jit(solution)/shard_map/ppermute | solution.py:304
  64.0 0.5 collective-permute-done.24.refs_4_
  64.5 0.8 %label_grad_out.1 = bf16[384,256]{1,0:T(8,128)(2,1)} custom-call(bf16[256,384]{1,0:T(8,128)(2,1)S(1)} %prepare.1.refs_0_.first_ref, bf16[128,384]{1,0:T(8,128)(2,1)S(1)} %get-tuple-element.139.refs_0_.second_ref, bf16[384,128]{1,0:T(8,128)(2,1)S(1)} %label_grad.1.refs_0_, f32[128,384]{1,0:T(8,128)S(1)} %get-tuple-element.152.refs_1_, ...), custom_call_target="tpu_custom_call" | custom-call | flops 1 | bytes 1 | tf_op jit(solution)/shard_map/label_grad_out/pallas_call | solution.py:294
  (33 shorter events, 0.8 us)
Async XLA Ops:
  1.7 19.2 %collective-permute-start = (bf16[256,384]{1,0:T(8,128)(2,1)S(1)}, bf16[256,384]{1,0:T(8,128)(2,1)S(1)}, u32[]{:S(2)}, u32[]{:S(2)}) collective-permute-start(bf16[256,384]{1,0:T(8,128)(2,1)S(1)} %prepare.1.refs_0_.first_ref), channel_id=1, source_target_pairs={{0,2},{1,3},{2,0},{3,1},{4,6},{5,7},{6,4},{7,5},{8,10},{9,11},{10,... | collective-permute-start | bytes 589832 | tf_op jit(solution)/shard_map/ppermute | solution.py:304
  5.8 15.1 %collective-permute-start.1 = (bf16[256,384]{1,0:T(8,128)(2,1)S(1)}, bf16[256,384]{1,0:T(8,128)(2,1)S(1)}, u32[]{:S(2)}, u32[]{:S(2)}) collective-permute-start(bf16[256,384]{1,0:T(8,128)(2,1)S(1)} %prepare.1.refs_0_.first_ref), channel_id=1, source_target_pairs={{0,1},{1,0},{2,3},{3,2},{4,5},{5,4},{6,7},{7,6},{8,9},{9,8},{10,11... | collective-permute-start | bytes 589832 | tf_op jit(solution)/shard_map/ppermute | solution.py:304
  7.4 13.5 %collective-permute-start.2 = (bf16[256,384]{1,0:T(8,128)(2,1)S(1)}, bf16[256,384]{1,0:T(8,128)(2,1)S(1)}, u32[]{:S(2)}, u32[]{:S(2)}) collective-permute-start(bf16[256,384]{1,0:T(8,128)(2,1)S(1)} %prepare.1.refs_0_.first_ref), channel_id=1, source_target_pairs={{0,3},{1,2},{2,1},{3,0},{4,7},{5,6},{6,5},{7,4},{8,11},{9,10},{10,... | collective-permute-start | bytes 589832 | tf_op jit(solution)/shard_map/ppermute | solution.py:304
  21.4 1.9 %collective-permute-start.3 = (bf16[2,128,384]{2,1,0:T(8,128)(2,1)S(1)}, bf16[2,128,384]{2,1,0:T(8,128)(2,1)S(1)}, u32[]{:S(2)}, u32[]{:S(2)}) collective-permute-start(bf16[2,128,384]{2,1,0:T(8,128)(2,1)S(1)} %multiply_theirs.5), channel_id=1, source_target_pairs={{0,4},{4,0},{8,12},{12,8},{16,20},{20,16},{24,28},{28,24},{1,5},{5... | collective-permute-start | bytes 589832 | tf_op jit(solution)/shard_map/ppermute | solution.py:304
  22.0 4.1 %collective-permute-start.5 = (bf16[2,128,384]{2,1,0:T(8,128)(2,1)S(1)}, bf16[2,128,384]{2,1,0:T(8,128)(2,1)S(1)}, u32[]{:S(2)}, u32[]{:S(2)}) collective-permute-start(bf16[2,128,384]{2,1,0:T(8,128)(2,1)S(1)} %multiply_theirs.6), channel_id=1, source_target_pairs={{0,4},{4,0},{8,12},{12,8},{16,20},{20,16},{24,28},{28,24},{1,5},{5... | collective-permute-start | bytes 589832 | tf_op jit(solution)/shard_map/ppermute | solution.py:304
  23.4 8.1 %collective-permute-start.4 = (bf16[128,384]{1,0:T(8,128)(2,1)S(1)}, bf16[128,384]{1,0:T(8,128)(2,1)S(1)}, u32[]{:S(2)}, u32[]{:S(2)}) collective-permute-start(bf16[128,384]{1,0:T(8,128)(2,1)S(1)} %get-tuple-element.93), channel_id=1, source_target_pairs={{0,24},{4,28},{8,16},{12,20},{16,8},{20,12},{24,0},{28,4},{1,25},{... | collective-permute-start | bytes 294920 | tf_op jit(solution)/shard_map/ppermute | solution.py:304
  26.2 5.3 %collective-permute-start.6 = (bf16[128,384]{1,0:T(8,128)(2,1)S(1)}, bf16[128,384]{1,0:T(8,128)(2,1)S(1)}, u32[]{:S(2)}, u32[]{:S(2)}) collective-permute-start(bf16[128,384]{1,0:T(8,128)(2,1)S(1)} %get-tuple-element.95), channel_id=1, source_target_pairs={{0,8},{4,12},{8,0},{12,4},{16,24},{20,28},{24,16},{28,20},{1,9},{5... | collective-permute-start | bytes 294920 | tf_op jit(solution)/shard_map/ppermute | solution.py:304
  26.8 4.7 %collective-permute-start.7 = (bf16[128,384]{1,0:T(8,128)(2,1)S(1)}, bf16[128,384]{1,0:T(8,128)(2,1)S(1)}, u32[]{:S(2)}, u32[]{:S(2)}) collective-permute-start(bf16[128,384]{1,0:T(8,128)(2,1)S(1)} %get-tuple-element.96), channel_id=1, source_target_pairs={{0,16},{4,20},{8,24},{12,28},{16,0},{20,4},{24,8},{28,12},{1,17},{... | collective-permute-start | bytes 294920 | tf_op jit(solution)/shard_map/ppermute | solution.py:304
  27.8 3.7 %copy-start = (s32[384]{0:T(512)S(1)}, s32[384]{0:T(512)}, u32[]{:S(2)}) copy-start(s32[384]{0:T(512)} %seed_ref.5) | copy-start | bytes 4612
  27.8 1.8 %collective-permute-start.8 = (bf16[4,128,384]{2,1,0:T(8,128)(2,1)S(1)}, bf16[4,128,384]{2,1,0:T(8,128)(2,1)S(1)}, u32[]{:S(2)}, u32[]{:S(2)}) collective-permute-start(bf16[4,128,384]{2,1,0:T(8,128)(2,1)S(1)} %multiply_theirs.7), channel_id=1, source_target_pairs={{0,4},{4,0},{8,12},{12,8},{16,20},{20,16},{24,28},{28,24},{1,5},{5... | collective-permute-start | bytes 1179656 | tf_op jit(solution)/shard_map/ppermute | solution.py:304
  29.7 7.0 %collective-permute-start.9 = (bf16[2,128,384]{2,1,0:T(8,128)(2,1)S(1)}, bf16[2,128,384]{2,1,0:T(8,128)(2,1)S(1)}, u32[]{:S(2)}, u32[]{:S(2)}) collective-permute-start(bf16[2,128,384]{2,1,0:T(8,128)(2,1)S(1)} %get-tuple-element.106), channel_id=1, source_target_pairs={{0,8},{4,12},{8,0},{12,4},{16,24},{20,28},{24,16},{28,20},{1,9},{5... | collective-permute-start | bytes 589832 | tf_op jit(solution)/shard_map/ppermute | solution.py:304
  31.6 15.1 %collective-permute-start.11 = (bf16[128,384]{1,0:T(8,128)(2,1)S(1)}, bf16[128,384]{1,0:T(8,128)(2,1)S(1)}, u32[]{:S(2)}, u32[]{:S(2)}) collective-permute-start(bf16[128,384]{1,0:T(8,128)(2,1)S(1)} %get-tuple-element.127.refs_0_.second_ref), channel_id=1, source_target_pairs={{0,3},{1,2},{2,1},{3,0},{4,7},{5,6},{6,5},{7,4},{8,11},{9,10},{10,... | collective-permute-start | bytes 294920 | tf_op jit(solution)/shard_map/ppermute | solution.py:304
  35.3 11.9 %collective-permute-start.12 = (bf16[128,384]{1,0:T(8,128)(2,1)S(1)}, bf16[128,384]{1,0:T(8,128)(2,1)S(1)}, u32[]{:S(2)}, u32[]{:S(2)}) collective-permute-start(bf16[128,384]{1,0:T(8,128)(2,1)S(1)} %get-tuple-element.127.refs_0_.second_ref), channel_id=1, source_target_pairs={{0,2},{1,3},{2,0},{3,1},{4,6},{5,7},{6,4},{7,5},{8,10},{9,11},{10,... | collective-permute-start | bytes 294920 | tf_op jit(solution)/shard_map/ppermute | solution.py:304
  36.8 4.8 %collective-permute-start.10 = (bf16[1,128,384]{2,1,0:T(8,128)(2,1)S(1)}, bf16[1,128,384]{2,1,0:T(8,128)(2,1)S(1)}, u32[]{:S(2)}, u32[]{:S(2)}) collective-permute-start(bf16[1,128,384]{2,1,0:T(8,128)(2,1)S(1)} %get-tuple-element.116), channel_id=1, source_target_pairs={{0,16},{4,20},{8,24},{12,28},{16,0},{20,4},{24,8},{28,12},{1,17},{... | collective-permute-start | bytes 294920 | tf_op jit(solution)/shard_map/ppermute | solution.py:304
  38.6 8.7 %collective-permute-start.13 = (bf16[128,384]{1,0:T(8,128)(2,1)S(1)}, bf16[128,384]{1,0:T(8,128)(2,1)S(1)}, u32[]{:S(2)}, u32[]{:S(2)}) collective-permute-start(bf16[128,384]{1,0:T(8,128)(2,1)S(1)} %get-tuple-element.127.refs_0_.second_ref), channel_id=1, source_target_pairs={{0,1},{1,0},{2,3},{3,2},{4,5},{5,4},{6,7},{7,6},{8,9},{9,8},{10,11... | collective-permute-start | bytes 294920 | tf_op jit(solution)/shard_map/ppermute | solution.py:304
  41.7 11.2 %collective-permute-start.18 = (bf16[128,384]{1,0:T(8,128)(2,1)S(1)}, bf16[128,384]{1,0:T(8,128)(2,1)S(1)}, u32[]{:S(2)}, u32[]{:S(2)}) collective-permute-start(bf16[128,384]{1,0:T(8,128)(2,1)S(1)} %get-tuple-element.139.refs_0_.second_ref), channel_id=1, source_target_pairs={{0,3},{1,2},{2,1},{3,0},{4,7},{5,6},{6,5},{7,4},{8,11},{9,10},{10,... | collective-permute-start | bytes 294920 | tf_op jit(solution)/shard_map/ppermute | solution.py:304
  45.4 8.6 %collective-permute-start.19 = (bf16[128,384]{1,0:T(8,128)(2,1)S(1)}, bf16[128,384]{1,0:T(8,128)(2,1)S(1)}, u32[]{:S(2)}, u32[]{:S(2)}) collective-permute-start(bf16[128,384]{1,0:T(8,128)(2,1)S(1)} %get-tuple-element.139.refs_0_.second_ref), channel_id=1, source_target_pairs={{0,2},{1,3},{2,0},{3,1},{4,6},{5,7},{6,4},{7,5},{8,10},{9,11},{10,... | collective-permute-start | bytes 294920 | tf_op jit(solution)/shard_map/ppermute | solution.py:304
  46.7 7.2 %collective-permute-start.20 = (bf16[128,384]{1,0:T(8,128)(2,1)S(1)}, bf16[128,384]{1,0:T(8,128)(2,1)S(1)}, u32[]{:S(2)}, u32[]{:S(2)}) collective-permute-start(bf16[128,384]{1,0:T(8,128)(2,1)S(1)} %get-tuple-element.139.refs_0_.second_ref), channel_id=1, source_target_pairs={{0,1},{1,0},{2,3},{3,2},{4,5},{5,4},{6,7},{7,6},{8,9},{9,8},{10,11... | collective-permute-start | bytes 294920 | tf_op jit(solution)/shard_map/ppermute | solution.py:304
  48.0 1.8 %collective-permute-start.14 = (bf16[4,128,384]{2,1,0:T(8,128)(2,1)S(1)}, bf16[4,128,384]{2,1,0:T(8,128)(2,1)S(1)}, u32[]{:S(2)}, u32[]{:S(2)}) collective-permute-start(bf16[4,128,384]{2,1,0:T(8,128)(2,1)S(1)} %multiply_theirs.8), channel_id=1, source_target_pairs={{0,4},{4,0},{8,12},{12,8},{16,20},{20,16},{24,28},{28,24},{1,5},{5... | collective-permute-start | bytes 1179656 | tf_op jit(solution)/shard_map/ppermute | solution.py:304
  49.9 9.3 %collective-permute-start.15 = (bf16[128,384]{1,0:T(8,128)(2,1)S(1)}, bf16[128,384]{1,0:T(8,128)(2,1)S(1)}, u32[]{:S(2)}, u32[]{:S(2)}) collective-permute-start(bf16[128,384]{1,0:T(8,128)(2,1)S(1)} %get-tuple-element.132), channel_id=1, source_target_pairs={{0,24},{4,28},{8,16},{12,20},{16,8},{20,12},{24,0},{28,4},{1,25},{... | collective-permute-start | bytes 294920 | tf_op jit(solution)/shard_map/ppermute | solution.py:304
  52.4 7.8 %collective-permute-start.16 = (bf16[128,384]{1,0:T(8,128)(2,1)S(1)}, bf16[128,384]{1,0:T(8,128)(2,1)S(1)}, u32[]{:S(2)}, u32[]{:S(2)}) collective-permute-start(bf16[128,384]{1,0:T(8,128)(2,1)S(1)} %get-tuple-element.133), channel_id=1, source_target_pairs={{0,8},{4,12},{8,0},{12,4},{16,24},{20,28},{24,16},{28,20},{1,9},{5... | collective-permute-start | bytes 294920 | tf_op jit(solution)/shard_map/ppermute | solution.py:304
  52.9 7.3 %collective-permute-start.17 = (bf16[128,384]{1,0:T(8,128)(2,1)S(1)}, bf16[128,384]{1,0:T(8,128)(2,1)S(1)}, u32[]{:S(2)}, u32[]{:S(2)}) collective-permute-start(bf16[128,384]{1,0:T(8,128)(2,1)S(1)} %get-tuple-element.134), channel_id=1, source_target_pairs={{0,16},{4,20},{8,24},{12,28},{16,0},{20,4},{24,8},{28,12},{1,17},{... | collective-permute-start | bytes 294920 | tf_op jit(solution)/shard_map/ppermute | solution.py:304
  54.7 1.8 %collective-permute-start.21 = (bf16[4,128,384]{2,1,0:T(8,128)(2,1)S(1)}, bf16[4,128,384]{2,1,0:T(8,128)(2,1)S(1)}, u32[]{:S(2)}, u32[]{:S(2)}) collective-permute-start(bf16[4,128,384]{2,1,0:T(8,128)(2,1)S(1)} %multiply_theirs.9), channel_id=1, source_target_pairs={{0,4},{4,0},{8,12},{12,8},{16,20},{20,16},{24,28},{28,24},{1,5},{5... | collective-permute-start | bytes 1179656 | tf_op jit(solution)/shard_map/ppermute | solution.py:304
  56.6 6.6 %collective-permute-start.22 = (bf16[128,384]{1,0:T(8,128)(2,1)S(1)}, bf16[128,384]{1,0:T(8,128)(2,1)S(1)}, u32[]{:S(2)}, u32[]{:S(2)}) collective-permute-start(bf16[128,384]{1,0:T(8,128)(2,1)S(1)} %get-tuple-element.144), channel_id=1, source_target_pairs={{0,24},{4,28},{8,16},{12,20},{16,8},{20,12},{24,0},{28,4},{1,25},{... | collective-permute-start | bytes 294920 | tf_op jit(solution)/shard_map/ppermute | solution.py:304
  58.6 5.4 %collective-permute-start.23 = (bf16[128,384]{1,0:T(8,128)(2,1)S(1)}, bf16[128,384]{1,0:T(8,128)(2,1)S(1)}, u32[]{:S(2)}, u32[]{:S(2)}) collective-permute-start(bf16[128,384]{1,0:T(8,128)(2,1)S(1)} %get-tuple-element.145), channel_id=1, source_target_pairs={{0,8},{4,12},{8,0},{12,4},{16,24},{20,28},{24,16},{28,20},{1,9},{5... | collective-permute-start | bytes 294920 | tf_op jit(solution)/shard_map/ppermute | solution.py:304
  59.1 5.4 %collective-permute-start.24 = (bf16[128,384]{1,0:T(8,128)(2,1)S(1)}, bf16[128,384]{1,0:T(8,128)(2,1)S(1)}, u32[]{:S(2)}, u32[]{:S(2)}) collective-permute-start(bf16[128,384]{1,0:T(8,128)(2,1)S(1)} %get-tuple-element.146), channel_id=1, source_target_pairs={{0,16},{4,20},{8,24},{12,28},{16,0},{20,4},{24,8},{28,12},{1,17},{... | collective-permute-start | bytes 294920 | tf_op jit(solution)/shard_map/ppermute | solution.py:304

commit v5 on v4

--- a/solution.py
+++ b/solution.py
@@ -8,12 +8,12 @@
 from jax.sharding import PartitionSpec as P
 
 ALPHA = 0.9
-VMEM_LIMIT = 40 * 1024 * 1024
+VMEM_LIMIT = 8 * 1024 * 1024
 CHEAP = pl.CostEstimate(flops=1, bytes_accessed=1, transcendentals=0)
 
 
-def params():
-    return pltpu.CompilerParams(vmem_limit_bytes=VMEM_LIMIT)
+def params(limit=VMEM_LIMIT):
+    return pltpu.CompilerParams(vmem_limit_bytes=limit)
 
 
 def after(arrays, *others):
@@ -25,7 +25,7 @@
     return ids != seed_row
 
 
-def prepare_kernel(cot_ref, seed_ref, out_ref, cot, seed, semaphores):
+def prepare_kernel(cot_ref, seed_ref, out_ref, part_ref, cot, seed, semaphores):
     copies = [
         pltpu.make_async_copy(cot_ref, cot, semaphores.at[0]),
         pltpu.make_async_copy(seed_ref, seed, semaphores.at[1]),
@@ -36,7 +36,9 @@
         copy.wait()
     part = cot[...].astype(jnp.float32).T
     keep = keep_of(seed[...][None, :], 0, part.shape[0])
-    out_ref[...] = jnp.where(keep, part, 0.0).astype(out_ref.dtype)
+    labels = jnp.where(keep, part, 0.0).astype(out_ref.dtype)
+    out_ref[...] = labels
+    part_ref[...] = labels[: part_ref.shape[0], :]
 
 
 def prepare(cotangent, seed_label):
@@ -47,15 +49,19 @@
     return pl.pallas_call(
         prepare_kernel,
         in_specs=[pl.BlockSpec(memory_space=pltpu.HBM)] * 2,
-        out_shape=jax.ShapeDtypeStruct((classes, segment), jnp.bfloat16),
+        out_shape=[
+            jax.ShapeDtypeStruct((count, segment), jnp.bfloat16)
+            for count in (classes, classes // 2)
+        ],
         scratch_shapes=[
             pltpu.VMEM(cotangent.shape, cotangent.dtype),
             pltpu.VMEM(seed_label.shape, seed_label.dtype),
             pltpu.SemaphoreType.DMA((2,)),
         ],
         name="prepare",
-        compiler_params=params(),
-        cost_estimate=CHEAP,
+        cost_estimate=pl.CostEstimate(flops=10**10, bytes_accessed=1, transcendentals=0),
+        compiler_params=params(),
+
     )(cotangent, seed_label)
 
 
@@ -72,82 +78,98 @@
     return jnp.where(position == 0, 0, (position + chips - 3) % (chips - 1) + 1)
 
 
-def densify_kernel(odd, place_ref, codes_ref, tiles_ref, out_ref):
-    slots, tile = tiles_ref.shape[3], tiles_ref.shape[4]
-    depth, segment = out_ref.shape[0], out_ref.shape[1] // pl.num_programs(0)
-    step = pl.program_id(0)
-    chip = chip_offset(step, pl.num_programs(0))
-    target = jnp.bitwise_xor(place_ref[0], 2 * chip + odd)
-    base = step * segment
-    out_ref[:, pl.ds(pl.multiple_of(base, tile), segment)] = jnp.zeros(
-        (depth, segment), out_ref.dtype
-    )
-
-    def add(position, carry):
-        total, before = carry
-        code = codes_ref[target, position]
-        block, slot, scale = code >> 16, (code >> 8) & 255, code & 255
-        term = tiles_ref[0, 0, 0, slot].astype(jnp.float32) * scale.astype(jnp.float32)
-        total = total * (block == before).astype(jnp.float32) + term
-        row, col = (block >> 4) * tile, base + (block & 15) * tile
-        out_ref[
-            pl.ds(pl.multiple_of(row, tile), tile), pl.ds(pl.multiple_of(col, tile), tile)
-        ] = total.astype(out_ref.dtype)
-        return total, block
-
-    start = (jnp.zeros((tile, tile), jnp.float32), jnp.int32(-1))
-    lax.fori_loop(0, slots, add, start, unroll=4)
-
-
-def densify(place, codes, tile_values, odd, depth, segment):
+def target_of(step, steps, row_place):
+    half = steps // 2
+    odd = jnp.where(step < half, 1, 0)
+    return jnp.bitwise_xor(row_place, 2 * chip_offset(step % half, half) + odd)
+
+
+def densify_kernel(place_ref, codes_ref, tiles_ref, out_ref, held_ref, semaphores):
+    targets, slots, tile, _ = held_ref.shape
+    segment = out_ref.shape[1] // targets
+
+    def copy_of(step):
+        target = target_of(step, targets, place_ref[0])
+        return pltpu.make_async_copy(
+            tiles_ref.at[0, 0, target], held_ref.at[step], semaphores.at[step]
+        )
+
+    for step in range(targets):
+        copy_of(step).start()
+    out_ref[...] = jnp.zeros_like(out_ref)
+
+    def build(step, carry):
+        target = target_of(step, targets, place_ref[0])
+        base = step * segment
+        copy_of(step).wait()
+
+        def add(position, carry):
+            total, before = carry
+            code = codes_ref[target, position]
+            block, slot, scale = code >> 16, (code >> 8) & 255, code & 255
+            term = held_ref[step, slot].astype(jnp.float32) * scale.astype(jnp.float32)
+            total = total * (block == before).astype(jnp.float32) + term
+            row, col = (block >> 4) * tile, base + (block & 15) * tile
+            out_ref[
+                pl.ds(pl.multiple_of(row, tile), tile), pl.ds(pl.multiple_of(col, tile), tile)
+            ] = total.astype(out_ref.dtype)
+            return total, block
+
+        start = (jnp.zeros((tile, tile), jnp.float32), jnp.int32(-1))
+        lax.fori_loop(0, slots, add, start, unroll=4)
+        return carry
+
+    lax.fori_loop(0, targets, build, 0)
+
+
+def densify(place, codes, tile_values, depth, segment):
     _, _, targets, slots, tile, _ = tile_values.shape
-    half = targets // 2
-    return pl.pallas_call(
-        functools.partial(densify_kernel, odd),
-        grid_spec=pltpu.PrefetchScalarGridSpec(
-            num_scalar_prefetch=2,
-            grid=(half,),
-            in_specs=[
-                pl.BlockSpec(
-                    (1, 1, 1, slots, tile, tile),
-                    lambda m, place, _: (
-                        0, 0, jnp.bitwise_xor(place[0], 2 * chip_offset(m, half) + odd), 0, 0, 0
-                    ),
-                )
-            ],
-            out_specs=pl.BlockSpec(memory_space=pltpu.VMEM),
-        ),
-        out_shape=jax.ShapeDtypeStruct((depth, half * segment), jnp.bfloat16),
-        name="densify_theirs" if odd else "densify_mine",
-        compiler_params=params(),
-        cost_estimate=CHEAP,
-    )(place, codes, tile_values)
-
-
-def multiply_kernel(offsets, first, rows, start, *refs):
-    label_refs, matrix_ref, out_ref = refs[:-2], refs[-2], refs[-1]
-    count, _, segment = out_ref.shape
-    label_refs = [label_refs[offsets.index(k)] for k in range(len(offsets))]
-    labels = jnp.concatenate([ref[first : first + rows, :] for ref in label_refs], axis=1)
-    for i in range(0, count, 2):
-        part = jnp.dot(
-            labels,
-            matrix_ref[:, (start + i) * segment : (start + i + 2) * segment],
-            preferred_element_type=jnp.float32,
-        )
-        out_ref[i] = part[:, :segment].astype(out_ref.dtype)
-        out_ref[i + 1] = part[:, segment:].astype(out_ref.dtype)
-
-
-def multiply(sources, first, rows, matrix, dtype, name, start, count, weight):
-    offsets, labels = sources
+    size = 2 * depth * targets * segment + 2 * tile_values.size
+    return pl.pallas_call(
+        densify_kernel,
+        in_specs=[pl.BlockSpec(memory_space=pltpu.SMEM)] * 2
+        + [pl.BlockSpec(memory_space=pltpu.HBM)],
+        out_specs=pl.BlockSpec(memory_space=pltpu.VMEM),
+        out_shape=jax.ShapeDtypeStruct((depth, targets * segment), jnp.bfloat16),
+        scratch_shapes=[
+            pltpu.VMEM((targets, slots, tile, tile), tile_values.dtype),
+            pltpu.SemaphoreType.DMA((targets,)),
+        ],
+        name="densify",
+        compiler_params=params(size + VMEM_LIMIT // 2),
+    )(place, codes, pltpu.with_memory_space_constraint(tile_values, pltpu.HBM))
+
+
+def multiply_kernel(offsets, firsts, rows, start, *refs):
+    count = len(offsets)
+    label_refs, matrix_ref, out_refs = refs[:count], refs[count], refs[count + 1 :]
+    parts = {
+        k: ref[first : first + rows, :] for k, first, ref in zip(offsets, firsts, label_refs)
+    }
+    labels = jnp.concatenate([parts[k] for k in range(count)], axis=1)
+    for out_ref in out_refs:
+        targets, _, segment = out_ref.shape
+        for i in range(0, targets, 2):
+            part = jnp.dot(
+                labels,
+                matrix_ref[:, (start + i) * segment : (start + i + 2) * segment],
+                preferred_element_type=jnp.float32,
+            )
+            out_ref[i] = part[:, :segment].astype(out_ref.dtype)
+            out_ref[i + 1] = part[:, segment:].astype(out_ref.dtype)
+        start += targets
+
+
+def multiply(sources, rows, matrix, dtype, name, start, count, weight, pieces=1):
+    offsets, firsts, labels = sources
     segment = labels[0].shape[1]
     depth, width = matrix.shape
-    return pl.pallas_call(
-        functools.partial(multiply_kernel, tuple(offsets), first, rows, start),
-        out_shape=jax.ShapeDtypeStruct((count, rows, segment), dtype),
+    shape = jax.ShapeDtypeStruct((count // pieces, rows, segment), dtype)
+    return pl.pallas_call(
+        functools.partial(multiply_kernel, tuple(offsets), tuple(firsts), rows, start),
+        out_shape=[shape] * pieces,
         name=name,
-        compiler_params=params(),
+        compiler_params=params(2 * depth * width + VMEM_LIMIT),
         cost_estimate=pl.CostEstimate(
             flops=2 * weight * depth * width * rows, bytes_accessed=1, transcendentals=0
         ),
@@ -304,11 +326,43 @@
     return lax.ppermute(array, axis, [(i, i ^ bits) for i in range(size)])
 
 
+def stack_kernel(own_ref, arrived_ref, out_ref):
+    rows = out_ref.shape[0] // 2
+    out_ref[:rows, :] = own_ref[rows:, :]
+    out_ref[rows:, :] = arrived_ref[rows:, :]
+
+
+def stack(own, arrived):
+    return pl.pallas_call(
+        stack_kernel,
+        out_shape=jax.ShapeDtypeStruct(own.shape, own.dtype),
+        name="stack_labels",
+        compiler_params=params(),
+        cost_estimate=CHEAP,
+    )(own, arrived)
+
+
 def gather(labels, n_col, order, late=(), waits=()):
     held = after(labels, waits) if late else labels
-    offsets = [k % n_col for k in order if k < n_col] + list(range(len(order) + 1, n_col))
+    offsets = [k for k in order if k < n_col] + list(range(len(order) + 1, n_col))
     parts = [flip(held if k in late else labels, "col", n_col, k) for k in offsets]
-    return [0] + offsets, [labels] + parts
+    return [0] + offsets, [0] * n_col, [labels] + parts
+
+
+def gather_both(labels, part, n_col, waits):
+    rows, half = part.shape[0], n_col // 2
+    across = flip(labels, "col", n_col, half)
+    others = [k for k in range(1, n_col) if k != half]
+    parts = [flip(part, "col", n_col, k) for k in others]
+    first = [0, half] + others, [0] * n_col, [labels, across] + parts
+    both, across = after((labels, across), waits)
+    both = stack(both, across)
+    sources = [0, half], [rows, rows], [labels, across]
+    for k in range(1, half):
+        arrived = flip(both, "col", n_col, k)
+        for values, more in zip(sources, ([k, k ^ half], [0, rows], [arrived, arrived])):
+            values.extend(more)
+    return first, sources, both
 
 
 def spread(parts, offsets, n_row):
@@ -324,27 +378,23 @@
     offsets = [0, chips - 1, *range(1, chips - 1)]
     col_place = lax.axis_index("col").astype(jnp.int32)
     place = jnp.stack([lax.axis_index("row").astype(jnp.int32), col_place])
-    first_in = prepare(cotangent, seed_label)
+    first_in, first_a = prepare(cotangent, seed_label)
     codes = slot_codes(col_place, blocks, tile_rows[0, 0], tile_cols[0, 0], tile_scale[0, 0])
-    to_theirs = densify(place, codes, tile_values, 1, depth, segment)
-    to_mine = densify(place, after(codes, to_theirs), tile_values, 0, depth, segment)
-
-    def for_theirs(labels, first, waits, splits=1, weight=0):
-        parts, count = [], chips // splits
-        for start in range(0, chips, count):
-            labels = labels[0], after(labels[1], waits)
-            waits = multiply(
-                labels, first, rows, to_theirs, jnp.bfloat16, "multiply_theirs",
-                start, count, weight,
-            )
-            parts.append(flip(waits, "row", n_row, 1))
-        return waits, parts
-
-    def for_mine(labels, first, waits, weight=0):
-        labels = labels[0], after(labels[1], waits)
+    matrix = densify(place, codes, tile_values, depth, segment)
+    sources_a, sources_b, both = gather_both(first_in, first_a, n_col, matrix)
+
+    def for_theirs(labels, waits, pieces=1):
+        labels = *labels[:2], after(labels[2], waits)
+        parts = multiply(
+            labels, rows, matrix, jnp.bfloat16, "multiply_theirs", 0, chips, 0, pieces
+        )
+        return parts, [flip(part, "row", n_row, 1) for part in parts]
+
+    def for_mine(labels, waits, weight=0):
+        labels = *labels[:2], after(labels[2], waits)
         return multiply(
-            labels, first, rows, to_mine, jnp.float32, "multiply_mine", 0, chips, weight
-        )
+            labels, rows, matrix, jnp.float32, "multiply_mine", chips, chips, weight
+        )[0]
 
     def add_pairs(mine, swapped):
         parts = []
@@ -352,12 +402,11 @@
             parts += pair(after(mine, parts), part, len(parts))
         return parts
 
-    arrived = gather(first_in, n_col, (2, 1, 3))
-    theirs, swapped_a = for_theirs(arrived, 0, to_mine, 2)
-    mine = for_mine(arrived, 0, theirs)
+    theirs, swapped_a = for_theirs(sources_a, both, 2)
+    mine = for_mine(sources_a, theirs, 20)
     parts_a = add_pairs(mine, swapped_a)
-    theirs, swapped_b = for_theirs(arrived, rows, parts_a)
-    mine = for_mine(arrived, rows, theirs, 20)
+    theirs, swapped_b = for_theirs(sources_b, parts_a)
+    mine = for_mine(sources_b, theirs, 20)
     pieces_a = spread(parts_a, offsets, n_row)
     done = halve(mine, swapped_b[0], [offsets.index(j) for j in range(chips)])
     pieces_b = [done[0], flip(done[1], "row", n_row, 2)]
@@ -372,12 +421,12 @@
     turned_a = turn(after(grad_a, done))
     grad_b, second_b = middle(seed_label, after(pieces_b, turned_a), rows)
 
-    theirs, swapped_a = for_theirs(sources_a, 0, [grad_b, second_b])
-    mine = for_mine(sources_a, 0, theirs, 20)
+    theirs, swapped_a = for_theirs(sources_a, [grad_b, second_b])
+    mine = for_mine(sources_a, theirs, 20)
     sources_b = gather(second_b, n_col, (3, 2, 1))
     parts_a = add_pairs(mine, swapped_a)
-    theirs, swapped_b = for_theirs(sources_b, 0, parts_a, 1)
-    mine = for_mine(sources_b, 0, theirs, 20)
+    theirs, swapped_b = for_theirs(sources_b, parts_a)
+    mine = for_mine(sources_b, theirs, 20)
     pieces_a = spread(parts_a, offsets, n_row)
     parts_b = add_pairs(mine, swapped_b)
     pieces_b = spread(parts_b, offsets, n_row)

time: 65.6 us -> 63.8 us (0.973)
  waiting for transfers between devices: 6.83 us -> 14.2 us
  starting transfers between devices: 34.3 us -> 29.8 us
  Pallas kernels: 22 us -> 18.1 us
  other arithmetic: 1.3 us -> 0.59 us
    ppermute x25 -> x26, waiting for transfers between devices: 6.83 us -> 14.2 us  [flip(): return lax.ppermute(array, axis, [(i, i ^ bits) for i in range(size)])]
    ppermute x25 -> x26, starting transfers between devices: 34.3 us -> 29.8 us  [flip(): return lax.ppermute(array, axis, [(i, i ^ bits) for i in range(size)])]
    pallas_call x11 -> x10, Pallas kernels: 18.6 us -> 14.6 us  [the longest x1 8.29 us: densify(): pl.pallas_call(densify_kernel, in_specs=[pl.BlockSpec(memory_space=pltpu....]
    or x1, other arithmetic: 0.74 us -> 0.03 us  [slot_codes(): codes = (place << 4 | tile_cols) << 16 | ids[None, :] << 8 | tile_scale]
  transfers between devices with their start and end apart: 25 -> 26, of which waited for: 8 -> 11; matrix products, arithmetic and copies ran while one was open for 2% -> 1% of each run, Pallas kernels for 30% -> 25%
where the time goes in v5:
time: 63.8 us; the launch traced here: 63.6 us
  starting transfers between devices  29.8 us (47%)
  Pallas kernels  18.1 us (28%)
  waiting for transfers between devices  14.2 us (22%)
  between operations  0.89 us (1%)
    ppermute x26, starting transfers between devices, flip(): return lax.ppermute(array, axis, [(i, i ^ bits) for i in range(size)])  29.8 us
    ppermute x26, waiting for transfers between devices, flip(): return lax.ppermute(array, axis, [(i, i ^ bits) for i in range(size)])  14.2 us
    pallas_call x1, Pallas kernels, densify(): pl.pallas_call(densify_kernel, in_specs=[pl.BlockSpec(memory_space=pltpu....  8.29 us
    pallas_call x8, Pallas kernels, multiply(): pl.pallas_call(functools.partial(multiply_kernel, tuple(offsets), tuple(f...  6.32 us
  transfers between devices with their start and end apart: 26, of which 11 were waited for; matrix products, arithmetic and copies ran while one was open for 1% of the time, Pallas kernels for 25%

profile of v5, /device:TPU:0, one launch (start us, length us, event | category | flops | bytes accessed | tf_op | source)
XLA Modules:
  0.0 63.6 jit_solution(9599424568326469575)
XLA Ops:
  0.7 1.1 %prepare.1 = (bf16[256,384]{1,0:T(8,128)(2,1)S(1)}, bf16[128,384]{1,0:T(8,128)(2,1)S(1)}) custom-call(bf16[384,256]{1,0:T(8,128)(2,1)} %cot_ref.1, s32[384]{0:T(512)} %seed_ref.5), custom_call_target="tpu_custom_call" | custom-call | flops 10000000000 | bytes 1 | tf_op jit(solution)/shard_map/prepare/pallas_call | solution.py:49
  1.8 3.1 %collective-permute-start.1 = (bf16[128,384]{1,0:T(8,128)(2,1)S(1)}, bf16[128,384]{1,0:T(8,128)(2,1)S(1)}, u32[]{:S(2)}, u32[]{:S(2)}) collective-permute-start(bf16[128,384]{1,0:T(8,128)(2,1)S(1)} %get-tuple-element.81), channel_id=1, source_target_pairs={{0,1},{1,0},{2,3},{3,2},{4,5},{5,4},{6,7},{7,6},{8,9},{9,8},{10,11... | collective-permute-start | bytes 294920 | tf_op jit(solution)/shard_map/ppermute | solution.py:326
  4.9 2.5 %collective-permute-start.2 = (bf16[128,384]{1,0:T(8,128)(2,1)S(1)}, bf16[128,384]{1,0:T(8,128)(2,1)S(1)}, u32[]{:S(2)}, u32[]{:S(2)}) collective-permute-start(bf16[128,384]{1,0:T(8,128)(2,1)S(1)} %get-tuple-element.81), channel_id=1, source_target_pairs={{0,3},{1,2},{2,1},{3,0},{4,7},{5,6},{6,5},{7,4},{8,11},{9,10},{10,... | collective-permute-start | bytes 294920 | tf_op jit(solution)/shard_map/ppermute | solution.py:326
  7.3 0.1 collective-permute-start
  7.5 0.3 convert_reduce_fusion
  7.8 0.2 select_reduce_fusion.codes_ref
  8.1 8.3 %densify.1.refs_4_ = bf16[1536,3072]{1,0:T(8,128)(2,1)S(1)} custom-call(s32[2]{0:T(128)S(1)} %pad_add_fusion.place_ref, s32[8,48]{1,0:T(8,128)S(1)} %select_reduce_fusion.codes_ref, bf16[1,1,8,48,128,128]{5,4,3,2,1,0:T(8,128)(2,1)} %tiles_ref.1), custom_call_target="tpu_custom_call" | custom-call | tf_op jit(solution)/shard_map/densify/pallas_call | solution.py:128
  16.4 4.1 %collective-permute-done.arrived_ref.refs_1_ = bf16[256,384]{1,0:T(8,128)(2,1)S(1)} collective-permute-done((bf16[256,384]{1,0:T(8,128)(2,1)S(1)}, bf16[256,384]{1,0:T(8,128)(2,1)S(1)}, u32[]{:S(2)}, u32[]{:S(2)}) %collective-permute-start) | collective-permute-done | bytes 196640 | tf_op jit(solution)/shard_map/ppermute | solution.py:326
  20.6 0.8 %multiply_theirs.4 = (bf16[2,128,384]{2,1,0:T(8,128)(2,1)S(1)}, bf16[2,128,384]{2,1,0:T(8,128)(2,1)S(1)}) custom-call(bf16[256,384]{1,0:T(8,128)(2,1)S(1)} %get-tuple-element.103.own_ref.refs_0_.first_ref, bf16[256,384]{1,0:T(8,128)(2,1)S(1)} %collective-permute-done.arrived_ref.refs_1_, bf16[128,384]{1,0:T(8,128)(2,1)S(1)} %collective-permute-done.1.refs_2_, ...), custom_call_target="tpu_custom_call" | custom-call | bytes 1 | tf_op jit(solution)/shard_map/multiply_theirs/pallas_call | solution.py:168
  21.5 0.5 collective-permute-start.5
  22.0 0.8 %multiply_mine.4.mine_ref = f32[4,128,384]{2,1,0:T(8,128)S(1)} custom-call(bf16[256,384]{1,0:T(8,128)(2,1)S(1)} %get-tuple-element.103.own_ref.refs_0_.first_ref, bf16[256,384]{1,0:T(8,128)(2,1)S(1)} %collective-permute-done.arrived_ref.refs_1_, bf16[128,384]{1,0:T(8,128)(2,1)S(1)} %collective-permute-done.1.refs_2_, ...), custom_call_target="tpu_custom_call" | custom-call | flops 24159191040 | bytes 1 | tf_op jit(solution)/shard_map/multiply_mine/pallas_call | solution.py:168
  22.8 0.1 collective-permute-done.3.theirs_ref
  23.0 2.5 %collective-permute-start.4 = (bf16[128,384]{1,0:T(8,128)(2,1)S(1)}, bf16[128,384]{1,0:T(8,128)(2,1)S(1)}, u32[]{:S(2)}, u32[]{:S(2)}) collective-permute-start(bf16[128,384]{1,0:T(8,128)(2,1)S(1)} %get-tuple-element.95), channel_id=1, source_target_pairs={{0,24},{4,28},{8,16},{12,20},{16,8},{20,12},{24,0},{28,4},{1,25},{... | collective-permute-start | bytes 294920 | tf_op jit(solution)/shard_map/ppermute | solution.py:326
  25.5 0.6 collective-permute-start.6
  26.1 0.5 collective-permute-start.7
  26.6 0.3 collective-permute-done.8.refs_2_.refs_3_
  27.0 0.8 %multiply_theirs.5 = bf16[4,128,384]{2,1,0:T(8,128)(2,1)S(1)} custom-call(bf16[256,384]{1,0:T(8,128)(2,1)S(1)} %get-tuple-element.103.own_ref.refs_0_.first_ref, bf16[256,384]{1,0:T(8,128)(2,1)S(1)} %collective-permute-done.arrived_ref.refs_1_, bf16[256,384]{1,0:T(8,128)(2,1)S(1)} %collective-permute-done.8.refs_2_.refs_3_, ...), custom_call_target="tpu_custom_call" | custom-call | bytes 1 | tf_op jit(solution)/shard_map/multiply_theirs/pallas_call | solution.py:168
  27.9 0.8 %multiply_mine.5.kept_ref = f32[4,128,384]{2,1,0:T(8,128)S(1)} custom-call(bf16[256,384]{1,0:T(8,128)(2,1)S(1)} %get-tuple-element.103.own_ref.refs_0_.first_ref, bf16[256,384]{1,0:T(8,128)(2,1)S(1)} %collective-permute-done.arrived_ref.refs_1_, bf16[256,384]{1,0:T(8,128)(2,1)S(1)} %collective-permute-done.8.refs_2_.refs_3_, ...), custom_call_target="tpu_custom_call" | custom-call | flops 24159191040 | bytes 1 | tf_op jit(solution)/shard_map/multiply_mine/pallas_call | solution.py:168
  28.7 0.9 %collective-permute-done.9.arrived_ref = bf16[4,128,384]{2,1,0:T(8,128)(2,1)S(1)} collective-permute-done((bf16[4,128,384]{2,1,0:T(8,128)(2,1)S(1)}, bf16[4,128,384]{2,1,0:T(8,128)(2,1)S(1)}, u32[]{:S(2)}, u32[]{:S(2)}) %collective-permute-start.9) | collective-permute-done | bytes 393248 | tf_op jit(solution)/shard_map/ppermute | solution.py:326
  29.6 1.6 %collective-permute-start.10 = (bf16[2,128,384]{2,1,0:T(8,128)(2,1)S(1)}, bf16[2,128,384]{2,1,0:T(8,128)(2,1)S(1)}, u32[]{:S(2)}, u32[]{:S(2)}) collective-permute-start(bf16[2,128,384]{2,1,0:T(8,128)(2,1)S(1)} %get-tuple-element.108), channel_id=1, source_target_pairs={{0,8},{4,12},{8,0},{12,4},{16,24},{20,28},{24,16},{28,20},{1,9},{5... | collective-permute-start | bytes 589832 | tf_op jit(solution)/shard_map/ppermute | solution.py:326
  31.2 0.1 first_grad.2
  31.3 2.5 %collective-permute-start.12 = (bf16[128,384]{1,0:T(8,128)(2,1)S(1)}, bf16[128,384]{1,0:T(8,128)(2,1)S(1)}, u32[]{:S(2)}, u32[]{:S(2)}) collective-permute-start(bf16[128,384]{1,0:T(8,128)(2,1)S(1)} %get-tuple-element.129.refs_0_.second_ref), channel_id=1, source_target_pairs={{0,3},{1,2},{2,1},{3,0},{4,7},{5,6},{6,5},{7,4},{8,11},{9,10},{10,... | collective-permute-start | bytes 294920 | tf_op jit(solution)/shard_map/ppermute | solution.py:326
  33.8 0.8 %collective-permute-start.13 = (bf16[128,384]{1,0:T(8,128)(2,1)S(1)}, bf16[128,384]{1,0:T(8,128)(2,1)S(1)}, u32[]{:S(2)}, u32[]{:S(2)}) collective-permute-start(bf16[128,384]{1,0:T(8,128)(2,1)S(1)} %get-tuple-element.129.refs_0_.second_ref), channel_id=1, source_target_pairs={{0,2},{1,3},{2,0},{3,1},{4,6},{5,7},{6,4},{7,5},{8,10},{9,11},{10,... | collective-permute-start | bytes 294920 | tf_op jit(solution)/shard_map/ppermute | solution.py:326
  34.6 2.0 %collective-permute-done.10.arrived_ref = bf16[2,128,384]{2,1,0:T(8,128)(2,1)S(1)} collective-permute-done((bf16[2,128,384]{2,1,0:T(8,128)(2,1)S(1)}, bf16[2,128,384]{2,1,0:T(8,128)(2,1)S(1)}, u32[]{:S(2)}, u32[]{:S(2)}) %collective-permute-start.10) | collective-permute-done | bytes 196640 | tf_op jit(solution)/shard_map/ppermute | solution.py:326
  36.7 1.6 %collective-permute-start.11 = (bf16[1,128,384]{2,1,0:T(8,128)(2,1)S(1)}, bf16[1,128,384]{2,1,0:T(8,128)(2,1)S(1)}, u32[]{:S(2)}, u32[]{:S(2)}) collective-permute-start(bf16[1,128,384]{2,1,0:T(8,128)(2,1)S(1)} %get-tuple-element.118), channel_id=1, source_target_pairs={{0,16},{4,20},{8,24},{12,28},{16,0},{20,4},{24,8},{28,12},{1,17},{... | collective-permute-start | bytes 294920 | tf_op jit(solution)/shard_map/ppermute | solution.py:326
  38.3 1.7 %collective-permute-start.14 = (bf16[128,384]{1,0:T(8,128)(2,1)S(1)}, bf16[128,384]{1,0:T(8,128)(2,1)S(1)}, u32[]{:S(2)}, u32[]{:S(2)}) collective-permute-start(bf16[128,384]{1,0:T(8,128)(2,1)S(1)} %get-tuple-element.129.refs_0_.second_ref), channel_id=1, source_target_pairs={{0,1},{1,0},{2,3},{3,2},{4,5},{5,4},{6,7},{7,6},{8,9},{9,8},{10,11... | collective-permute-start | bytes 294920 | tf_op jit(solution)/shard_map/ppermute | solution.py:326
  39.9 0.1 turn_grad.1.refs_0_
  40.0 1.3 %collective-permute-done.11.refs_1_ = bf16[1,128,384]{2,1,0:T(8,128)(2,1)S(1)} collective-permute-done((bf16[1,128,384]{2,1,0:T(8,128)(2,1)S(1)}, bf16[1,128,384]{2,1,0:T(8,128)(2,1)S(1)}, u32[]{:S(2)}, u32[]{:S(2)}) %collective-permute-start.11) | collective-permute-done | bytes 98336 | tf_op jit(solution)/shard_map/ppermute | solution.py:326
  41.4 2.4 %collective-permute-start.19 = (bf16[128,384]{1,0:T(8,128)(2,1)S(1)}, bf16[128,384]{1,0:T(8,128)(2,1)S(1)}, u32[]{:S(2)}, u32[]{:S(2)}) collective-permute-start(bf16[128,384]{1,0:T(8,128)(2,1)S(1)} %get-tuple-element.141.refs_0_.second_ref), channel_id=1, source_target_pairs={{0,3},{1,2},{2,1},{3,0},{4,7},{5,6},{6,5},{7,4},{8,11},{9,10},{10,... | collective-permute-start | bytes 294920 | tf_op jit(solution)/shard_map/ppermute | solution.py:326
  43.8 0.8 %collective-permute-start.20 = (bf16[128,384]{1,0:T(8,128)(2,1)S(1)}, bf16[128,384]{1,0:T(8,128)(2,1)S(1)}, u32[]{:S(2)}, u32[]{:S(2)}) collective-permute-start(bf16[128,384]{1,0:T(8,128)(2,1)S(1)} %get-tuple-element.141.refs_0_.second_ref), channel_id=1, source_target_pairs={{0,2},{1,3},{2,0},{3,1},{4,6},{5,7},{6,4},{7,5},{8,10},{9,11},{10,... | collective-permute-start | bytes 294920 | tf_op jit(solution)/shard_map/ppermute | solution.py:326
  44.6 1.3 %collective-permute-start.21 = (bf16[128,384]{1,0:T(8,128)(2,1)S(1)}, bf16[128,384]{1,0:T(8,128)(2,1)S(1)}, u32[]{:S(2)}, u32[]{:S(2)}) collective-permute-start(bf16[128,384]{1,0:T(8,128)(2,1)S(1)} %get-tuple-element.141.refs_0_.second_ref), channel_id=1, source_target_pairs={{0,1},{1,0},{2,3},{3,2},{4,5},{5,4},{6,7},{7,6},{8,9},{9,8},{10,11... | collective-permute-start | bytes 294920 | tf_op jit(solution)/shard_map/ppermute | solution.py:326
  45.9 0.8 %multiply_theirs.6 = bf16[4,128,384]{2,1,0:T(8,128)(2,1)S(1)} custom-call(bf16[128,384]{1,0:T(8,128)(2,1)S(1)} %get-tuple-element.129.refs_0_.second_ref, bf16[128,384]{1,0:T(8,128)(2,1)S(1)} %collective-permute-done.12.refs_1_, bf16[128,384]{1,0:T(8,128)(2,1)S(1)} %collective-permute-done.13.refs_2_, bf16[128,384]{1,0:T(8,128)(2,1)S(1)} %collective-permute-done.14.refs_3_, ...), custom_call_target="tpu_custom_call" | custom-call | bytes 1 | tf_op jit(solution)/shard_map/multiply_theirs/pallas_call | solution.py:168
  46.8 0.8 %multiply_mine.6.mine_ref = f32[4,128,384]{2,1,0:T(8,128)S(1)} custom-call(bf16[128,384]{1,0:T(8,128)(2,1)S(1)} %get-tuple-element.129.refs_0_.second_ref, bf16[128,384]{1,0:T(8,128)(2,1)S(1)} %collective-permute-done.12.refs_1_, bf16[128,384]{1,0:T(8,128)(2,1)S(1)} %collective-permute-done.13.refs_2_, bf16[128,384]{1,0:T(8,128)(2,1)S(1)} %collective-permute-done.14.refs_3_, ...), custom_call_target="tpu_custom_call" | custom-call | flops 24159191040 | bytes 1 | tf_op jit(solution)/shard_map/multiply_mine/pallas_call | solution.py:168
  47.6 0.9 %collective-permute-done.15.theirs_ref = bf16[4,128,384]{2,1,0:T(8,128)(2,1)S(1)} collective-permute-done((bf16[4,128,384]{2,1,0:T(8,128)(2,1)S(1)}, bf16[4,128,384]{2,1,0:T(8,128)(2,1)S(1)}, u32[]{:S(2)}, u32[]{:S(2)}) %collective-permute-start.15) | collective-permute-done | bytes 393248 | tf_op jit(solution)/shard_map/ppermute | solution.py:326
  48.6 2.5 %collective-permute-start.16 = (bf16[128,384]{1,0:T(8,128)(2,1)S(1)}, bf16[128,384]{1,0:T(8,128)(2,1)S(1)}, u32[]{:S(2)}, u32[]{:S(2)}) collective-permute-start(bf16[128,384]{1,0:T(8,128)(2,1)S(1)} %get-tuple-element.134), channel_id=1, source_target_pairs={{0,24},{4,28},{8,16},{12,20},{16,8},{20,12},{24,0},{28,4},{1,25},{... | collective-permute-start | bytes 294920 | tf_op jit(solution)/shard_map/ppermute | solution.py:326
  51.1 0.5 collective-permute-start.17
  51.6 0.5 collective-permute-start.18
  52.1 0.8 %multiply_theirs.7 = bf16[4,128,384]{2,1,0:T(8,128)(2,1)S(1)} custom-call(bf16[128,384]{1,0:T(8,128)(2,1)S(1)} %get-tuple-element.141.refs_0_.second_ref, bf16[128,384]{1,0:T(8,128)(2,1)S(1)} %collective-permute-done.19.refs_1_, bf16[128,384]{1,0:T(8,128)(2,1)S(1)} %collective-permute-done.20.refs_2_, bf16[128,384]{1,0:T(8,128)(2,1)S(1)} %collective-permute-done.21.refs_3_, ...), custom_call_target="tpu_custom_call" | custom-call | bytes 1 | tf_op jit(solution)/shard_map/multiply_theirs/pallas_call | solution.py:168
  53.0 0.8 %multiply_mine.7.mine_ref = f32[4,128,384]{2,1,0:T(8,128)S(1)} custom-call(bf16[128,384]{1,0:T(8,128)(2,1)S(1)} %get-tuple-element.141.refs_0_.second_ref, bf16[128,384]{1,0:T(8,128)(2,1)S(1)} %collective-permute-done.19.refs_1_, bf16[128,384]{1,0:T(8,128)(2,1)S(1)} %collective-permute-done.20.refs_2_, bf16[128,384]{1,0:T(8,128)(2,1)S(1)} %collective-permute-done.21.refs_3_, ...), custom_call_target="tpu_custom_call" | custom-call | flops 24159191040 | bytes 1 | tf_op jit(solution)/shard_map/multiply_mine/pallas_call | solution.py:168
  53.8 0.9 %collective-permute-done.22.theirs_ref = bf16[4,128,384]{2,1,0:T(8,128)(2,1)S(1)} collective-permute-done((bf16[4,128,384]{2,1,0:T(8,128)(2,1)S(1)}, bf16[4,128,384]{2,1,0:T(8,128)(2,1)S(1)}, u32[]{:S(2)}, u32[]{:S(2)}) %collective-permute-start.22) | collective-permute-done | bytes 393248 | tf_op jit(solution)/shard_map/ppermute | solution.py:326
  54.8 2.5 %collective-permute-start.23 = (bf16[128,384]{1,0:T(8,128)(2,1)S(1)}, bf16[128,384]{1,0:T(8,128)(2,1)S(1)}, u32[]{:S(2)}, u32[]{:S(2)}) collective-permute-start(bf16[128,384]{1,0:T(8,128)(2,1)S(1)} %get-tuple-element.146), channel_id=1, source_target_pairs={{0,24},{4,28},{8,16},{12,20},{16,8},{20,12},{24,0},{28,4},{1,25},{... | collective-permute-start | bytes 294920 | tf_op jit(solution)/shard_map/ppermute | solution.py:326
  57.3 0.5 collective-permute-start.24
  57.8 0.5 collective-permute-start.25
  58.4 0.2 label_grad.1.refs_0_
  58.5 0.8 %first_grad_out.1 = bf16[384,256]{1,0:T(8,128)(2,1)} custom-call(bf16[384,128]{1,0:T(8,128)(2,1)S(1)} %turn_grad.1.refs_0_, bf16[128,384]{1,0:T(8,128)(2,1)S(1)} %get-tuple-element.153.refs_1_), custom_call_target="tpu_custom_call" | custom-call | flops 1 | bytes 1 | tf_op jit(solution)/shard_map/first_grad_out/pallas_call | solution.py:275
  59.3 2.1 %collective-permute-done.23.refs_2_ = bf16[128,384]{1,0:T(8,128)(2,1)S(1)} collective-permute-done((bf16[128,384]{1,0:T(8,128)(2,1)S(1)}, bf16[128,384]{1,0:T(8,128)(2,1)S(1)}, u32[]{:S(2)}, u32[]{:S(2)}) %collective-permute-start.23) | collective-permute-done | bytes 98336 | tf_op jit(solution)/shard_map/ppermute | solution.py:326
  61.4 1.4 %collective-permute-done.24.refs_3_ = bf16[128,384]{1,0:T(8,128)(2,1)S(1)} collective-permute-done((bf16[128,384]{1,0:T(8,128)(2,1)S(1)}, bf16[128,384]{1,0:T(8,128)(2,1)S(1)}, u32[]{:S(2)}, u32[]{:S(2)}) %collective-permute-start.24) | collective-permute-done | bytes 98336 | tf_op jit(solution)/shard_map/ppermute | solution.py:326
  62.8 0.8 %label_grad_out.1 = bf16[384,256]{1,0:T(8,128)(2,1)} custom-call(bf16[256,384]{1,0:T(8,128)(2,1)S(1)} %get-tuple-element.103.own_ref.refs_0_.first_ref, bf16[128,384]{1,0:T(8,128)(2,1)S(1)} %get-tuple-element.141.refs_0_.second_ref, bf16[384,128]{1,0:T(8,128)(2,1)S(1)} %label_grad.1.refs_0_, f32[128,384]{1,0:T(8,128)S(1)} %get-tuple-element.154.refs_1_, ...), custom_call_target="tpu_custom_call" | custom-call | flops 1 | bytes 1 | tf_op jit(solution)/shard_map/label_grad_out/pallas_call | solution.py:316
  (40 shorter events, 1.0 us)
Async XLA Ops:
  0.6 6.8 %copy-start.2 = (s32[1,1,8,48]{3,2,1,0:T(8,128)S(1)}, s32[1,1,8,48]{3,2,1,0:T(8,128)}, u32[]{:S(2)}) copy-start(s32[1,1,8,48]{3,2,1,0:T(8,128)} %param.10) | copy-start | bytes 4612
  0.6 6.8 %copy-start.1 = (s32[1,1,8,48]{3,2,1,0:T(8,128)S(1)}, s32[1,1,8,48]{3,2,1,0:T(8,128)}, u32[]{:S(2)}) copy-start(s32[1,1,8,48]{3,2,1,0:T(8,128)} %param.11) | copy-start | bytes 4612
  0.7 6.8 %copy-start.3 = (s32[1,1,8,48]{3,2,1,0:T(8,128)S(1)}, s32[1,1,8,48]{3,2,1,0:T(8,128)}, u32[]{:S(2)}) copy-start(s32[1,1,8,48]{3,2,1,0:T(8,128)} %param.9) | copy-start | bytes 4612
  1.8 18.8 %collective-permute-start.1 = (bf16[128,384]{1,0:T(8,128)(2,1)S(1)}, bf16[128,384]{1,0:T(8,128)(2,1)S(1)}, u32[]{:S(2)}, u32[]{:S(2)}) collective-permute-start(bf16[128,384]{1,0:T(8,128)(2,1)S(1)} %get-tuple-element.81), channel_id=1, source_target_pairs={{0,1},{1,0},{2,3},{3,2},{4,5},{5,4},{6,7},{7,6},{8,9},{9,8},{10,11... | collective-permute-start | bytes 294920 | tf_op jit(solution)/shard_map/ppermute | solution.py:326
  4.9 15.7 %collective-permute-start.2 = (bf16[128,384]{1,0:T(8,128)(2,1)S(1)}, bf16[128,384]{1,0:T(8,128)(2,1)S(1)}, u32[]{:S(2)}, u32[]{:S(2)}) collective-permute-start(bf16[128,384]{1,0:T(8,128)(2,1)S(1)} %get-tuple-element.81), channel_id=1, source_target_pairs={{0,3},{1,2},{2,1},{3,0},{4,7},{5,6},{6,5},{7,4},{8,11},{9,10},{10,... | collective-permute-start | bytes 294920 | tf_op jit(solution)/shard_map/ppermute | solution.py:326
  7.3 13.2 %collective-permute-start = (bf16[256,384]{1,0:T(8,128)(2,1)S(1)}, bf16[256,384]{1,0:T(8,128)(2,1)S(1)}, u32[]{:S(2)}, u32[]{:S(2)}) collective-permute-start(bf16[256,384]{1,0:T(8,128)(2,1)S(1)} %get-tuple-element.103.own_ref.refs_0_.first_ref), channel_id=1, source_target_pairs={{0,2},{1,3},{2,0},{3,1},{4,6},{5,7},{6,4},{7,5},{8,10},{9,11},{10,... | collective-permute-start | bytes 589832 | tf_op jit(solution)/shard_map/ppermute | solution.py:326
  20.5 6.5 %collective-permute-start.8 = (bf16[256,384]{1,0:T(8,128)(2,1)S(1)}, bf16[256,384]{1,0:T(8,128)(2,1)S(1)}, u32[]{:S(2)}, u32[]{:S(2)}) collective-permute-start(bf16[256,384]{1,0:T(8,128)(2,1)S(1)} %stack_labels.1), channel_id=1, source_target_pairs={{0,1},{1,0},{2,3},{3,2},{4,5},{5,4},{6,7},{7,6},{8,9},{9,8},{10,11... | collective-permute-start | bytes 589832 | tf_op jit(solution)/shard_map/ppermute | solution.py:326
  21.4 1.5 %collective-permute-start.3 = (bf16[2,128,384]{2,1,0:T(8,128)(2,1)S(1)}, bf16[2,128,384]{2,1,0:T(8,128)(2,1)S(1)}, u32[]{:S(2)}, u32[]{:S(2)}) collective-permute-start(bf16[2,128,384]{2,1,0:T(8,128)(2,1)S(1)} %get-tuple-element.88), channel_id=1, source_target_pairs={{0,4},{4,0},{8,12},{12,8},{16,20},{20,16},{24,28},{28,24},{1,5},{5... | collective-permute-start | bytes 589832 | tf_op jit(solution)/shard_map/ppermute | solution.py:326
  21.5 4.0 %collective-permute-start.5 = (bf16[2,128,384]{2,1,0:T(8,128)(2,1)S(1)}, bf16[2,128,384]{2,1,0:T(8,128)(2,1)S(1)}, u32[]{:S(2)}, u32[]{:S(2)}) collective-permute-start(bf16[2,128,384]{2,1,0:T(8,128)(2,1)S(1)} %get-tuple-element.89), channel_id=1, source_target_pairs={{0,4},{4,0},{8,12},{12,8},{16,20},{20,16},{24,28},{28,24},{1,5},{5... | collective-permute-start | bytes 589832 | tf_op jit(solution)/shard_map/ppermute | solution.py:326
  23.0 8.2 %collective-permute-start.4 = (bf16[128,384]{1,0:T(8,128)(2,1)S(1)}, bf16[128,384]{1,0:T(8,128)(2,1)S(1)}, u32[]{:S(2)}, u32[]{:S(2)}) collective-permute-start(bf16[128,384]{1,0:T(8,128)(2,1)S(1)} %get-tuple-element.95), channel_id=1, source_target_pairs={{0,24},{4,28},{8,16},{12,20},{16,8},{20,12},{24,0},{28,4},{1,25},{... | collective-permute-start | bytes 294920 | tf_op jit(solution)/shard_map/ppermute | solution.py:326
  25.5 5.7 %collective-permute-start.6 = (bf16[128,384]{1,0:T(8,128)(2,1)S(1)}, bf16[128,384]{1,0:T(8,128)(2,1)S(1)}, u32[]{:S(2)}, u32[]{:S(2)}) collective-permute-start(bf16[128,384]{1,0:T(8,128)(2,1)S(1)} %get-tuple-element.97), channel_id=1, source_target_pairs={{0,8},{4,12},{8,0},{12,4},{16,24},{20,28},{24,16},{28,20},{1,9},{5... | collective-permute-start | bytes 294920 | tf_op jit(solution)/shard_map/ppermute | solution.py:326
  26.1 5.1 %collective-permute-start.7 = (bf16[128,384]{1,0:T(8,128)(2,1)S(1)}, bf16[128,384]{1,0:T(8,128)(2,1)S(1)}, u32[]{:S(2)}, u32[]{:S(2)}) collective-permute-start(bf16[128,384]{1,0:T(8,128)(2,1)S(1)} %get-tuple-element.98), channel_id=1, source_target_pairs={{0,16},{4,20},{8,24},{12,28},{16,0},{20,4},{24,8},{28,12},{1,17},{... | collective-permute-start | bytes 294920 | tf_op jit(solution)/shard_map/ppermute | solution.py:326
  27.8 3.4 %copy-start = (s32[384]{0:T(512)S(1)}, s32[384]{0:T(512)}, u32[]{:S(2)}) copy-start(s32[384]{0:T(512)} %seed_ref.5) | copy-start | bytes 4612
  27.8 1.8 %collective-permute-start.9 = (bf16[4,128,384]{2,1,0:T(8,128)(2,1)S(1)}, bf16[4,128,384]{2,1,0:T(8,128)(2,1)S(1)}, u32[]{:S(2)}, u32[]{:S(2)}) collective-permute-start(bf16[4,128,384]{2,1,0:T(8,128)(2,1)S(1)} %multiply_theirs.5), channel_id=1, source_target_pairs={{0,4},{4,0},{8,12},{12,8},{16,20},{20,16},{24,28},{28,24},{1,5},{5... | collective-permute-start | bytes 1179656 | tf_op jit(solution)/shard_map/ppermute | solution.py:326
  29.6 7.0 %collective-permute-start.10 = (bf16[2,128,384]{2,1,0:T(8,128)(2,1)S(1)}, bf16[2,128,384]{2,1,0:T(8,128)(2,1)S(1)}, u32[]{:S(2)}, u32[]{:S(2)}) collective-permute-start(bf16[2,128,384]{2,1,0:T(8,128)(2,1)S(1)} %get-tuple-element.108), channel_id=1, source_target_pairs={{0,8},{4,12},{8,0},{12,4},{16,24},{20,28},{24,16},{28,20},{1,9},{5... | collective-permute-start | bytes 589832 | tf_op jit(solution)/shard_map/ppermute | solution.py:326
  31.3 13.3 %collective-permute-start.12 = (bf16[128,384]{1,0:T(8,128)(2,1)S(1)}, bf16[128,384]{1,0:T(8,128)(2,1)S(1)}, u32[]{:S(2)}, u32[]{:S(2)}) collective-permute-start(bf16[128,384]{1,0:T(8,128)(2,1)S(1)} %get-tuple-element.129.refs_0_.second_ref), channel_id=1, source_target_pairs={{0,3},{1,2},{2,1},{3,0},{4,7},{5,6},{6,5},{7,4},{8,11},{9,10},{10,... | collective-permute-start | bytes 294920 | tf_op jit(solution)/shard_map/ppermute | solution.py:326
  33.8 12.1 %collective-permute-start.13 = (bf16[128,384]{1,0:T(8,128)(2,1)S(1)}, bf16[128,384]{1,0:T(8,128)(2,1)S(1)}, u32[]{:S(2)}, u32[]{:S(2)}) collective-permute-start(bf16[128,384]{1,0:T(8,128)(2,1)S(1)} %get-tuple-element.129.refs_0_.second_ref), channel_id=1, source_target_pairs={{0,2},{1,3},{2,0},{3,1},{4,6},{5,7},{6,4},{7,5},{8,10},{9,11},{10,... | collective-permute-start | bytes 294920 | tf_op jit(solution)/shard_map/ppermute | solution.py:326
  36.7 4.7 %collective-permute-start.11 = (bf16[1,128,384]{2,1,0:T(8,128)(2,1)S(1)}, bf16[1,128,384]{2,1,0:T(8,128)(2,1)S(1)}, u32[]{:S(2)}, u32[]{:S(2)}) collective-permute-start(bf16[1,128,384]{2,1,0:T(8,128)(2,1)S(1)} %get-tuple-element.118), channel_id=1, source_target_pairs={{0,16},{4,20},{8,24},{12,28},{16,0},{20,4},{24,8},{28,12},{1,17},{... | collective-permute-start | bytes 294920 | tf_op jit(solution)/shard_map/ppermute | solution.py:326
  38.3 7.6 %collective-permute-start.14 = (bf16[128,384]{1,0:T(8,128)(2,1)S(1)}, bf16[128,384]{1,0:T(8,128)(2,1)S(1)}, u32[]{:S(2)}, u32[]{:S(2)}) collective-permute-start(bf16[128,384]{1,0:T(8,128)(2,1)S(1)} %get-tuple-element.129.refs_0_.second_ref), channel_id=1, source_target_pairs={{0,1},{1,0},{2,3},{3,2},{4,5},{5,4},{6,7},{7,6},{8,9},{9,8},{10,11... | collective-permute-start | bytes 294920 | tf_op jit(solution)/shard_map/ppermute | solution.py:326
  41.4 10.2 %collective-permute-start.19 = (bf16[128,384]{1,0:T(8,128)(2,1)S(1)}, bf16[128,384]{1,0:T(8,128)(2,1)S(1)}, u32[]{:S(2)}, u32[]{:S(2)}) collective-permute-start(bf16[128,384]{1,0:T(8,128)(2,1)S(1)} %get-tuple-element.141.refs_0_.second_ref), channel_id=1, source_target_pairs={{0,3},{1,2},{2,1},{3,0},{4,7},{5,6},{6,5},{7,4},{8,11},{9,10},{10,... | collective-permute-start | bytes 294920 | tf_op jit(solution)/shard_map/ppermute | solution.py:326
  43.8 8.3 %collective-permute-start.20 = (bf16[128,384]{1,0:T(8,128)(2,1)S(1)}, bf16[128,384]{1,0:T(8,128)(2,1)S(1)}, u32[]{:S(2)}, u32[]{:S(2)}) collective-permute-start(bf16[128,384]{1,0:T(8,128)(2,1)S(1)} %get-tuple-element.141.refs_0_.second_ref), channel_id=1, source_target_pairs={{0,2},{1,3},{2,0},{3,1},{4,6},{5,7},{6,4},{7,5},{8,10},{9,11},{10,... | collective-permute-start | bytes 294920 | tf_op jit(solution)/shard_map/ppermute | solution.py:326
  44.6 7.5 %collective-permute-start.21 = (bf16[128,384]{1,0:T(8,128)(2,1)S(1)}, bf16[128,384]{1,0:T(8,128)(2,1)S(1)}, u32[]{:S(2)}, u32[]{:S(2)}) collective-permute-start(bf16[128,384]{1,0:T(8,128)(2,1)S(1)} %get-tuple-element.141.refs_0_.second_ref), channel_id=1, source_target_pairs={{0,1},{1,0},{2,3},{3,2},{4,5},{5,4},{6,7},{7,6},{8,9},{9,8},{10,11... | collective-permute-start | bytes 294920 | tf_op jit(solution)/shard_map/ppermute | solution.py:326
  46.7 1.8 %collective-permute-start.15 = (bf16[4,128,384]{2,1,0:T(8,128)(2,1)S(1)}, bf16[4,128,384]{2,1,0:T(8,128)(2,1)S(1)}, u32[]{:S(2)}, u32[]{:S(2)}) collective-permute-start(bf16[4,128,384]{2,1,0:T(8,128)(2,1)S(1)} %multiply_theirs.6), channel_id=1, source_target_pairs={{0,4},{4,0},{8,12},{12,8},{16,20},{20,16},{24,28},{28,24},{1,5},{5... | collective-permute-start | bytes 1179656 | tf_op jit(solution)/shard_map/ppermute | solution.py:326
  48.6 9.3 %collective-permute-start.16 = (bf16[128,384]{1,0:T(8,128)(2,1)S(1)}, bf16[128,384]{1,0:T(8,128)(2,1)S(1)}, u32[]{:S(2)}, u32[]{:S(2)}) collective-permute-start(bf16[128,384]{1,0:T(8,128)(2,1)S(1)} %get-tuple-element.134), channel_id=1, source_target_pairs={{0,24},{4,28},{8,16},{12,20},{16,8},{20,12},{24,0},{28,4},{1,25},{... | collective-permute-start | bytes 294920 | tf_op jit(solution)/shard_map/ppermute | solution.py:326
  51.1 7.3 %collective-permute-start.17 = (bf16[128,384]{1,0:T(8,128)(2,1)S(1)}, bf16[128,384]{1,0:T(8,128)(2,1)S(1)}, u32[]{:S(2)}, u32[]{:S(2)}) collective-permute-start(bf16[128,384]{1,0:T(8,128)(2,1)S(1)} %get-tuple-element.135), channel_id=1, source_target_pairs={{0,8},{4,12},{8,0},{12,4},{16,24},{20,28},{24,16},{28,20},{1,9},{5... | collective-permute-start | bytes 294920 | tf_op jit(solution)/shard_map/ppermute | solution.py:326
  51.6 6.7 %collective-permute-start.18 = (bf16[128,384]{1,0:T(8,128)(2,1)S(1)}, bf16[128,384]{1,0:T(8,128)(2,1)S(1)}, u32[]{:S(2)}, u32[]{:S(2)}) collective-permute-start(bf16[128,384]{1,0:T(8,128)(2,1)S(1)} %get-tuple-element.136), channel_id=1, source_target_pairs={{0,16},{4,20},{8,24},{12,28},{16,0},{20,4},{24,8},{28,12},{1,17},{... | collective-permute-start | bytes 294920 | tf_op jit(solution)/shard_map/ppermute | solution.py:326
  52.9 1.8 %collective-permute-start.22 = (bf16[4,128,384]{2,1,0:T(8,128)(2,1)S(1)}, bf16[4,128,384]{2,1,0:T(8,128)(2,1)S(1)}, u32[]{:S(2)}, u32[]{:S(2)}) collective-permute-start(bf16[4,128,384]{2,1,0:T(8,128)(2,1)S(1)} %multiply_theirs.7), channel_id=1, source_target_pairs={{0,4},{4,0},{8,12},{12,8},{16,20},{20,16},{24,28},{28,24},{1,5},{5... | collective-permute-start | bytes 1179656 | tf_op jit(solution)/shard_map/ppermute | solution.py:326
  54.8 6.6 %collective-permute-start.23 = (bf16[128,384]{1,0:T(8,128)(2,1)S(1)}, bf16[128,384]{1,0:T(8,128)(2,1)S(1)}, u32[]{:S(2)}, u32[]{:S(2)}) collective-permute-start(bf16[128,384]{1,0:T(8,128)(2,1)S(1)} %get-tuple-element.146), channel_id=1, source_target_pairs={{0,24},{4,28},{8,16},{12,20},{16,8},{20,12},{24,0},{28,4},{1,25},{... | collective-permute-start | bytes 294920 | tf_op jit(solution)/shard_map/ppermute | solution.py:326
  57.3 5.5 %collective-permute-start.24 = (bf16[128,384]{1,0:T(8,128)(2,1)S(1)}, bf16[128,384]{1,0:T(8,128)(2,1)S(1)}, u32[]{:S(2)}, u32[]{:S(2)}) collective-permute-start(bf16[128,384]{1,0:T(8,128)(2,1)S(1)} %get-tuple-element.147), channel_id=1, source_target_pairs={{0,8},{4,12},{8,0},{12,4},{16,24},{20,28},{24,16},{28,20},{1,9},{5... | collective-permute-start | bytes 294920 | tf_op jit(solution)/shard_map/ppermute | solution.py:326
  57.8 5.0 %collective-permute-start.25 = (bf16[128,384]{1,0:T(8,128)(2,1)S(1)}, bf16[128,384]{1,0:T(8,128)(2,1)S(1)}, u32[]{:S(2)}, u32[]{:S(2)}) collective-permute-start(bf16[128,384]{1,0:T(8,128)(2,1)S(1)} %get-tuple-element.148), channel_id=1, source_target_pairs={{0,16},{4,20},{8,24},{12,28},{16,0},{20,4},{24,8},{28,12},{1,17},{... | collective-permute-start | bytes 294920 | tf_op jit(solution)/shard_map/ppermute | solution.py:326

commit v6 on v5

--- a/solution.py
+++ b/solution.py
@@ -25,7 +25,7 @@
     return ids != seed_row
 
 
-def prepare_kernel(cot_ref, seed_ref, out_ref, part_ref, cot, seed, semaphores):
+def prepare_kernel(cot_ref, seed_ref, out_ref, first_ref, last_ref, cot, seed, semaphores):
     copies = [
         pltpu.make_async_copy(cot_ref, cot, semaphores.at[0]),
         pltpu.make_async_copy(seed_ref, seed, semaphores.at[1]),
@@ -38,7 +38,9 @@
     keep = keep_of(seed[...][None, :], 0, part.shape[0])
     labels = jnp.where(keep, part, 0.0).astype(out_ref.dtype)
     out_ref[...] = labels
-    part_ref[...] = labels[: part_ref.shape[0], :]
+    rows = first_ref.shape[0]
+    first_ref[...] = labels[:rows, :]
+    last_ref[...] = labels[rows:, :]
 
 
 def prepare(cotangent, seed_label):
@@ -51,7 +53,7 @@
         in_specs=[pl.BlockSpec(memory_space=pltpu.HBM)] * 2,
         out_shape=[
             jax.ShapeDtypeStruct((count, segment), jnp.bfloat16)
-            for count in (classes, classes // 2)
+            for count in (classes, classes // 2, classes // 2)
         ],
         scratch_shapes=[
             pltpu.VMEM(cotangent.shape, cotangent.dtype),
@@ -327,15 +329,16 @@
 
 
 def stack_kernel(own_ref, arrived_ref, out_ref):
-    rows = out_ref.shape[0] // 2
-    out_ref[:rows, :] = own_ref[rows:, :]
-    out_ref[rows:, :] = arrived_ref[rows:, :]
+    rows = own_ref.shape[0]
+    out_ref[:rows, :] = own_ref[...]
+    out_ref[rows:, :] = arrived_ref[...]
 
 
 def stack(own, arrived):
+    rows, segment = own.shape
     return pl.pallas_call(
         stack_kernel,
-        out_shape=jax.ShapeDtypeStruct(own.shape, own.dtype),
+        out_shape=jax.ShapeDtypeStruct((2 * rows, segment), own.dtype),
         name="stack_labels",
         compiler_params=params(),
         cost_estimate=CHEAP,
@@ -349,20 +352,19 @@
     return [0] + offsets, [0] * n_col, [labels] + parts
 
 
-def gather_both(labels, part, n_col, waits):
-    rows, half = part.shape[0], n_col // 2
-    across = flip(labels, "col", n_col, half)
-    others = [k for k in range(1, n_col) if k != half]
-    parts = [flip(part, "col", n_col, k) for k in others]
-    first = [0, half] + others, [0] * n_col, [labels, across] + parts
-    both, across = after((labels, across), waits)
-    both = stack(both, across)
-    sources = [0, half], [rows, rows], [labels, across]
+def gather_both(first, last, n_col, waits):
+    rows, half = first.shape[0], n_col // 2
+    others = [half] + [k for k in range(1, n_col) if k != half]
+    parts = [flip(first, "col", n_col, k) for k in others]
+    across = flip(last, "col", n_col, half)
+    sources_first = [0] + others, [0] * n_col, [first] + parts
+    both = stack(*after((last, across), waits))
+    sources = [0, half], [0, 0], [last, across]
     for k in range(1, half):
         arrived = flip(both, "col", n_col, k)
         for values, more in zip(sources, ([k, k ^ half], [0, rows], [arrived, arrived])):
             values.extend(more)
-    return first, sources, both
+    return sources_first, sources, both
 
 
 def spread(parts, offsets, n_row):
@@ -378,10 +380,10 @@
     offsets = [0, chips - 1, *range(1, chips - 1)]
     col_place = lax.axis_index("col").astype(jnp.int32)
     place = jnp.stack([lax.axis_index("row").astype(jnp.int32), col_place])
-    first_in, first_a = prepare(cotangent, seed_label)
+    first_in, first_a, first_b = prepare(cotangent, seed_label)
     codes = slot_codes(col_place, blocks, tile_rows[0, 0], tile_cols[0, 0], tile_scale[0, 0])
     matrix = densify(place, codes, tile_values, depth, segment)
-    sources_a, sources_b, both = gather_both(first_in, first_a, n_col, matrix)
+    sources_a, sources_b, both = gather_both(first_a, first_b, n_col, matrix)
 
     def for_theirs(labels, waits, pieces=1):
         labels = *labels[:2], after(labels[2], waits)
@@ -421,11 +423,11 @@
     turned_a = turn(after(grad_a, done))
     grad_b, second_b = middle(seed_label, after(pieces_b, turned_a), rows)
 
-    theirs, swapped_a = for_theirs(sources_a, [grad_b, second_b])
+    theirs, swapped_a = for_theirs(sources_a, [grad_b, second_b], 2)
     mine = for_mine(sources_a, theirs, 20)
     sources_b = gather(second_b, n_col, (3, 2, 1))
     parts_a = add_pairs(mine, swapped_a)
-    theirs, swapped_b = for_theirs(sources_b, parts_a)
+    theirs, swapped_b = for_theirs(sources_b, parts_a, 2)
     mine = for_mine(sources_b, theirs, 20)
     pieces_a = spread(parts_a, offsets, n_row)
     parts_b = add_pairs(mine, swapped_b)

time: 63.8 us -> 63.2 us (level)
  waiting for transfers between devices: 14.2 us -> 10.2 us
  starting transfers between devices: 29.8 us -> 33.4 us
    ppermute x26 -> x29, waiting for transfers between devices: 14.2 us -> 10.2 us  [flip(): return lax.ppermute(array, axis, [(i, i ^ bits) for i in range(size)])]
    ppermute x26 -> x29, starting transfers between devices: 29.8 us -> 33.4 us  [flip(): return lax.ppermute(array, axis, [(i, i ^ bits) for i in range(size)])]
  transfers between devices with their start and end apart: 26 -> 29, of which waited for: 11 -> 12; matrix products, arithmetic and copies ran while one was open for 1% -> 1% of each run, Pallas kernels for 25% -> 26%
where the time goes in v6:
time: 63.2 us; the launch traced here: 63.1 us
  starting transfers between devices  33.4 us (53%)
  Pallas kernels  18.1 us (29%)
  waiting for transfers between devices  10.2 us (16%)
  between operations  0.87 us (1%)
    ppermute x29, starting transfers between devices, flip(): return lax.ppermute(array, axis, [(i, i ^ bits) for i in range(size)])  33.4 us
    ppermute x29, waiting for transfers between devices, flip(): return lax.ppermute(array, axis, [(i, i ^ bits) for i in range(size)])  10.2 us
    pallas_call x1, Pallas kernels, densify(): pl.pallas_call(densify_kernel, in_specs=[pl.BlockSpec(memory_space=pltpu....  8.3 us
    pallas_call x8, Pallas kernels, multiply(): pl.pallas_call(functools.partial(multiply_kernel, tuple(offsets), tuple(f...  6.34 us
  transfers between devices with their start and end apart: 29, of which 12 were waited for; matrix products, arithmetic and copies ran while one was open for 1% of the time, Pallas kernels for 26%

profile of v6, /device:TPU:0, one launch (start us, length us, event | category | flops | bytes accessed | tf_op | source)
XLA Modules:
  0.0 63.1 jit_solution(5015114322487118187)
XLA Ops:
  0.7 1.1 %prepare.1 = (bf16[256,384]{1,0:T(8,128)(2,1)S(1)}, bf16[128,384]{1,0:T(8,128)(2,1)S(1)}, bf16[128,384]{1,0:T(8,128)(2,1)S(1)}) custom-call(bf16[384,256]{1,0:T(8,128)(2,1)} %cot_ref.1, s32[384]{0:T(512)} %seed_ref.5), custom_call_target="tpu_custom_call" | custom-call | flops 10000000000 | bytes 1 | tf_op jit(solution)/shard_map/prepare/pallas_call | solution.py:51
  1.8 5.1 %collective-permute-start.2 = (bf16[128,384]{1,0:T(8,128)(2,1)S(1)}, bf16[128,384]{1,0:T(8,128)(2,1)S(1)}, u32[]{:S(2)}, u32[]{:S(2)}) collective-permute-start(bf16[128,384]{1,0:T(8,128)(2,1)S(1)} %get-tuple-element.97.refs_0_), channel_id=1, source_target_pairs={{0,3},{1,2},{2,1},{3,0},{4,7},{5,6},{6,5},{7,4},{8,11},{9,10},{10,... | collective-permute-start | bytes 294920 | tf_op jit(solution)/shard_map/ppermute | solution.py:328
  6.9 0.6 %collective-permute-start = (bf16[128,384]{1,0:T(8,128)(2,1)S(1)}, bf16[128,384]{1,0:T(8,128)(2,1)S(1)}, u32[]{:S(2)}, u32[]{:S(2)}) collective-permute-start(bf16[128,384]{1,0:T(8,128)(2,1)S(1)} %get-tuple-element.97.refs_0_), channel_id=1, source_target_pairs={{0,2},{1,3},{2,0},{3,1},{4,6},{5,7},{6,4},{7,5},{8,10},{9,11},{10,... | collective-permute-start | bytes 294920 | tf_op jit(solution)/shard_map/ppermute | solution.py:328
  7.5 2.3 %collective-permute-start.3 = (bf16[128,384]{1,0:T(8,128)(2,1)S(1)}, bf16[128,384]{1,0:T(8,128)(2,1)S(1)}, u32[]{:S(2)}, u32[]{:S(2)}) collective-permute-start(bf16[128,384]{1,0:T(8,128)(2,1)S(1)} %get-tuple-element.110.own_ref.refs_0_), channel_id=1, source_target_pairs={{0,2},{1,3},{2,0},{3,1},{4,6},{5,7},{6,4},{7,5},{8,10},{9,11},{10,... | collective-permute-start | bytes 294920 | tf_op jit(solution)/shard_map/ppermute | solution.py:328
  9.9 0.3 convert_reduce_fusion
  10.2 0.2 select_reduce_fusion.codes_ref
  10.4 8.3 %densify.1.refs_4_ = bf16[1536,3072]{1,0:T(8,128)(2,1)S(1)} custom-call(s32[2]{0:T(128)S(1)} %pad_add_fusion.place_ref, s32[8,48]{1,0:T(8,128)S(1)} %select_reduce_fusion.codes_ref, bf16[1,1,8,48,128,128]{5,4,3,2,1,0:T(8,128)(2,1)} %tiles_ref.1), custom_call_target="tpu_custom_call" | custom-call | tf_op jit(solution)/shard_map/densify/pallas_call | solution.py:130
  18.7 0.6 collective-permute-done.3.arrived_ref.refs_1_
  19.4 1.5 %collective-permute-start.9 = (bf16[256,384]{1,0:T(8,128)(2,1)S(1)}, bf16[256,384]{1,0:T(8,128)(2,1)S(1)}, u32[]{:S(2)}, u32[]{:S(2)}) collective-permute-start(bf16[256,384]{1,0:T(8,128)(2,1)S(1)} %stack_labels.1), channel_id=1, source_target_pairs={{0,1},{1,0},{2,3},{3,2},{4,5},{5,4},{6,7},{7,6},{8,9},{9,8},{10,11... | collective-permute-start | bytes 589832 | tf_op jit(solution)/shard_map/ppermute | solution.py:328
  20.9 0.8 %multiply_theirs.4 = (bf16[2,128,384]{2,1,0:T(8,128)(2,1)S(1)}, bf16[2,128,384]{2,1,0:T(8,128)(2,1)S(1)}) custom-call(bf16[128,384]{1,0:T(8,128)(2,1)S(1)} %get-tuple-element.97.refs_0_, bf16[128,384]{1,0:T(8,128)(2,1)S(1)} %collective-permute-done.refs_1_, bf16[128,384]{1,0:T(8,128)(2,1)S(1)} %collective-permute-done.1.refs_2_, ...), custom_call_target="tpu_custom_call" | custom-call | bytes 1 | tf_op jit(solution)/shard_map/multiply_theirs/pallas_call | solution.py:170
  21.8 0.5 collective-permute-start.6
  22.3 0.8 %multiply_mine.4.mine_ref = f32[4,128,384]{2,1,0:T(8,128)S(1)} custom-call(bf16[128,384]{1,0:T(8,128)(2,1)S(1)} %get-tuple-element.97.refs_0_, bf16[128,384]{1,0:T(8,128)(2,1)S(1)} %collective-permute-done.refs_1_, bf16[128,384]{1,0:T(8,128)(2,1)S(1)} %collective-permute-done.1.refs_2_, bf16[128,384]{1,0:T(8,128)(2,1)S(1)} %collective-permute-done.2.refs_3_, ...), custom_call_target="tpu_custom_call" | custom-call | flops 24159191040 | bytes 1 | tf_op jit(solution)/shard_map/multiply_mine/pallas_call | solution.py:170
  23.0 0.1 collective-permute-done.4.theirs_ref
  23.2 2.5 %collective-permute-start.5 = (bf16[128,384]{1,0:T(8,128)(2,1)S(1)}, bf16[128,384]{1,0:T(8,128)(2,1)S(1)}, u32[]{:S(2)}, u32[]{:S(2)}) collective-permute-start(bf16[128,384]{1,0:T(8,128)(2,1)S(1)} %get-tuple-element.102), channel_id=1, source_target_pairs={{0,24},{4,28},{8,16},{12,20},{16,8},{20,12},{24,0},{28,4},{1,25},{... | collective-permute-start | bytes 294920 | tf_op jit(solution)/shard_map/ppermute | solution.py:328
  25.8 0.6 collective-permute-start.7
  26.4 0.5 collective-permute-start.8
  26.9 0.8 %multiply_theirs.5 = bf16[4,128,384]{2,1,0:T(8,128)(2,1)S(1)} custom-call(bf16[128,384]{1,0:T(8,128)(2,1)S(1)} %get-tuple-element.110.own_ref.refs_0_, bf16[128,384]{1,0:T(8,128)(2,1)S(1)} %collective-permute-done.3.arrived_ref.refs_1_, bf16[256,384]{1,0:T(8,128)(2,1)S(1)} %collective-permute-done.9.refs_2_.refs_3_, ...), custom_call_target="tpu_custom_call" | custom-call | bytes 1 | tf_op jit(solution)/shard_map/multiply_theirs/pallas_call | solution.py:170
  27.8 0.8 %multiply_mine.5.kept_ref = f32[4,128,384]{2,1,0:T(8,128)S(1)} custom-call(bf16[128,384]{1,0:T(8,128)(2,1)S(1)} %get-tuple-element.110.own_ref.refs_0_, bf16[128,384]{1,0:T(8,128)(2,1)S(1)} %collective-permute-done.3.arrived_ref.refs_1_, bf16[256,384]{1,0:T(8,128)(2,1)S(1)} %collective-permute-done.9.refs_2_.refs_3_, ...), custom_call_target="tpu_custom_call" | custom-call | flops 24159191040 | bytes 1 | tf_op jit(solution)/shard_map/multiply_mine/pallas_call | solution.py:170
  28.6 0.9 %collective-permute-done.10.arrived_ref = bf16[4,128,384]{2,1,0:T(8,128)(2,1)S(1)} collective-permute-done((bf16[4,128,384]{2,1,0:T(8,128)(2,1)S(1)}, bf16[4,128,384]{2,1,0:T(8,128)(2,1)S(1)}, u32[]{:S(2)}, u32[]{:S(2)}) %collective-permute-start.10) | collective-permute-done | bytes 393248 | tf_op jit(solution)/shard_map/ppermute | solution.py:328
  29.6 1.5 %collective-permute-start.11 = (bf16[2,128,384]{2,1,0:T(8,128)(2,1)S(1)}, bf16[2,128,384]{2,1,0:T(8,128)(2,1)S(1)}, u32[]{:S(2)}, u32[]{:S(2)}) collective-permute-start(bf16[2,128,384]{2,1,0:T(8,128)(2,1)S(1)} %get-tuple-element.115), channel_id=1, source_target_pairs={{0,8},{4,12},{8,0},{12,4},{16,24},{20,28},{24,16},{28,20},{1,9},{5... | collective-permute-start | bytes 589832 | tf_op jit(solution)/shard_map/ppermute | solution.py:328
  31.4 1.8 %collective-permute-start.14 = (bf16[128,384]{1,0:T(8,128)(2,1)S(1)}, bf16[128,384]{1,0:T(8,128)(2,1)S(1)}, u32[]{:S(2)}, u32[]{:S(2)}) collective-permute-start(bf16[128,384]{1,0:T(8,128)(2,1)S(1)} %get-tuple-element.139.refs_0_.second_ref), channel_id=1, source_target_pairs={{0,2},{1,3},{2,0},{3,1},{4,6},{5,7},{6,4},{7,5},{8,10},{9,11},{10,... | collective-permute-start | bytes 294920 | tf_op jit(solution)/shard_map/ppermute | solution.py:328
  33.2 1.3 %collective-permute-start.13 = (bf16[128,384]{1,0:T(8,128)(2,1)S(1)}, bf16[128,384]{1,0:T(8,128)(2,1)S(1)}, u32[]{:S(2)}, u32[]{:S(2)}) collective-permute-start(bf16[128,384]{1,0:T(8,128)(2,1)S(1)} %get-tuple-element.139.refs_0_.second_ref), channel_id=1, source_target_pairs={{0,3},{1,2},{2,1},{3,0},{4,7},{5,6},{6,5},{7,4},{8,11},{9,10},{10,... | collective-permute-start | bytes 294920 | tf_op jit(solution)/shard_map/ppermute | solution.py:328
  34.4 2.2 %collective-permute-done.11.arrived_ref = bf16[2,128,384]{2,1,0:T(8,128)(2,1)S(1)} collective-permute-done((bf16[2,128,384]{2,1,0:T(8,128)(2,1)S(1)}, bf16[2,128,384]{2,1,0:T(8,128)(2,1)S(1)}, u32[]{:S(2)}, u32[]{:S(2)}) %collective-permute-start.11) | collective-permute-done | bytes 196640 | tf_op jit(solution)/shard_map/ppermute | solution.py:328
  36.6 1.6 %collective-permute-start.12 = (bf16[1,128,384]{2,1,0:T(8,128)(2,1)S(1)}, bf16[1,128,384]{2,1,0:T(8,128)(2,1)S(1)}, u32[]{:S(2)}, u32[]{:S(2)}) collective-permute-start(bf16[1,128,384]{2,1,0:T(8,128)(2,1)S(1)} %get-tuple-element.125), channel_id=1, source_target_pairs={{0,16},{4,20},{8,24},{12,28},{16,0},{20,4},{24,8},{28,12},{1,17},{... | collective-permute-start | bytes 294920 | tf_op jit(solution)/shard_map/ppermute | solution.py:328
  38.2 0.6 collective-permute-start.15
  38.9 2.4 %collective-permute-done.12.refs_1_ = bf16[1,128,384]{2,1,0:T(8,128)(2,1)S(1)} collective-permute-done((bf16[1,128,384]{2,1,0:T(8,128)(2,1)S(1)}, bf16[1,128,384]{2,1,0:T(8,128)(2,1)S(1)}, u32[]{:S(2)}, u32[]{:S(2)}) %collective-permute-start.12) | collective-permute-done | bytes 98336 | tf_op jit(solution)/shard_map/ppermute | solution.py:328
  41.4 0.7 %collective-permute-start.23 = (bf16[128,384]{1,0:T(8,128)(2,1)S(1)}, bf16[128,384]{1,0:T(8,128)(2,1)S(1)}, u32[]{:S(2)}, u32[]{:S(2)}) collective-permute-start(bf16[128,384]{1,0:T(8,128)(2,1)S(1)} %get-tuple-element.154.refs_0_.second_ref), channel_id=1, source_target_pairs={{0,1},{1,0},{2,3},{3,2},{4,5},{5,4},{6,7},{7,6},{8,9},{9,8},{10,11... | collective-permute-start | bytes 294920 | tf_op jit(solution)/shard_map/ppermute | solution.py:328
  42.0 1.8 %collective-permute-start.22 = (bf16[128,384]{1,0:T(8,128)(2,1)S(1)}, bf16[128,384]{1,0:T(8,128)(2,1)S(1)}, u32[]{:S(2)}, u32[]{:S(2)}) collective-permute-start(bf16[128,384]{1,0:T(8,128)(2,1)S(1)} %get-tuple-element.154.refs_0_.second_ref), channel_id=1, source_target_pairs={{0,2},{1,3},{2,0},{3,1},{4,6},{5,7},{6,4},{7,5},{8,10},{9,11},{10,... | collective-permute-start | bytes 294920 | tf_op jit(solution)/shard_map/ppermute | solution.py:328
  43.9 2.0 %collective-permute-start.21 = (bf16[128,384]{1,0:T(8,128)(2,1)S(1)}, bf16[128,384]{1,0:T(8,128)(2,1)S(1)}, u32[]{:S(2)}, u32[]{:S(2)}) collective-permute-start(bf16[128,384]{1,0:T(8,128)(2,1)S(1)} %get-tuple-element.154.refs_0_.second_ref), channel_id=1, source_target_pairs={{0,3},{1,2},{2,1},{3,0},{4,7},{5,6},{6,5},{7,4},{8,11},{9,10},{10,... | collective-permute-start | bytes 294920 | tf_op jit(solution)/shard_map/ppermute | solution.py:328
  45.8 0.8 %multiply_theirs.6 = (bf16[2,128,384]{2,1,0:T(8,128)(2,1)S(1)}, bf16[2,128,384]{2,1,0:T(8,128)(2,1)S(1)}) custom-call(bf16[128,384]{1,0:T(8,128)(2,1)S(1)} %get-tuple-element.139.refs_0_.second_ref, bf16[128,384]{1,0:T(8,128)(2,1)S(1)} %collective-permute-done.13.refs_1_, bf16[128,384]{1,0:T(8,128)(2,1)S(1)} %collective-permute-done.14.refs_2_, ...), custom_call_target="tpu_custom_call" | custom-call | bytes 1 | tf_op jit(solution)/shard_map/multiply_theirs/pallas_call | solution.py:170
  46.7 0.5 collective-permute-start.18
  47.2 0.8 %multiply_mine.6.mine_ref = f32[4,128,384]{2,1,0:T(8,128)S(1)} custom-call(bf16[128,384]{1,0:T(8,128)(2,1)S(1)} %get-tuple-element.139.refs_0_.second_ref, bf16[128,384]{1,0:T(8,128)(2,1)S(1)} %collective-permute-done.13.refs_1_, bf16[128,384]{1,0:T(8,128)(2,1)S(1)} %collective-permute-done.14.refs_2_, bf16[128,384]{1,0:T(8,128)(2,1)S(1)} %collective-permute-done.15.refs_3_, ...), custom_call_target="tpu_custom_call" | custom-call | flops 24159191040 | bytes 1 | tf_op jit(solution)/shard_map/multiply_mine/pallas_call | solution.py:170
  48.0 0.1 collective-permute-done.16.theirs_ref
  48.2 2.5 %collective-permute-start.17 = (bf16[128,384]{1,0:T(8,128)(2,1)S(1)}, bf16[128,384]{1,0:T(8,128)(2,1)S(1)}, u32[]{:S(2)}, u32[]{:S(2)}) collective-permute-start(bf16[128,384]{1,0:T(8,128)(2,1)S(1)} %get-tuple-element.144), channel_id=1, source_target_pairs={{0,24},{4,28},{8,16},{12,20},{16,8},{20,12},{24,0},{28,4},{1,25},{... | collective-permute-start | bytes 294920 | tf_op jit(solution)/shard_map/ppermute | solution.py:328
  50.7 0.6 %collective-permute-start.19 = (bf16[128,384]{1,0:T(8,128)(2,1)S(1)}, bf16[128,384]{1,0:T(8,128)(2,1)S(1)}, u32[]{:S(2)}, u32[]{:S(2)}) collective-permute-start(bf16[128,384]{1,0:T(8,128)(2,1)S(1)} %get-tuple-element.146), channel_id=1, source_target_pairs={{0,8},{4,12},{8,0},{12,4},{16,24},{20,28},{24,16},{28,20},{1,9},{5... | collective-permute-start | bytes 294920 | tf_op jit(solution)/shard_map/ppermute | solution.py:328
  51.4 0.5 collective-permute-start.20
  51.9 0.8 %multiply_theirs.7 = (bf16[2,128,384]{2,1,0:T(8,128)(2,1)S(1)}, bf16[2,128,384]{2,1,0:T(8,128)(2,1)S(1)}) custom-call(bf16[128,384]{1,0:T(8,128)(2,1)S(1)} %get-tuple-element.154.refs_0_.second_ref, bf16[128,384]{1,0:T(8,128)(2,1)S(1)} %collective-permute-done.21.refs_1_, bf16[128,384]{1,0:T(8,128)(2,1)S(1)} %collective-permute-done.22.refs_2_, ...), custom_call_target="tpu_custom_call" | custom-call | bytes 1 | tf_op jit(solution)/shard_map/multiply_theirs/pallas_call | solution.py:170
  52.7 0.5 collective-permute-start.25
  53.2 0.8 %multiply_mine.7.mine_ref = f32[4,128,384]{2,1,0:T(8,128)S(1)} custom-call(bf16[128,384]{1,0:T(8,128)(2,1)S(1)} %get-tuple-element.154.refs_0_.second_ref, bf16[128,384]{1,0:T(8,128)(2,1)S(1)} %collective-permute-done.21.refs_1_, bf16[128,384]{1,0:T(8,128)(2,1)S(1)} %collective-permute-done.22.refs_2_, bf16[128,384]{1,0:T(8,128)(2,1)S(1)} %collective-permute-done.23.refs_3_, ...), custom_call_target="tpu_custom_call" | custom-call | flops 24159191040 | bytes 1 | tf_op jit(solution)/shard_map/multiply_mine/pallas_call | solution.py:170
  54.0 0.1 collective-permute-done.24.theirs_ref
  54.2 2.5 %collective-permute-start.26 = (bf16[128,384]{1,0:T(8,128)(2,1)S(1)}, bf16[128,384]{1,0:T(8,128)(2,1)S(1)}, u32[]{:S(2)}, u32[]{:S(2)}) collective-permute-start(bf16[128,384]{1,0:T(8,128)(2,1)S(1)} %get-tuple-element.159), channel_id=1, source_target_pairs={{0,24},{4,28},{8,16},{12,20},{16,8},{20,12},{24,0},{28,4},{1,25},{... | collective-permute-start | bytes 294920 | tf_op jit(solution)/shard_map/ppermute | solution.py:328
  56.7 0.6 %collective-permute-start.27 = (bf16[128,384]{1,0:T(8,128)(2,1)S(1)}, bf16[128,384]{1,0:T(8,128)(2,1)S(1)}, u32[]{:S(2)}, u32[]{:S(2)}) collective-permute-start(bf16[128,384]{1,0:T(8,128)(2,1)S(1)} %get-tuple-element.161), channel_id=1, source_target_pairs={{0,8},{4,12},{8,0},{12,4},{16,24},{20,28},{24,16},{28,20},{1,9},{5... | collective-permute-start | bytes 294920 | tf_op jit(solution)/shard_map/ppermute | solution.py:328
  57.4 0.5 collective-permute-start.28
  57.9 0.2 label_grad.1.refs_0_
  58.0 0.8 %first_grad_out.1 = bf16[384,256]{1,0:T(8,128)(2,1)} custom-call(bf16[384,128]{1,0:T(8,128)(2,1)S(1)} %turn_grad.1.refs_0_, bf16[128,384]{1,0:T(8,128)(2,1)S(1)} %get-tuple-element.167.refs_1_), custom_call_target="tpu_custom_call" | custom-call | flops 1 | bytes 1 | tf_op jit(solution)/shard_map/first_grad_out/pallas_call | solution.py:277
  58.8 2.0 %collective-permute-done.26.refs_2_ = bf16[128,384]{1,0:T(8,128)(2,1)S(1)} collective-permute-done((bf16[128,384]{1,0:T(8,128)(2,1)S(1)}, bf16[128,384]{1,0:T(8,128)(2,1)S(1)}, u32[]{:S(2)}, u32[]{:S(2)}) %collective-permute-start.26) | collective-permute-done | bytes 98336 | tf_op jit(solution)/shard_map/ppermute | solution.py:328
  60.8 1.4 %collective-permute-done.27.refs_3_ = bf16[128,384]{1,0:T(8,128)(2,1)S(1)} collective-permute-done((bf16[128,384]{1,0:T(8,128)(2,1)S(1)}, bf16[128,384]{1,0:T(8,128)(2,1)S(1)}, u32[]{:S(2)}, u32[]{:S(2)}) %collective-permute-start.27) | collective-permute-done | bytes 98336 | tf_op jit(solution)/shard_map/ppermute | solution.py:328
  62.3 0.8 %label_grad_out.1 = bf16[384,256]{1,0:T(8,128)(2,1)} custom-call(bf16[256,384]{1,0:T(8,128)(2,1)S(1)} %get-tuple-element.130.first_ref, bf16[128,384]{1,0:T(8,128)(2,1)S(1)} %get-tuple-element.154.refs_0_.second_ref, bf16[384,128]{1,0:T(8,128)(2,1)S(1)} %label_grad.1.refs_0_, f32[128,384]{1,0:T(8,128)S(1)} %get-tuple-element.168.refs_1_, ...), custom_call_target="tpu_custom_call" | custom-call | flops 1 | bytes 1 | tf_op jit(solution)/shard_map/label_grad_out/pallas_call | solution.py:318
  (48 shorter events, 1.3 us)
Async XLA Ops:
  0.6 9.2 %copy-start.1 = (s32[1,1,8,48]{3,2,1,0:T(8,128)S(1)}, s32[1,1,8,48]{3,2,1,0:T(8,128)}, u32[]{:S(2)}) copy-start(s32[1,1,8,48]{3,2,1,0:T(8,128)} %param.11) | copy-start | bytes 4612
  0.6 9.2 %copy-start.2 = (s32[1,1,8,48]{3,2,1,0:T(8,128)S(1)}, s32[1,1,8,48]{3,2,1,0:T(8,128)}, u32[]{:S(2)}) copy-start(s32[1,1,8,48]{3,2,1,0:T(8,128)} %param.10) | copy-start | bytes 4612
  0.7 9.2 %copy-start.3 = (s32[1,1,8,48]{3,2,1,0:T(8,128)S(1)}, s32[1,1,8,48]{3,2,1,0:T(8,128)}, u32[]{:S(2)}) copy-start(s32[1,1,8,48]{3,2,1,0:T(8,128)} %param.9) | copy-start | bytes 4612
  1.8 19.1 %collective-permute-start.2 = (bf16[128,384]{1,0:T(8,128)(2,1)S(1)}, bf16[128,384]{1,0:T(8,128)(2,1)S(1)}, u32[]{:S(2)}, u32[]{:S(2)}) collective-permute-start(bf16[128,384]{1,0:T(8,128)(2,1)S(1)} %get-tuple-element.97.refs_0_), channel_id=1, source_target_pairs={{0,3},{1,2},{2,1},{3,0},{4,7},{5,6},{6,5},{7,4},{8,11},{9,10},{10,... | collective-permute-start | bytes 294920 | tf_op jit(solution)/shard_map/ppermute | solution.py:328
  6.9 14.0 %collective-permute-start.1 = (bf16[128,384]{1,0:T(8,128)(2,1)S(1)}, bf16[128,384]{1,0:T(8,128)(2,1)S(1)}, u32[]{:S(2)}, u32[]{:S(2)}) collective-permute-start(bf16[128,384]{1,0:T(8,128)(2,1)S(1)} %get-tuple-element.97.refs_0_), channel_id=1, source_target_pairs={{0,1},{1,0},{2,3},{3,2},{4,5},{5,4},{6,7},{7,6},{8,9},{9,8},{10,11... | collective-permute-start | bytes 294920 | tf_op jit(solution)/shard_map/ppermute | solution.py:328
  6.9 14.0 %collective-permute-start = (bf16[128,384]{1,0:T(8,128)(2,1)S(1)}, bf16[128,384]{1,0:T(8,128)(2,1)S(1)}, u32[]{:S(2)}, u32[]{:S(2)}) collective-permute-start(bf16[128,384]{1,0:T(8,128)(2,1)S(1)} %get-tuple-element.97.refs_0_), channel_id=1, source_target_pairs={{0,2},{1,3},{2,0},{3,1},{4,6},{5,7},{6,4},{7,5},{8,10},{9,11},{10,... | collective-permute-start | bytes 294920 | tf_op jit(solution)/shard_map/ppermute | solution.py:328
  7.5 11.8 %collective-permute-start.3 = (bf16[128,384]{1,0:T(8,128)(2,1)S(1)}, bf16[128,384]{1,0:T(8,128)(2,1)S(1)}, u32[]{:S(2)}, u32[]{:S(2)}) collective-permute-start(bf16[128,384]{1,0:T(8,128)(2,1)S(1)} %get-tuple-element.110.own_ref.refs_0_), channel_id=1, source_target_pairs={{0,2},{1,3},{2,0},{3,1},{4,6},{5,7},{6,4},{7,5},{8,10},{9,11},{10,... | collective-permute-start | bytes 294920 | tf_op jit(solution)/shard_map/ppermute | solution.py:328
  19.4 7.5 %collective-permute-start.9 = (bf16[256,384]{1,0:T(8,128)(2,1)S(1)}, bf16[256,384]{1,0:T(8,128)(2,1)S(1)}, u32[]{:S(2)}, u32[]{:S(2)}) collective-permute-start(bf16[256,384]{1,0:T(8,128)(2,1)S(1)} %stack_labels.1), channel_id=1, source_target_pairs={{0,1},{1,0},{2,3},{3,2},{4,5},{5,4},{6,7},{7,6},{8,9},{9,8},{10,11... | collective-permute-start | bytes 589832 | tf_op jit(solution)/shard_map/ppermute | solution.py:328
  21.7 1.5 %collective-permute-start.4 = (bf16[2,128,384]{2,1,0:T(8,128)(2,1)S(1)}, bf16[2,128,384]{2,1,0:T(8,128)(2,1)S(1)}, u32[]{:S(2)}, u32[]{:S(2)}) collective-permute-start(bf16[2,128,384]{2,1,0:T(8,128)(2,1)S(1)} %get-tuple-element.95), channel_id=1, source_target_pairs={{0,4},{4,0},{8,12},{12,8},{16,20},{20,16},{24,28},{28,24},{1,5},{5... | collective-permute-start | bytes 589832 | tf_op jit(solution)/shard_map/ppermute | solution.py:328
  21.8 4.0 %collective-permute-start.6 = (bf16[2,128,384]{2,1,0:T(8,128)(2,1)S(1)}, bf16[2,128,384]{2,1,0:T(8,128)(2,1)S(1)}, u32[]{:S(2)}, u32[]{:S(2)}) collective-permute-start(bf16[2,128,384]{2,1,0:T(8,128)(2,1)S(1)} %get-tuple-element.96), channel_id=1, source_target_pairs={{0,4},{4,0},{8,12},{12,8},{16,20},{20,16},{24,28},{28,24},{1,5},{5... | collective-permute-start | bytes 589832 | tf_op jit(solution)/shard_map/ppermute | solution.py:328
  23.2 8.1 %collective-permute-start.5 = (bf16[128,384]{1,0:T(8,128)(2,1)S(1)}, bf16[128,384]{1,0:T(8,128)(2,1)S(1)}, u32[]{:S(2)}, u32[]{:S(2)}) collective-permute-start(bf16[128,384]{1,0:T(8,128)(2,1)S(1)} %get-tuple-element.102), channel_id=1, source_target_pairs={{0,24},{4,28},{8,16},{12,20},{16,8},{20,12},{24,0},{28,4},{1,25},{... | collective-permute-start | bytes 294920 | tf_op jit(solution)/shard_map/ppermute | solution.py:328
  25.8 5.4 %collective-permute-start.7 = (bf16[128,384]{1,0:T(8,128)(2,1)S(1)}, bf16[128,384]{1,0:T(8,128)(2,1)S(1)}, u32[]{:S(2)}, u32[]{:S(2)}) collective-permute-start(bf16[128,384]{1,0:T(8,128)(2,1)S(1)} %get-tuple-element.104), channel_id=1, source_target_pairs={{0,8},{4,12},{8,0},{12,4},{16,24},{20,28},{24,16},{28,20},{1,9},{5... | collective-permute-start | bytes 294920 | tf_op jit(solution)/shard_map/ppermute | solution.py:328
  26.4 4.9 %collective-permute-start.8 = (bf16[128,384]{1,0:T(8,128)(2,1)S(1)}, bf16[128,384]{1,0:T(8,128)(2,1)S(1)}, u32[]{:S(2)}, u32[]{:S(2)}) collective-permute-start(bf16[128,384]{1,0:T(8,128)(2,1)S(1)} %get-tuple-element.105), channel_id=1, source_target_pairs={{0,16},{4,20},{8,24},{12,28},{16,0},{20,4},{24,8},{28,12},{1,17},{... | collective-permute-start | bytes 294920 | tf_op jit(solution)/shard_map/ppermute | solution.py:328
  27.7 3.6 %copy-start = (s32[384]{0:T(512)S(1)}, s32[384]{0:T(512)}, u32[]{:S(2)}) copy-start(s32[384]{0:T(512)} %seed_ref.5) | copy-start | bytes 4612
  27.7 1.8 %collective-permute-start.10 = (bf16[4,128,384]{2,1,0:T(8,128)(2,1)S(1)}, bf16[4,128,384]{2,1,0:T(8,128)(2,1)S(1)}, u32[]{:S(2)}, u32[]{:S(2)}) collective-permute-start(bf16[4,128,384]{2,1,0:T(8,128)(2,1)S(1)} %multiply_theirs.5), channel_id=1, source_target_pairs={{0,4},{4,0},{8,12},{12,8},{16,20},{20,16},{24,28},{28,24},{1,5},{5... | collective-permute-start | bytes 1179656 | tf_op jit(solution)/shard_map/ppermute | solution.py:328
  29.6 7.0 %collective-permute-start.11 = (bf16[2,128,384]{2,1,0:T(8,128)(2,1)S(1)}, bf16[2,128,384]{2,1,0:T(8,128)(2,1)S(1)}, u32[]{:S(2)}, u32[]{:S(2)}) collective-permute-start(bf16[2,128,384]{2,1,0:T(8,128)(2,1)S(1)} %get-tuple-element.115), channel_id=1, source_target_pairs={{0,8},{4,12},{8,0},{12,4},{16,24},{20,28},{24,16},{28,20},{1,9},{5... | collective-permute-start | bytes 589832 | tf_op jit(solution)/shard_map/ppermute | solution.py:328
  31.4 12.5 %collective-permute-start.14 = (bf16[128,384]{1,0:T(8,128)(2,1)S(1)}, bf16[128,384]{1,0:T(8,128)(2,1)S(1)}, u32[]{:S(2)}, u32[]{:S(2)}) collective-permute-start(bf16[128,384]{1,0:T(8,128)(2,1)S(1)} %get-tuple-element.139.refs_0_.second_ref), channel_id=1, source_target_pairs={{0,2},{1,3},{2,0},{3,1},{4,6},{5,7},{6,4},{7,5},{8,10},{9,11},{10,... | collective-permute-start | bytes 294920 | tf_op jit(solution)/shard_map/ppermute | solution.py:328
  33.2 12.7 %collective-permute-start.13 = (bf16[128,384]{1,0:T(8,128)(2,1)S(1)}, bf16[128,384]{1,0:T(8,128)(2,1)S(1)}, u32[]{:S(2)}, u32[]{:S(2)}) collective-permute-start(bf16[128,384]{1,0:T(8,128)(2,1)S(1)} %get-tuple-element.139.refs_0_.second_ref), channel_id=1, source_target_pairs={{0,3},{1,2},{2,1},{3,0},{4,7},{5,6},{6,5},{7,4},{8,11},{9,10},{10,... | collective-permute-start | bytes 294920 | tf_op jit(solution)/shard_map/ppermute | solution.py:328
  36.6 4.7 %collective-permute-start.12 = (bf16[1,128,384]{2,1,0:T(8,128)(2,1)S(1)}, bf16[1,128,384]{2,1,0:T(8,128)(2,1)S(1)}, u32[]{:S(2)}, u32[]{:S(2)}) collective-permute-start(bf16[1,128,384]{2,1,0:T(8,128)(2,1)S(1)} %get-tuple-element.125), channel_id=1, source_target_pairs={{0,16},{4,20},{8,24},{12,28},{16,0},{20,4},{24,8},{28,12},{1,17},{... | collective-permute-start | bytes 294920 | tf_op jit(solution)/shard_map/ppermute | solution.py:328
  38.2 7.6 %collective-permute-start.15 = (bf16[128,384]{1,0:T(8,128)(2,1)S(1)}, bf16[128,384]{1,0:T(8,128)(2,1)S(1)}, u32[]{:S(2)}, u32[]{:S(2)}) collective-permute-start(bf16[128,384]{1,0:T(8,128)(2,1)S(1)} %get-tuple-element.139.refs_0_.second_ref), channel_id=1, source_target_pairs={{0,1},{1,0},{2,3},{3,2},{4,5},{5,4},{6,7},{7,6},{8,9},{9,8},{10,11... | collective-permute-start | bytes 294920 | tf_op jit(solution)/shard_map/ppermute | solution.py:328
  41.4 10.0 %collective-permute-start.23 = (bf16[128,384]{1,0:T(8,128)(2,1)S(1)}, bf16[128,384]{1,0:T(8,128)(2,1)S(1)}, u32[]{:S(2)}, u32[]{:S(2)}) collective-permute-start(bf16[128,384]{1,0:T(8,128)(2,1)S(1)} %get-tuple-element.154.refs_0_.second_ref), channel_id=1, source_target_pairs={{0,1},{1,0},{2,3},{3,2},{4,5},{5,4},{6,7},{7,6},{8,9},{9,8},{10,11... | collective-permute-start | bytes 294920 | tf_op jit(solution)/shard_map/ppermute | solution.py:328
  42.0 9.8 %collective-permute-start.22 = (bf16[128,384]{1,0:T(8,128)(2,1)S(1)}, bf16[128,384]{1,0:T(8,128)(2,1)S(1)}, u32[]{:S(2)}, u32[]{:S(2)}) collective-permute-start(bf16[128,384]{1,0:T(8,128)(2,1)S(1)} %get-tuple-element.154.refs_0_.second_ref), channel_id=1, source_target_pairs={{0,2},{1,3},{2,0},{3,1},{4,6},{5,7},{6,4},{7,5},{8,10},{9,11},{10,... | collective-permute-start | bytes 294920 | tf_op jit(solution)/shard_map/ppermute | solution.py:328
  43.9 8.0 %collective-permute-start.21 = (bf16[128,384]{1,0:T(8,128)(2,1)S(1)}, bf16[128,384]{1,0:T(8,128)(2,1)S(1)}, u32[]{:S(2)}, u32[]{:S(2)}) collective-permute-start(bf16[128,384]{1,0:T(8,128)(2,1)S(1)} %get-tuple-element.154.refs_0_.second_ref), channel_id=1, source_target_pairs={{0,3},{1,2},{2,1},{3,0},{4,7},{5,6},{6,5},{7,4},{8,11},{9,10},{10,... | collective-permute-start | bytes 294920 | tf_op jit(solution)/shard_map/ppermute | solution.py:328
  46.6 1.5 %collective-permute-start.16 = (bf16[2,128,384]{2,1,0:T(8,128)(2,1)S(1)}, bf16[2,128,384]{2,1,0:T(8,128)(2,1)S(1)}, u32[]{:S(2)}, u32[]{:S(2)}) collective-permute-start(bf16[2,128,384]{2,1,0:T(8,128)(2,1)S(1)} %get-tuple-element.137), channel_id=1, source_target_pairs={{0,4},{4,0},{8,12},{12,8},{16,20},{20,16},{24,28},{28,24},{1,5},{5... | collective-permute-start | bytes 589832 | tf_op jit(solution)/shard_map/ppermute | solution.py:328
  46.7 4.0 %collective-permute-start.18 = (bf16[2,128,384]{2,1,0:T(8,128)(2,1)S(1)}, bf16[2,128,384]{2,1,0:T(8,128)(2,1)S(1)}, u32[]{:S(2)}, u32[]{:S(2)}) collective-permute-start(bf16[2,128,384]{2,1,0:T(8,128)(2,1)S(1)} %get-tuple-element.138), channel_id=1, source_target_pairs={{0,4},{4,0},{8,12},{12,8},{16,20},{20,16},{24,28},{28,24},{1,5},{5... | collective-permute-start | bytes 589832 | tf_op jit(solution)/shard_map/ppermute | solution.py:328
  48.2 9.7 %collective-permute-start.17 = (bf16[128,384]{1,0:T(8,128)(2,1)S(1)}, bf16[128,384]{1,0:T(8,128)(2,1)S(1)}, u32[]{:S(2)}, u32[]{:S(2)}) collective-permute-start(bf16[128,384]{1,0:T(8,128)(2,1)S(1)} %get-tuple-element.144), channel_id=1, source_target_pairs={{0,24},{4,28},{8,16},{12,20},{16,8},{20,12},{24,0},{28,4},{1,25},{... | collective-permute-start | bytes 294920 | tf_op jit(solution)/shard_map/ppermute | solution.py:328
  50.7 6.7 %collective-permute-start.19 = (bf16[128,384]{1,0:T(8,128)(2,1)S(1)}, bf16[128,384]{1,0:T(8,128)(2,1)S(1)}, u32[]{:S(2)}, u32[]{:S(2)}) collective-permute-start(bf16[128,384]{1,0:T(8,128)(2,1)S(1)} %get-tuple-element.146), channel_id=1, source_target_pairs={{0,8},{4,12},{8,0},{12,4},{16,24},{20,28},{24,16},{28,20},{1,9},{5... | collective-permute-start | bytes 294920 | tf_op jit(solution)/shard_map/ppermute | solution.py:328
  51.4 6.5 %collective-permute-start.20 = (bf16[128,384]{1,0:T(8,128)(2,1)S(1)}, bf16[128,384]{1,0:T(8,128)(2,1)S(1)}, u32[]{:S(2)}, u32[]{:S(2)}) collective-permute-start(bf16[128,384]{1,0:T(8,128)(2,1)S(1)} %get-tuple-element.147), channel_id=1, source_target_pairs={{0,16},{4,20},{8,24},{12,28},{16,0},{20,4},{24,8},{28,12},{1,17},{... | collective-permute-start | bytes 294920 | tf_op jit(solution)/shard_map/ppermute | solution.py:328
  52.7 1.5 %collective-permute-start.24 = (bf16[2,128,384]{2,1,0:T(8,128)(2,1)S(1)}, bf16[2,128,384]{2,1,0:T(8,128)(2,1)S(1)}, u32[]{:S(2)}, u32[]{:S(2)}) collective-permute-start(bf16[2,128,384]{2,1,0:T(8,128)(2,1)S(1)} %get-tuple-element.152), channel_id=1, source_target_pairs={{0,4},{4,0},{8,12},{12,8},{16,20},{20,16},{24,28},{28,24},{1,5},{5... | collective-permute-start | bytes 589832 | tf_op jit(solution)/shard_map/ppermute | solution.py:328
  52.7 4.0 %collective-permute-start.25 = (bf16[2,128,384]{2,1,0:T(8,128)(2,1)S(1)}, bf16[2,128,384]{2,1,0:T(8,128)(2,1)S(1)}, u32[]{:S(2)}, u32[]{:S(2)}) collective-permute-start(bf16[2,128,384]{2,1,0:T(8,128)(2,1)S(1)} %get-tuple-element.153), channel_id=1, source_target_pairs={{0,4},{4,0},{8,12},{12,8},{16,20},{20,16},{24,28},{28,24},{1,5},{5... | collective-permute-start | bytes 589832 | tf_op jit(solution)/shard_map/ppermute | solution.py:328
  54.2 6.6 %collective-permute-start.26 = (bf16[128,384]{1,0:T(8,128)(2,1)S(1)}, bf16[128,384]{1,0:T(8,128)(2,1)S(1)}, u32[]{:S(2)}, u32[]{:S(2)}) collective-permute-start(bf16[128,384]{1,0:T(8,128)(2,1)S(1)} %get-tuple-element.159), channel_id=1, source_target_pairs={{0,24},{4,28},{8,16},{12,20},{16,8},{20,12},{24,0},{28,4},{1,25},{... | collective-permute-start | bytes 294920 | tf_op jit(solution)/shard_map/ppermute | solution.py:328
  56.7 5.5 %collective-permute-start.27 = (bf16[128,384]{1,0:T(8,128)(2,1)S(1)}, bf16[128,384]{1,0:T(8,128)(2,1)S(1)}, u32[]{:S(2)}, u32[]{:S(2)}) collective-permute-start(bf16[128,384]{1,0:T(8,128)(2,1)S(1)} %get-tuple-element.161), channel_id=1, source_target_pairs={{0,8},{4,12},{8,0},{12,4},{16,24},{20,28},{24,16},{28,20},{1,9},{5... | collective-permute-start | bytes 294920 | tf_op jit(solution)/shard_map/ppermute | solution.py:328
  57.4 4.9 %collective-permute-start.28 = (bf16[128,384]{1,0:T(8,128)(2,1)S(1)}, bf16[128,384]{1,0:T(8,128)(2,1)S(1)}, u32[]{:S(2)}, u32[]{:S(2)}) collective-permute-start(bf16[128,384]{1,0:T(8,128)(2,1)S(1)} %get-tuple-element.162), channel_id=1, source_target_pairs={{0,16},{4,20},{8,24},{12,28},{16,0},{20,4},{24,8},{28,12},{1,17},{... | collective-permute-start | bytes 294920 | tf_op jit(solution)/shard_map/ppermute | solution.py:328

commit v7 on v6

--- a/solution.py
+++ b/solution.py
@@ -196,9 +196,11 @@
     )(mine, theirs)
 
 
-def halve_kernel(order, kept_ref, arrived_ref, stay_ref, send_ref):
+def halve_kernel(order, kept_ref, *refs):
+    arrived_refs, (stay_ref, send_ref) = refs[:-2], refs[-2:]
+    arrived = [ref.at[i] for ref in arrived_refs for i in range(ref.shape[0])]
     for i in range(kept_ref.shape[0]):
-        total = kept_ref[order[i]] + arrived_ref[order[i]].astype(jnp.float32)
+        total = kept_ref[order[i]] + arrived[order[i]][...].astype(jnp.float32)
         if i % 2:
             send_ref[i // 2] = total.astype(send_ref.dtype)
         else:
@@ -217,7 +219,7 @@
         name="halve_sum",
         compiler_params=params(),
         cost_estimate=CHEAP,
-    )(kept, arrived)
+    )(kept, *arrived)
 
 
 def add_pieces(pieces):
@@ -407,16 +409,17 @@
     theirs, swapped_a = for_theirs(sources_a, both, 2)
     mine = for_mine(sources_a, theirs, 20)
     parts_a = add_pairs(mine, swapped_a)
-    theirs, swapped_b = for_theirs(sources_b, parts_a)
+    theirs, swapped_b = for_theirs(sources_b, parts_a, 2)
     mine = for_mine(sources_b, theirs, 20)
     pieces_a = spread(parts_a, offsets, n_row)
-    done = halve(mine, swapped_b[0], [offsets.index(j) for j in range(chips)])
+    done = halve(mine, swapped_b, [offsets.index(j) for j in range(chips)])
     pieces_b = [done[0], flip(done[1], "row", n_row, 2)]
 
     grad_a, second_a = middle(seed_label, after(pieces_a, done), 0)
     done, step = [grad_a, second_a], 4
     while step < n_row:
-        done = halve(*after(pieces_b, done), range(chips))
+        kept, arrived = after(pieces_b, done)
+        done = halve(kept, [arrived], range(chips))
         pieces_b = [done[0], flip(done[1], "row", n_row, step)]
         step *= 2
     sources_a = gather(second_a, n_col, (3, 2, 1), (1,), done)

time: 63.2 us -> 63.3 us (level)
    ppermute x29 -> x30, starting transfers between devices: 33.4 us -> 33.9 us  [flip(): return lax.ppermute(array, axis, [(i, i ^ bits) for i in range(size)])]
    ppermute x29 -> x30, waiting for transfers between devices: 10.2 us -> 9.77 us  [flip(): return lax.ppermute(array, axis, [(i, i ^ bits) for i in range(size)])]
  transfers between devices with their start and end apart: 29 -> 30, of which waited for: 12 -> 13; matrix products, arithmetic and copies ran while one was open for 1% -> 1% of each run, Pallas kernels for 26% -> 26%
where the time goes in v7:
time: 63.3 us; the launch traced here: 63.2 us
  starting transfers between devices  33.9 us (54%)
  Pallas kernels  18.1 us (29%)
  waiting for transfers between devices  9.77 us (15%)
  between operations  0.87 us (1%)
    ppermute x30, starting transfers between devices, flip(): return lax.ppermute(array, axis, [(i, i ^ bits) for i in range(size)])  33.9 us
    ppermute x30, waiting for transfers between devices, flip(): return lax.ppermute(array, axis, [(i, i ^ bits) for i in range(size)])  9.77 us
    pallas_call x1, Pallas kernels, densify(): pl.pallas_call(densify_kernel, in_specs=[pl.BlockSpec(memory_space=pltpu....  8.3 us
    pallas_call x8, Pallas kernels, multiply(): pl.pallas_call(functools.partial(multiply_kernel, tuple(offsets), tuple(f...  6.31 us
  transfers between devices with their start and end apart: 30, of which 13 were waited for; matrix products, arithmetic and copies ran while one was open for 1% of the time, Pallas kernels for 26%

profile of v7, /device:TPU:0, one launch (start us, length us, event | category | flops | bytes accessed | tf_op | source)
XLA Modules:
  0.0 63.2 jit_solution(7640469688066734386)
XLA Ops:
  0.7 1.1 %prepare.1 = (bf16[256,384]{1,0:T(8,128)(2,1)S(1)}, bf16[128,384]{1,0:T(8,128)(2,1)S(1)}, bf16[128,384]{1,0:T(8,128)(2,1)S(1)}) custom-call(bf16[384,256]{1,0:T(8,128)(2,1)} %cot_ref.1, s32[384]{0:T(512)} %seed_ref.5), custom_call_target="tpu_custom_call" | custom-call | flops 10000000000 | bytes 1 | tf_op jit(solution)/shard_map/prepare/pallas_call | solution.py:51
  1.8 5.1 %collective-permute-start.2 = (bf16[128,384]{1,0:T(8,128)(2,1)S(1)}, bf16[128,384]{1,0:T(8,128)(2,1)S(1)}, u32[]{:S(2)}, u32[]{:S(2)}) collective-permute-start(bf16[128,384]{1,0:T(8,128)(2,1)S(1)} %get-tuple-element.99.refs_0_), channel_id=1, source_target_pairs={{0,3},{1,2},{2,1},{3,0},{4,7},{5,6},{6,5},{7,4},{8,11},{9,10},{10,... | collective-permute-start | bytes 294920 | tf_op jit(solution)/shard_map/ppermute | solution.py:330
  6.9 0.6 %collective-permute-start = (bf16[128,384]{1,0:T(8,128)(2,1)S(1)}, bf16[128,384]{1,0:T(8,128)(2,1)S(1)}, u32[]{:S(2)}, u32[]{:S(2)}) collective-permute-start(bf16[128,384]{1,0:T(8,128)(2,1)S(1)} %get-tuple-element.99.refs_0_), channel_id=1, source_target_pairs={{0,2},{1,3},{2,0},{3,1},{4,6},{5,7},{6,4},{7,5},{8,10},{9,11},{10,... | collective-permute-start | bytes 294920 | tf_op jit(solution)/shard_map/ppermute | solution.py:330
  7.5 2.3 %collective-permute-start.3 = (bf16[128,384]{1,0:T(8,128)(2,1)S(1)}, bf16[128,384]{1,0:T(8,128)(2,1)S(1)}, u32[]{:S(2)}, u32[]{:S(2)}) collective-permute-start(bf16[128,384]{1,0:T(8,128)(2,1)S(1)} %get-tuple-element.114.own_ref.refs_0_), channel_id=1, source_target_pairs={{0,2},{1,3},{2,0},{3,1},{4,6},{5,7},{6,4},{7,5},{8,10},{9,11},{10,... | collective-permute-start | bytes 294920 | tf_op jit(solution)/shard_map/ppermute | solution.py:330
  9.9 0.3 convert_reduce_fusion
  10.2 0.2 select_reduce_fusion.codes_ref
  10.4 8.3 %densify.1.refs_4_ = bf16[1536,3072]{1,0:T(8,128)(2,1)S(1)} custom-call(s32[2]{0:T(128)S(1)} %pad_add_fusion.place_ref, s32[8,48]{1,0:T(8,128)S(1)} %select_reduce_fusion.codes_ref, bf16[1,1,8,48,128,128]{5,4,3,2,1,0:T(8,128)(2,1)} %tiles_ref.1), custom_call_target="tpu_custom_call" | custom-call | tf_op jit(solution)/shard_map/densify/pallas_call | solution.py:130
  18.7 0.6 collective-permute-done.3.arrived_ref.refs_1_
  19.4 1.5 %collective-permute-start.9 = (bf16[256,384]{1,0:T(8,128)(2,1)S(1)}, bf16[256,384]{1,0:T(8,128)(2,1)S(1)}, u32[]{:S(2)}, u32[]{:S(2)}) collective-permute-start(bf16[256,384]{1,0:T(8,128)(2,1)S(1)} %stack_labels.1), channel_id=1, source_target_pairs={{0,1},{1,0},{2,3},{3,2},{4,5},{5,4},{6,7},{7,6},{8,9},{9,8},{10,11... | collective-permute-start | bytes 589832 | tf_op jit(solution)/shard_map/ppermute | solution.py:330
  20.9 0.8 %multiply_theirs.4 = (bf16[2,128,384]{2,1,0:T(8,128)(2,1)S(1)}, bf16[2,128,384]{2,1,0:T(8,128)(2,1)S(1)}) custom-call(bf16[128,384]{1,0:T(8,128)(2,1)S(1)} %get-tuple-element.99.refs_0_, bf16[128,384]{1,0:T(8,128)(2,1)S(1)} %collective-permute-done.refs_1_, bf16[128,384]{1,0:T(8,128)(2,1)S(1)} %collective-permute-done.1.refs_2_, ...), custom_call_target="tpu_custom_call" | custom-call | bytes 1 | tf_op jit(solution)/shard_map/multiply_theirs/pallas_call | solution.py:170
  21.8 0.5 collective-permute-start.6
  22.3 0.8 %multiply_mine.4.mine_ref = f32[4,128,384]{2,1,0:T(8,128)S(1)} custom-call(bf16[128,384]{1,0:T(8,128)(2,1)S(1)} %get-tuple-element.99.refs_0_, bf16[128,384]{1,0:T(8,128)(2,1)S(1)} %collective-permute-done.refs_1_, bf16[128,384]{1,0:T(8,128)(2,1)S(1)} %collective-permute-done.1.refs_2_, bf16[128,384]{1,0:T(8,128)(2,1)S(1)} %collective-permute-done.2.refs_3_, ...), custom_call_target="tpu_custom_call" | custom-call | flops 24159191040 | bytes 1 | tf_op jit(solution)/shard_map/multiply_mine/pallas_call | solution.py:170
  23.1 0.1 collective-permute-done.4.theirs_ref
  23.2 2.5 %collective-permute-start.5 = (bf16[128,384]{1,0:T(8,128)(2,1)S(1)}, bf16[128,384]{1,0:T(8,128)(2,1)S(1)}, u32[]{:S(2)}, u32[]{:S(2)}) collective-permute-start(bf16[128,384]{1,0:T(8,128)(2,1)S(1)} %get-tuple-element.104), channel_id=1, source_target_pairs={{0,24},{4,28},{8,16},{12,20},{16,8},{20,12},{24,0},{28,4},{1,25},{... | collective-permute-start | bytes 294920 | tf_op jit(solution)/shard_map/ppermute | solution.py:330
  25.8 0.6 collective-permute-start.7
  26.4 0.5 collective-permute-start.8
  26.9 0.8 %multiply_theirs.5 = (bf16[2,128,384]{2,1,0:T(8,128)(2,1)S(1)}, bf16[2,128,384]{2,1,0:T(8,128)(2,1)S(1)}) custom-call(bf16[128,384]{1,0:T(8,128)(2,1)S(1)} %get-tuple-element.114.own_ref.refs_0_, bf16[128,384]{1,0:T(8,128)(2,1)S(1)} %collective-permute-done.3.arrived_ref.refs_1_, bf16[256,384]{1,0:T(8,128)(2,1)S(1)} %collective-permute-done.9.refs_2_.refs_3_, ...), custom_call_target="tpu_custom_call" | custom-call | bytes 1 | tf_op jit(solution)/shard_map/multiply_theirs/pallas_call | solution.py:170
  27.8 0.5 collective-permute-start.11
  28.3 0.8 %multiply_mine.5.kept_ref = f32[4,128,384]{2,1,0:T(8,128)S(1)} custom-call(bf16[128,384]{1,0:T(8,128)(2,1)S(1)} %get-tuple-element.114.own_ref.refs_0_, bf16[128,384]{1,0:T(8,128)(2,1)S(1)} %collective-permute-done.3.arrived_ref.refs_1_, bf16[256,384]{1,0:T(8,128)(2,1)S(1)} %collective-permute-done.9.refs_2_.refs_3_, ...), custom_call_target="tpu_custom_call" | custom-call | flops 24159191040 | bytes 1 | tf_op jit(solution)/shard_map/multiply_mine/pallas_call | solution.py:170
  29.1 0.1 collective-permute-done.10.refs_0_
  29.2 0.3 collective-permute-done.11.refs_1_
  29.6 1.6 %collective-permute-start.12 = (bf16[2,128,384]{2,1,0:T(8,128)(2,1)S(1)}, bf16[2,128,384]{2,1,0:T(8,128)(2,1)S(1)}, u32[]{:S(2)}, u32[]{:S(2)}) collective-permute-start(bf16[2,128,384]{2,1,0:T(8,128)(2,1)S(1)} %get-tuple-element.119), channel_id=1, source_target_pairs={{0,8},{4,12},{8,0},{12,4},{16,24},{20,28},{24,16},{28,20},{1,9},{5... | collective-permute-start | bytes 589832 | tf_op jit(solution)/shard_map/ppermute | solution.py:330
  31.4 1.8 %collective-permute-start.15 = (bf16[128,384]{1,0:T(8,128)(2,1)S(1)}, bf16[128,384]{1,0:T(8,128)(2,1)S(1)}, u32[]{:S(2)}, u32[]{:S(2)}) collective-permute-start(bf16[128,384]{1,0:T(8,128)(2,1)S(1)} %get-tuple-element.143.refs_0_.second_ref), channel_id=1, source_target_pairs={{0,2},{1,3},{2,0},{3,1},{4,6},{5,7},{6,4},{7,5},{8,10},{9,11},{10,... | collective-permute-start | bytes 294920 | tf_op jit(solution)/shard_map/ppermute | solution.py:330
  33.2 1.3 %collective-permute-start.14 = (bf16[128,384]{1,0:T(8,128)(2,1)S(1)}, bf16[128,384]{1,0:T(8,128)(2,1)S(1)}, u32[]{:S(2)}, u32[]{:S(2)}) collective-permute-start(bf16[128,384]{1,0:T(8,128)(2,1)S(1)} %get-tuple-element.143.refs_0_.second_ref), channel_id=1, source_target_pairs={{0,3},{1,2},{2,1},{3,0},{4,7},{5,6},{6,5},{7,4},{8,11},{9,10},{10,... | collective-permute-start | bytes 294920 | tf_op jit(solution)/shard_map/ppermute | solution.py:330
  34.4 2.2 %collective-permute-done.12.refs_0_ = bf16[2,128,384]{2,1,0:T(8,128)(2,1)S(1)} collective-permute-done((bf16[2,128,384]{2,1,0:T(8,128)(2,1)S(1)}, bf16[2,128,384]{2,1,0:T(8,128)(2,1)S(1)}, u32[]{:S(2)}, u32[]{:S(2)}) %collective-permute-start.12) | collective-permute-done | bytes 196640 | tf_op jit(solution)/shard_map/ppermute | solution.py:330
  36.7 1.6 %collective-permute-start.13 = (bf16[1,128,384]{2,1,0:T(8,128)(2,1)S(1)}, bf16[1,128,384]{2,1,0:T(8,128)(2,1)S(1)}, u32[]{:S(2)}, u32[]{:S(2)}) collective-permute-start(bf16[1,128,384]{2,1,0:T(8,128)(2,1)S(1)} %get-tuple-element.129), channel_id=1, source_target_pairs={{0,16},{4,20},{8,24},{12,28},{16,0},{20,4},{24,8},{28,12},{1,17},{... | collective-permute-start | bytes 294920 | tf_op jit(solution)/shard_map/ppermute | solution.py:330
  38.3 0.6 collective-permute-start.16
  39.0 2.4 %collective-permute-done.13.refs_1_ = bf16[1,128,384]{2,1,0:T(8,128)(2,1)S(1)} collective-permute-done((bf16[1,128,384]{2,1,0:T(8,128)(2,1)S(1)}, bf16[1,128,384]{2,1,0:T(8,128)(2,1)S(1)}, u32[]{:S(2)}, u32[]{:S(2)}) %collective-permute-start.13) | collective-permute-done | bytes 98336 | tf_op jit(solution)/shard_map/ppermute | solution.py:330
  41.4 0.7 %collective-permute-start.24 = (bf16[128,384]{1,0:T(8,128)(2,1)S(1)}, bf16[128,384]{1,0:T(8,128)(2,1)S(1)}, u32[]{:S(2)}, u32[]{:S(2)}) collective-permute-start(bf16[128,384]{1,0:T(8,128)(2,1)S(1)} %get-tuple-element.158.refs_0_.second_ref), channel_id=1, source_target_pairs={{0,1},{1,0},{2,3},{3,2},{4,5},{5,4},{6,7},{7,6},{8,9},{9,8},{10,11... | collective-permute-start | bytes 294920 | tf_op jit(solution)/shard_map/ppermute | solution.py:330
  42.1 1.8 %collective-permute-start.23 = (bf16[128,384]{1,0:T(8,128)(2,1)S(1)}, bf16[128,384]{1,0:T(8,128)(2,1)S(1)}, u32[]{:S(2)}, u32[]{:S(2)}) collective-permute-start(bf16[128,384]{1,0:T(8,128)(2,1)S(1)} %get-tuple-element.158.refs_0_.second_ref), channel_id=1, source_target_pairs={{0,2},{1,3},{2,0},{3,1},{4,6},{5,7},{6,4},{7,5},{8,10},{9,11},{10,... | collective-permute-start | bytes 294920 | tf_op jit(solution)/shard_map/ppermute | solution.py:330
  43.9 2.0 %collective-permute-start.22 = (bf16[128,384]{1,0:T(8,128)(2,1)S(1)}, bf16[128,384]{1,0:T(8,128)(2,1)S(1)}, u32[]{:S(2)}, u32[]{:S(2)}) collective-permute-start(bf16[128,384]{1,0:T(8,128)(2,1)S(1)} %get-tuple-element.158.refs_0_.second_ref), channel_id=1, source_target_pairs={{0,3},{1,2},{2,1},{3,0},{4,7},{5,6},{6,5},{7,4},{8,11},{9,10},{10,... | collective-permute-start | bytes 294920 | tf_op jit(solution)/shard_map/ppermute | solution.py:330
  45.9 0.8 %multiply_theirs.6 = (bf16[2,128,384]{2,1,0:T(8,128)(2,1)S(1)}, bf16[2,128,384]{2,1,0:T(8,128)(2,1)S(1)}) custom-call(bf16[128,384]{1,0:T(8,128)(2,1)S(1)} %get-tuple-element.143.refs_0_.second_ref, bf16[128,384]{1,0:T(8,128)(2,1)S(1)} %collective-permute-done.14.refs_1_, bf16[128,384]{1,0:T(8,128)(2,1)S(1)} %collective-permute-done.15.refs_2_, ...), custom_call_target="tpu_custom_call" | custom-call | bytes 1 | tf_op jit(solution)/shard_map/multiply_theirs/pallas_call | solution.py:170
  46.8 0.5 collective-permute-start.19
  47.3 0.8 %multiply_mine.6.mine_ref = f32[4,128,384]{2,1,0:T(8,128)S(1)} custom-call(bf16[128,384]{1,0:T(8,128)(2,1)S(1)} %get-tuple-element.143.refs_0_.second_ref, bf16[128,384]{1,0:T(8,128)(2,1)S(1)} %collective-permute-done.14.refs_1_, bf16[128,384]{1,0:T(8,128)(2,1)S(1)} %collective-permute-done.15.refs_2_, bf16[128,384]{1,0:T(8,128)(2,1)S(1)} %collective-permute-done.16.refs_3_, ...), custom_call_target="tpu_custom_call" | custom-call | flops 24159191040 | bytes 1 | tf_op jit(solution)/shard_map/multiply_mine/pallas_call | solution.py:170
  48.3 2.5 %collective-permute-start.18 = (bf16[128,384]{1,0:T(8,128)(2,1)S(1)}, bf16[128,384]{1,0:T(8,128)(2,1)S(1)}, u32[]{:S(2)}, u32[]{:S(2)}) collective-permute-start(bf16[128,384]{1,0:T(8,128)(2,1)S(1)} %get-tuple-element.148), channel_id=1, source_target_pairs={{0,24},{4,28},{8,16},{12,20},{16,8},{20,12},{24,0},{28,4},{1,25},{... | collective-permute-start | bytes 294920 | tf_op jit(solution)/shard_map/ppermute | solution.py:330
  50.8 0.6 collective-permute-start.20
  51.4 0.5 collective-permute-start.21
  51.9 0.8 %multiply_theirs.7 = (bf16[2,128,384]{2,1,0:T(8,128)(2,1)S(1)}, bf16[2,128,384]{2,1,0:T(8,128)(2,1)S(1)}) custom-call(bf16[128,384]{1,0:T(8,128)(2,1)S(1)} %get-tuple-element.158.refs_0_.second_ref, bf16[128,384]{1,0:T(8,128)(2,1)S(1)} %collective-permute-done.22.refs_1_, bf16[128,384]{1,0:T(8,128)(2,1)S(1)} %collective-permute-done.23.refs_2_, ...), custom_call_target="tpu_custom_call" | custom-call | bytes 1 | tf_op jit(solution)/shard_map/multiply_theirs/pallas_call | solution.py:170
  52.8 0.5 collective-permute-start.26
  53.3 0.8 %multiply_mine.7.mine_ref = f32[4,128,384]{2,1,0:T(8,128)S(1)} custom-call(bf16[128,384]{1,0:T(8,128)(2,1)S(1)} %get-tuple-element.158.refs_0_.second_ref, bf16[128,384]{1,0:T(8,128)(2,1)S(1)} %collective-permute-done.22.refs_1_, bf16[128,384]{1,0:T(8,128)(2,1)S(1)} %collective-permute-done.23.refs_2_, bf16[128,384]{1,0:T(8,128)(2,1)S(1)} %collective-permute-done.24.refs_3_, ...), custom_call_target="tpu_custom_call" | custom-call | flops 24159191040 | bytes 1 | tf_op jit(solution)/shard_map/multiply_mine/pallas_call | solution.py:170
  54.3 2.5 %collective-permute-start.27 = (bf16[128,384]{1,0:T(8,128)(2,1)S(1)}, bf16[128,384]{1,0:T(8,128)(2,1)S(1)}, u32[]{:S(2)}, u32[]{:S(2)}) collective-permute-start(bf16[128,384]{1,0:T(8,128)(2,1)S(1)} %get-tuple-element.163), channel_id=1, source_target_pairs={{0,24},{4,28},{8,16},{12,20},{16,8},{20,12},{24,0},{28,4},{1,25},{... | collective-permute-start | bytes 294920 | tf_op jit(solution)/shard_map/ppermute | solution.py:330
  56.8 0.6 collective-permute-start.28
  57.5 0.5 collective-permute-start.29
  58.0 0.2 label_grad.1.refs_0_
  58.1 0.8 %first_grad_out.1 = bf16[384,256]{1,0:T(8,128)(2,1)} custom-call(bf16[384,128]{1,0:T(8,128)(2,1)S(1)} %turn_grad.1.refs_0_, bf16[128,384]{1,0:T(8,128)(2,1)S(1)} %get-tuple-element.171.refs_1_), custom_call_target="tpu_custom_call" | custom-call | flops 1 | bytes 1 | tf_op jit(solution)/shard_map/first_grad_out/pallas_call | solution.py:279
  58.9 2.0 %collective-permute-done.27.refs_2_ = bf16[128,384]{1,0:T(8,128)(2,1)S(1)} collective-permute-done((bf16[128,384]{1,0:T(8,128)(2,1)S(1)}, bf16[128,384]{1,0:T(8,128)(2,1)S(1)}, u32[]{:S(2)}, u32[]{:S(2)}) %collective-permute-start.27) | collective-permute-done | bytes 98336 | tf_op jit(solution)/shard_map/ppermute | solution.py:330
  60.9 1.4 %collective-permute-done.28.refs_3_ = bf16[128,384]{1,0:T(8,128)(2,1)S(1)} collective-permute-done((bf16[128,384]{1,0:T(8,128)(2,1)S(1)}, bf16[128,384]{1,0:T(8,128)(2,1)S(1)}, u32[]{:S(2)}, u32[]{:S(2)}) %collective-permute-start.28) | collective-permute-done | bytes 98336 | tf_op jit(solution)/shard_map/ppermute | solution.py:330
  62.4 0.8 %label_grad_out.1 = bf16[384,256]{1,0:T(8,128)(2,1)} custom-call(bf16[256,384]{1,0:T(8,128)(2,1)S(1)} %get-tuple-element.134.first_ref, bf16[128,384]{1,0:T(8,128)(2,1)S(1)} %get-tuple-element.158.refs_0_.second_ref, bf16[384,128]{1,0:T(8,128)(2,1)S(1)} %label_grad.1.refs_0_, f32[128,384]{1,0:T(8,128)S(1)} %get-tuple-element.172.refs_1_, ...), custom_call_target="tpu_custom_call" | custom-call | flops 1 | bytes 1 | tf_op jit(solution)/shard_map/label_grad_out/pallas_call | solution.py:320
  (50 shorter events, 1.6 us)
Async XLA Ops:
  0.6 9.2 %copy-start.1 = (s32[1,1,8,48]{3,2,1,0:T(8,128)S(1)}, s32[1,1,8,48]{3,2,1,0:T(8,128)}, u32[]{:S(2)}) copy-start(s32[1,1,8,48]{3,2,1,0:T(8,128)} %param.11) | copy-start | bytes 4612
  0.6 9.2 %copy-start.2 = (s32[1,1,8,48]{3,2,1,0:T(8,128)S(1)}, s32[1,1,8,48]{3,2,1,0:T(8,128)}, u32[]{:S(2)}) copy-start(s32[1,1,8,48]{3,2,1,0:T(8,128)} %param.10) | copy-start | bytes 4612
  0.7 9.2 %copy-start.3 = (s32[1,1,8,48]{3,2,1,0:T(8,128)S(1)}, s32[1,1,8,48]{3,2,1,0:T(8,128)}, u32[]{:S(2)}) copy-start(s32[1,1,8,48]{3,2,1,0:T(8,128)} %param.9) | copy-start | bytes 4612
  1.8 19.1 %collective-permute-start.2 = (bf16[128,384]{1,0:T(8,128)(2,1)S(1)}, bf16[128,384]{1,0:T(8,128)(2,1)S(1)}, u32[]{:S(2)}, u32[]{:S(2)}) collective-permute-start(bf16[128,384]{1,0:T(8,128)(2,1)S(1)} %get-tuple-element.99.refs_0_), channel_id=1, source_target_pairs={{0,3},{1,2},{2,1},{3,0},{4,7},{5,6},{6,5},{7,4},{8,11},{9,10},{10,... | collective-permute-start | bytes 294920 | tf_op jit(solution)/shard_map/ppermute | solution.py:330
  6.9 14.0 %collective-permute-start.1 = (bf16[128,384]{1,0:T(8,128)(2,1)S(1)}, bf16[128,384]{1,0:T(8,128)(2,1)S(1)}, u32[]{:S(2)}, u32[]{:S(2)}) collective-permute-start(bf16[128,384]{1,0:T(8,128)(2,1)S(1)} %get-tuple-element.99.refs_0_), channel_id=1, source_target_pairs={{0,1},{1,0},{2,3},{3,2},{4,5},{5,4},{6,7},{7,6},{8,9},{9,8},{10,11... | collective-permute-start | bytes 294920 | tf_op jit(solution)/shard_map/ppermute | solution.py:330
  6.9 14.0 %collective-permute-start = (bf16[128,384]{1,0:T(8,128)(2,1)S(1)}, bf16[128,384]{1,0:T(8,128)(2,1)S(1)}, u32[]{:S(2)}, u32[]{:S(2)}) collective-permute-start(bf16[128,384]{1,0:T(8,128)(2,1)S(1)} %get-tuple-element.99.refs_0_), channel_id=1, source_target_pairs={{0,2},{1,3},{2,0},{3,1},{4,6},{5,7},{6,4},{7,5},{8,10},{9,11},{10,... | collective-permute-start | bytes 294920 | tf_op jit(solution)/shard_map/ppermute | solution.py:330
  7.5 11.8 %collective-permute-start.3 = (bf16[128,384]{1,0:T(8,128)(2,1)S(1)}, bf16[128,384]{1,0:T(8,128)(2,1)S(1)}, u32[]{:S(2)}, u32[]{:S(2)}) collective-permute-start(bf16[128,384]{1,0:T(8,128)(2,1)S(1)} %get-tuple-element.114.own_ref.refs_0_), channel_id=1, source_target_pairs={{0,2},{1,3},{2,0},{3,1},{4,6},{5,7},{6,4},{7,5},{8,10},{9,11},{10,... | collective-permute-start | bytes 294920 | tf_op jit(solution)/shard_map/ppermute | solution.py:330
  19.4 7.5 %collective-permute-start.9 = (bf16[256,384]{1,0:T(8,128)(2,1)S(1)}, bf16[256,384]{1,0:T(8,128)(2,1)S(1)}, u32[]{:S(2)}, u32[]{:S(2)}) collective-permute-start(bf16[256,384]{1,0:T(8,128)(2,1)S(1)} %stack_labels.1), channel_id=1, source_target_pairs={{0,1},{1,0},{2,3},{3,2},{4,5},{5,4},{6,7},{7,6},{8,9},{9,8},{10,11... | collective-permute-start | bytes 589832 | tf_op jit(solution)/shard_map/ppermute | solution.py:330
  21.7 1.5 %collective-permute-start.4 = (bf16[2,128,384]{2,1,0:T(8,128)(2,1)S(1)}, bf16[2,128,384]{2,1,0:T(8,128)(2,1)S(1)}, u32[]{:S(2)}, u32[]{:S(2)}) collective-permute-start(bf16[2,128,384]{2,1,0:T(8,128)(2,1)S(1)} %get-tuple-element.97), channel_id=1, source_target_pairs={{0,4},{4,0},{8,12},{12,8},{16,20},{20,16},{24,28},{28,24},{1,5},{5... | collective-permute-start | bytes 589832 | tf_op jit(solution)/shard_map/ppermute | solution.py:330
  21.8 4.0 %collective-permute-start.6 = (bf16[2,128,384]{2,1,0:T(8,128)(2,1)S(1)}, bf16[2,128,384]{2,1,0:T(8,128)(2,1)S(1)}, u32[]{:S(2)}, u32[]{:S(2)}) collective-permute-start(bf16[2,128,384]{2,1,0:T(8,128)(2,1)S(1)} %get-tuple-element.98), channel_id=1, source_target_pairs={{0,4},{4,0},{8,12},{12,8},{16,20},{20,16},{24,28},{28,24},{1,5},{5... | collective-permute-start | bytes 589832 | tf_op jit(solution)/shard_map/ppermute | solution.py:330
  23.2 8.1 %collective-permute-start.5 = (bf16[128,384]{1,0:T(8,128)(2,1)S(1)}, bf16[128,384]{1,0:T(8,128)(2,1)S(1)}, u32[]{:S(2)}, u32[]{:S(2)}) collective-permute-start(bf16[128,384]{1,0:T(8,128)(2,1)S(1)} %get-tuple-element.104), channel_id=1, source_target_pairs={{0,24},{4,28},{8,16},{12,20},{16,8},{20,12},{24,0},{28,4},{1,25},{... | collective-permute-start | bytes 294920 | tf_op jit(solution)/shard_map/ppermute | solution.py:330
  25.8 5.4 %collective-permute-start.7 = (bf16[128,384]{1,0:T(8,128)(2,1)S(1)}, bf16[128,384]{1,0:T(8,128)(2,1)S(1)}, u32[]{:S(2)}, u32[]{:S(2)}) collective-permute-start(bf16[128,384]{1,0:T(8,128)(2,1)S(1)} %get-tuple-element.106), channel_id=1, source_target_pairs={{0,8},{4,12},{8,0},{12,4},{16,24},{20,28},{24,16},{28,20},{1,9},{5... | collective-permute-start | bytes 294920 | tf_op jit(solution)/shard_map/ppermute | solution.py:330
  26.4 4.9 %collective-permute-start.8 = (bf16[128,384]{1,0:T(8,128)(2,1)S(1)}, bf16[128,384]{1,0:T(8,128)(2,1)S(1)}, u32[]{:S(2)}, u32[]{:S(2)}) collective-permute-start(bf16[128,384]{1,0:T(8,128)(2,1)S(1)} %get-tuple-element.107), channel_id=1, source_target_pairs={{0,16},{4,20},{8,24},{12,28},{16,0},{20,4},{24,8},{28,12},{1,17},{... | collective-permute-start | bytes 294920 | tf_op jit(solution)/shard_map/ppermute | solution.py:330
  27.7 1.5 %collective-permute-start.10 = (bf16[2,128,384]{2,1,0:T(8,128)(2,1)S(1)}, bf16[2,128,384]{2,1,0:T(8,128)(2,1)S(1)}, u32[]{:S(2)}, u32[]{:S(2)}) collective-permute-start(bf16[2,128,384]{2,1,0:T(8,128)(2,1)S(1)} %get-tuple-element.112), channel_id=1, source_target_pairs={{0,4},{4,0},{8,12},{12,8},{16,20},{20,16},{24,28},{28,24},{1,5},{5... | collective-permute-start | bytes 589832 | tf_op jit(solution)/shard_map/ppermute | solution.py:330
  27.8 3.5 %copy-start = (s32[384]{0:T(512)S(1)}, s32[384]{0:T(512)}, u32[]{:S(2)}) copy-start(s32[384]{0:T(512)} %seed_ref.5) | copy-start | bytes 4612
  27.8 1.7 %collective-permute-start.11 = (bf16[2,128,384]{2,1,0:T(8,128)(2,1)S(1)}, bf16[2,128,384]{2,1,0:T(8,128)(2,1)S(1)}, u32[]{:S(2)}, u32[]{:S(2)}) collective-permute-start(bf16[2,128,384]{2,1,0:T(8,128)(2,1)S(1)} %get-tuple-element.113), channel_id=1, source_target_pairs={{0,4},{4,0},{8,12},{12,8},{16,20},{20,16},{24,28},{28,24},{1,5},{5... | collective-permute-start | bytes 589832 | tf_op jit(solution)/shard_map/ppermute | solution.py:330
  29.6 7.1 %collective-permute-start.12 = (bf16[2,128,384]{2,1,0:T(8,128)(2,1)S(1)}, bf16[2,128,384]{2,1,0:T(8,128)(2,1)S(1)}, u32[]{:S(2)}, u32[]{:S(2)}) collective-permute-start(bf16[2,128,384]{2,1,0:T(8,128)(2,1)S(1)} %get-tuple-element.119), channel_id=1, source_target_pairs={{0,8},{4,12},{8,0},{12,4},{16,24},{20,28},{24,16},{28,20},{1,9},{5... | collective-permute-start | bytes 589832 | tf_op jit(solution)/shard_map/ppermute | solution.py:330
  31.4 12.5 %collective-permute-start.15 = (bf16[128,384]{1,0:T(8,128)(2,1)S(1)}, bf16[128,384]{1,0:T(8,128)(2,1)S(1)}, u32[]{:S(2)}, u32[]{:S(2)}) collective-permute-start(bf16[128,384]{1,0:T(8,128)(2,1)S(1)} %get-tuple-element.143.refs_0_.second_ref), channel_id=1, source_target_pairs={{0,2},{1,3},{2,0},{3,1},{4,6},{5,7},{6,4},{7,5},{8,10},{9,11},{10,... | collective-permute-start | bytes 294920 | tf_op jit(solution)/shard_map/ppermute | solution.py:330
  33.2 12.7 %collective-permute-start.14 = (bf16[128,384]{1,0:T(8,128)(2,1)S(1)}, bf16[128,384]{1,0:T(8,128)(2,1)S(1)}, u32[]{:S(2)}, u32[]{:S(2)}) collective-permute-start(bf16[128,384]{1,0:T(8,128)(2,1)S(1)} %get-tuple-element.143.refs_0_.second_ref), channel_id=1, source_target_pairs={{0,3},{1,2},{2,1},{3,0},{4,7},{5,6},{6,5},{7,4},{8,11},{9,10},{10,... | collective-permute-start | bytes 294920 | tf_op jit(solution)/shard_map/ppermute | solution.py:330
  36.7 4.7 %collective-permute-start.13 = (bf16[1,128,384]{2,1,0:T(8,128)(2,1)S(1)}, bf16[1,128,384]{2,1,0:T(8,128)(2,1)S(1)}, u32[]{:S(2)}, u32[]{:S(2)}) collective-permute-start(bf16[1,128,384]{2,1,0:T(8,128)(2,1)S(1)} %get-tuple-element.129), channel_id=1, source_target_pairs={{0,16},{4,20},{8,24},{12,28},{16,0},{20,4},{24,8},{28,12},{1,17},{... | collective-permute-start | bytes 294920 | tf_op jit(solution)/shard_map/ppermute | solution.py:330
  38.3 7.6 %collective-permute-start.16 = (bf16[128,384]{1,0:T(8,128)(2,1)S(1)}, bf16[128,384]{1,0:T(8,128)(2,1)S(1)}, u32[]{:S(2)}, u32[]{:S(2)}) collective-permute-start(bf16[128,384]{1,0:T(8,128)(2,1)S(1)} %get-tuple-element.143.refs_0_.second_ref), channel_id=1, source_target_pairs={{0,1},{1,0},{2,3},{3,2},{4,5},{5,4},{6,7},{7,6},{8,9},{9,8},{10,11... | collective-permute-start | bytes 294920 | tf_op jit(solution)/shard_map/ppermute | solution.py:330
  41.4 10.0 %collective-permute-start.24 = (bf16[128,384]{1,0:T(8,128)(2,1)S(1)}, bf16[128,384]{1,0:T(8,128)(2,1)S(1)}, u32[]{:S(2)}, u32[]{:S(2)}) collective-permute-start(bf16[128,384]{1,0:T(8,128)(2,1)S(1)} %get-tuple-element.158.refs_0_.second_ref), channel_id=1, source_target_pairs={{0,1},{1,0},{2,3},{3,2},{4,5},{5,4},{6,7},{7,6},{8,9},{9,8},{10,11... | collective-permute-start | bytes 294920 | tf_op jit(solution)/shard_map/ppermute | solution.py:330
  42.1 9.8 %collective-permute-start.23 = (bf16[128,384]{1,0:T(8,128)(2,1)S(1)}, bf16[128,384]{1,0:T(8,128)(2,1)S(1)}, u32[]{:S(2)}, u32[]{:S(2)}) collective-permute-start(bf16[128,384]{1,0:T(8,128)(2,1)S(1)} %get-tuple-element.158.refs_0_.second_ref), channel_id=1, source_target_pairs={{0,2},{1,3},{2,0},{3,1},{4,6},{5,7},{6,4},{7,5},{8,10},{9,11},{10,... | collective-permute-start | bytes 294920 | tf_op jit(solution)/shard_map/ppermute | solution.py:330
  43.9 8.0 %collective-permute-start.22 = (bf16[128,384]{1,0:T(8,128)(2,1)S(1)}, bf16[128,384]{1,0:T(8,128)(2,1)S(1)}, u32[]{:S(2)}, u32[]{:S(2)}) collective-permute-start(bf16[128,384]{1,0:T(8,128)(2,1)S(1)} %get-tuple-element.158.refs_0_.second_ref), channel_id=1, source_target_pairs={{0,3},{1,2},{2,1},{3,0},{4,7},{5,6},{6,5},{7,4},{8,11},{9,10},{10,... | collective-permute-start | bytes 294920 | tf_op jit(solution)/shard_map/ppermute | solution.py:330
  46.7 1.5 %collective-permute-start.17 = (bf16[2,128,384]{2,1,0:T(8,128)(2,1)S(1)}, bf16[2,128,384]{2,1,0:T(8,128)(2,1)S(1)}, u32[]{:S(2)}, u32[]{:S(2)}) collective-permute-start(bf16[2,128,384]{2,1,0:T(8,128)(2,1)S(1)} %get-tuple-element.141), channel_id=1, source_target_pairs={{0,4},{4,0},{8,12},{12,8},{16,20},{20,16},{24,28},{28,24},{1,5},{5... | collective-permute-start | bytes 589832 | tf_op jit(solution)/shard_map/ppermute | solution.py:330
  46.8 4.0 %collective-permute-start.19 = (bf16[2,128,384]{2,1,0:T(8,128)(2,1)S(1)}, bf16[2,128,384]{2,1,0:T(8,128)(2,1)S(1)}, u32[]{:S(2)}, u32[]{:S(2)}) collective-permute-start(bf16[2,128,384]{2,1,0:T(8,128)(2,1)S(1)} %get-tuple-element.142), channel_id=1, source_target_pairs={{0,4},{4,0},{8,12},{12,8},{16,20},{20,16},{24,28},{28,24},{1,5},{5... | collective-permute-start | bytes 589832 | tf_op jit(solution)/shard_map/ppermute | solution.py:330
  48.3 9.7 %collective-permute-start.18 = (bf16[128,384]{1,0:T(8,128)(2,1)S(1)}, bf16[128,384]{1,0:T(8,128)(2,1)S(1)}, u32[]{:S(2)}, u32[]{:S(2)}) collective-permute-start(bf16[128,384]{1,0:T(8,128)(2,1)S(1)} %get-tuple-element.148), channel_id=1, source_target_pairs={{0,24},{4,28},{8,16},{12,20},{16,8},{20,12},{24,0},{28,4},{1,25},{... | collective-permute-start | bytes 294920 | tf_op jit(solution)/shard_map/ppermute | solution.py:330
  50.8 6.6 %collective-permute-start.20 = (bf16[128,384]{1,0:T(8,128)(2,1)S(1)}, bf16[128,384]{1,0:T(8,128)(2,1)S(1)}, u32[]{:S(2)}, u32[]{:S(2)}) collective-permute-start(bf16[128,384]{1,0:T(8,128)(2,1)S(1)} %get-tuple-element.150), channel_id=1, source_target_pairs={{0,8},{4,12},{8,0},{12,4},{16,24},{20,28},{24,16},{28,20},{1,9},{5... | collective-permute-start | bytes 294920 | tf_op jit(solution)/shard_map/ppermute | solution.py:330
  51.4 6.5 %collective-permute-start.21 = (bf16[128,384]{1,0:T(8,128)(2,1)S(1)}, bf16[128,384]{1,0:T(8,128)(2,1)S(1)}, u32[]{:S(2)}, u32[]{:S(2)}) collective-permute-start(bf16[128,384]{1,0:T(8,128)(2,1)S(1)} %get-tuple-element.151), channel_id=1, source_target_pairs={{0,16},{4,20},{8,24},{12,28},{16,0},{20,4},{24,8},{28,12},{1,17},{... | collective-permute-start | bytes 294920 | tf_op jit(solution)/shard_map/ppermute | solution.py:330
  52.7 1.5 %collective-permute-start.25 = (bf16[2,128,384]{2,1,0:T(8,128)(2,1)S(1)}, bf16[2,128,384]{2,1,0:T(8,128)(2,1)S(1)}, u32[]{:S(2)}, u32[]{:S(2)}) collective-permute-start(bf16[2,128,384]{2,1,0:T(8,128)(2,1)S(1)} %get-tuple-element.156), channel_id=1, source_target_pairs={{0,4},{4,0},{8,12},{12,8},{16,20},{20,16},{24,28},{28,24},{1,5},{5... | collective-permute-start | bytes 589832 | tf_op jit(solution)/shard_map/ppermute | solution.py:330
  52.8 4.0 %collective-permute-start.26 = (bf16[2,128,384]{2,1,0:T(8,128)(2,1)S(1)}, bf16[2,128,384]{2,1,0:T(8,128)(2,1)S(1)}, u32[]{:S(2)}, u32[]{:S(2)}) collective-permute-start(bf16[2,128,384]{2,1,0:T(8,128)(2,1)S(1)} %get-tuple-element.157), channel_id=1, source_target_pairs={{0,4},{4,0},{8,12},{12,8},{16,20},{20,16},{24,28},{28,24},{1,5},{5... | collective-permute-start | bytes 589832 | tf_op jit(solution)/shard_map/ppermute | solution.py:330
  54.3 6.6 %collective-permute-start.27 = (bf16[128,384]{1,0:T(8,128)(2,1)S(1)}, bf16[128,384]{1,0:T(8,128)(2,1)S(1)}, u32[]{:S(2)}, u32[]{:S(2)}) collective-permute-start(bf16[128,384]{1,0:T(8,128)(2,1)S(1)} %get-tuple-element.163), channel_id=1, source_target_pairs={{0,24},{4,28},{8,16},{12,20},{16,8},{20,12},{24,0},{28,4},{1,25},{... | collective-permute-start | bytes 294920 | tf_op jit(solution)/shard_map/ppermute | solution.py:330
  56.8 5.4 %collective-permute-start.28 = (bf16[128,384]{1,0:T(8,128)(2,1)S(1)}, bf16[128,384]{1,0:T(8,128)(2,1)S(1)}, u32[]{:S(2)}, u32[]{:S(2)}) collective-permute-start(bf16[128,384]{1,0:T(8,128)(2,1)S(1)} %get-tuple-element.165), channel_id=1, source_target_pairs={{0,8},{4,12},{8,0},{12,4},{16,24},{20,28},{24,16},{28,20},{1,9},{5... | collective-permute-start | bytes 294920 | tf_op jit(solution)/shard_map/ppermute | solution.py:330
  57.5 4.9 %collective-permute-start.29 = (bf16[128,384]{1,0:T(8,128)(2,1)S(1)}, bf16[128,384]{1,0:T(8,128)(2,1)S(1)}, u32[]{:S(2)}, u32[]{:S(2)}) collective-permute-start(bf16[128,384]{1,0:T(8,128)(2,1)S(1)} %get-tuple-element.166), channel_id=1, source_target_pairs={{0,16},{4,20},{8,24},{12,28},{16,0},{20,4},{24,8},{28,12},{1,17},{... | collective-permute-start | bytes 294920 | tf_op jit(solution)/shard_map/ppermute | solution.py:330
